TPU v7x, 512 devices: a whole 4x8x8 slice. The times are simulated.
512 devices in a mesh: gx: 32 (over x, y), gy: 16 (over z, core).
Axes of the slice: x: 4, y: 8, z: 8, core: 2. Of those that a mesh axis runs over, the one named last changes fastest.
Arguments:
- latent: bfloat16 [32, 16, 16, 64, 128], P('gx', 'gy'), may hold values from -6 to 6
- occupancy: int32 [32, 16, 16], P('gx', 'gy'), may hold values from 0 to 1, as said below
- carry_x: float32 [32, 16, 16], P('gx', 'gy'), may hold values from 0.003 to 1
- carry_y: float32 [32, 16, 16], P('gx', 'gy'), may hold values from 0.003 to 1
- w_in: bfloat16 [16, 64], replicated, may hold values from -1.5 to 1.5
- w_down: bfloat16 [512, 128], replicated, may hold values from -0.25 to 0.25
- w_mid: bfloat16 [7, 128, 128], replicated, may hold values from -0.1875 to 0.1875
- w_up: bfloat16 [128, 512], replicated, may hold values from -0.5 to 0.5
- w_out: bfloat16 [64, 16], replicated, may hold values from -0.75 to 0.75
Outputs:
- denoised: bfloat16 [32, 16, 16, 64, 128], P('gx', 'gy')
Inputs may be any that keep to these rules, and one draw needn't show every extreme that they name: `occupancy`: every tile has at least one and at most 12 occupied blocks; some tile has exactly 12.
All inputs are finite; a program needn't handle non-finite values.
Results may differ from a plain program's by a relative error of at most 0.015.
Values sent between devices are 32-bit elements; how exact they have to be, the bound alone decides.
No kernel may reach another device: no remote copies, remote signals or barrier semaphores. Data moves between devices by JAX's collectives and lax.ppermute only.
A program may use at most 64 MiB of HBM per device.

v0:
```python
import jax
import jax.numpy as jnp
from jax import lax
from jax.sharding import PartitionSpec as P

STEPS = 2


def prefix(part, axis, combine, identity):
    place = lax.axis_index(axis)
    gathered = jax.tree.map(lambda a: lax.all_gather(a, axis), part)
    state = jax.tree.map(lambda a, e: jnp.zeros_like(a) + jnp.asarray(e, a.dtype), part, identity)

    def one(step, state):
        return combine(
            state, jax.tree.map(lambda a: lax.dynamic_index_in_dim(a, step, 0, False), gathered)
        )

    return lax.fori_loop(0, place, one, state)


def block_net(blocks, w_in, w_down, w_mid, w_up, w_out):
    count = blocks.shape[0]
    chan = w_in.shape[0]
    fb_width = w_down.shape[1]
    eye_block = jnp.eye(8, dtype=jnp.bfloat16)
    wide_in = jnp.kron(eye_block, w_in)
    wide_out = jnp.kron(eye_block, w_out)
    voxel_rows = blocks.reshape(count * 64, 8 * chan)
    first_rows = jax.nn.silu(
        jnp.dot(voxel_rows, wide_in, preferred_element_type=jnp.float32)
    ).astype(jnp.bfloat16)
    pre = jnp.dot(first_rows, w_down, preferred_element_type=jnp.float32)
    pre = pre * lax.rsqrt(jnp.mean(pre * pre, axis=-1, keepdims=True) + 1e-06)
    second = jax.nn.silu(pre).astype(jnp.bfloat16)
    coarse = second.reshape(count, 4, 4, 4, fb_width)
    stencil = [coarse]
    for axis_num in (1, 2, 3):
        widths = [(0, 0)] * 5
        widths[axis_num] = (1, 1)
        padded = jnp.pad(coarse, widths)
        for offset in (-1, 1):
            stencil.append(lax.slice_in_dim(padded, 1 + offset, 5 + offset, axis=axis_num))
    stacked = jnp.concatenate(stencil, axis=-1).reshape(count * 64, 7 * fb_width)
    mixed = jnp.dot(
        stacked, w_mid.reshape(7 * fb_width, fb_width), preferred_element_type=jnp.float32
    )
    middle = (second.astype(jnp.float32) + jax.nn.silu(mixed)).astype(jnp.bfloat16)
    upper = jax.nn.silu(
        jnp.dot(middle, w_up, preferred_element_type=jnp.float32) + first_rows.astype(jnp.float32)
    ).astype(jnp.bfloat16)
    update = jnp.dot(upper, wide_out, preferred_element_type=jnp.float32)
    return update.reshape(count, 64, 8 * chan)


def strip_x(field, which):
    picked = jnp.take(field, which, axis=-7)
    reduced = jnp.mean(picked, axis=-4)
    shape = reduced.shape
    reduced = reduced.reshape(shape[:-1] + (2, shape[-1] // 2))
    return jnp.mean(reduced, axis=-2)


def strip_y(field, which):
    picked = jnp.take(field, which, axis=-6)
    reduced = jnp.mean(picked, axis=-3)
    shape = reduced.shape
    reduced = reduced.reshape(shape[:-1] + (2, 2, shape[-1] // 4))
    reduced = jnp.mean(reduced, axis=-2)
    return reduced.reshape(shape[:-1] + (shape[-1] // 2,))


def spread_x(plane):
    whole = jnp.concatenate([plane, plane], axis=-1)
    return jnp.expand_dims(jnp.expand_dims(whole, -6), -4)


def spread_y(plane):
    shape = plane.shape
    split = plane.reshape(shape[:-1] + (2, 1, shape[-1] // 2))
    split = jnp.broadcast_to(split, shape[:-1] + (2, 2, shape[-1] // 2))
    whole = split.reshape(shape[:-1] + (2 * shape[-1],))
    return jnp.expand_dims(jnp.expand_dims(whole, -5), -3)


def gain_x(decay_rates):
    chan = decay_rates.shape[-1]
    width = 8 * chan
    lanes = jnp.arange(width)
    sub_x = lanes // (4 * chan)
    corner = jnp.arange(4)
    place = (8 * corner[:, None, None] + 2 * corner[None, :, None] + sub_x[None, None, :]).astype(
        jnp.float32
    ) + 0.5
    logs = jnp.concatenate([jnp.log(decay_rates)] * 8, axis=-1)
    field = jnp.exp(place / 32.0 * logs[..., None, None, :])
    return field.reshape(decay_rates.shape[:-1] + (4, 1, 1, 4, 1, 1, width))


def gain_y(decay_rates):
    chan = decay_rates.shape[-1]
    width = 8 * chan
    lanes = jnp.arange(width)
    sub_y = lanes // (2 * chan) % 2
    corner = jnp.arange(4)
    place = (8 * corner[:, None, None] + 2 * corner[None, :, None] + sub_y[None, None, :]).astype(
        jnp.float32
    ) + 0.5
    logs = jnp.concatenate([jnp.log(decay_rates)] * 8, axis=-1)
    field = jnp.exp(place / 32.0 * logs[..., None, None, :])
    return field.reshape(decay_rates.shape[:-1] + (1, 4, 1, 1, 4, 1, width))


def edge_carry(decay_rates):
    places = jnp.arange(24, 32).astype(jnp.float32) + 0.5
    return jnp.mean(jnp.exp(places[:, None] / 32.0 * jnp.log(decay_rates)[None, :]), axis=0)


def compose(earlier, latter):
    factor_early, term_early = earlier
    factor_late, term_late = latter
    return (factor_late * factor_early, jnp.tile(factor_late, 4) * term_early + term_late)


def per_device(latent, occupancy, carry_x, carry_y, w_in, w_down, w_mid, w_up, w_out):
    current = latent[0, 0]
    occupied = occupancy[0, 0]
    rates_x = carry_x[0, 0]
    rates_y = carry_y[0, 0]
    nblocks, cells, width = current.shape
    depth = nblocks // 16
    shaped = (4, 4, depth, 4, 4, 4, width)
    column_num = lax.axis_index("gx")
    row_num = lax.axis_index("gy")
    first_column = column_num == 0
    first_row = row_num == 0
    field_x = gain_x(rates_x)
    field_y = gain_y(rates_y)
    edge_x = edge_carry(rates_x)
    edge_y = edge_carry(rates_y)
    factor_x = jnp.where(first_column, 0.0, edge_x)
    factor_y = jnp.where(first_row, 0.0, edge_y)
    occupied_f = occupied.astype(jnp.float32)
    for step in range(STEPS):
        update = block_net(current, w_in, w_down, w_mid, w_up, w_out) * occupied_f[:, None, None]
        pred = (current.astype(jnp.float32) + update).astype(jnp.bfloat16).reshape(shaped)
        values = pred.astype(jnp.float32)
        west = strip_x(values, 0)
        east = strip_x(values, 3)
        term_x = east - jnp.tile(factor_x, 4) * west
        ignored_x, before_x = prefix(
            (factor_x, term_x), "gx", compose, (jnp.ones_like(factor_x), jnp.zeros_like(term_x))
        )
        drift_x = jnp.where(first_column, 0.0, before_x - west)
        matched = values + field_x * spread_x(drift_x)
        south = strip_y(matched, 0)
        north = strip_y(matched, 3)
        term_y = north - jnp.tile(factor_y, 4) * south
        ignored_y, before_y = prefix(
            (factor_y, term_y), "gy", compose, (jnp.ones_like(factor_y), jnp.zeros_like(term_y))
        )
        drift_y = jnp.where(first_row, 0.0, before_y - south)
        current = (
            (matched + field_y * spread_y(drift_y))
            .astype(jnp.bfloat16)
            .reshape(nblocks, cells, width)
        )
    return current[None, None]


def solution(mesh):
    in_specs = (
        P("gx", "gy", None, None, None),
        P("gx", "gy", None),
        P("gx", "gy", None),
        P("gx", "gy", None),
        P(),
        P(),
        P(),
        P(),
        P(),
    )
    out_specs = P("gx", "gy", None, None, None)
    return jax.shard_map(
        per_device, mesh=mesh, in_specs=in_specs, out_specs=out_specs, check_vma=False
    )
```

profile of v0, /device:TPU:511, one launch (start us, length us, event | category | flops | bytes accessed | tf_op | source)
XLA Modules:
  0.0 300.2 jit_solution(1023508931346438572)
XLA Ops:
  0.1 0.8 broadcast_multiply_fusion.5
  1.1 1.7 fusion.3
  3.7 0.9 pad_slice_fusion.2
  5.0 1.2 copy-done.3
  6.2 2.9 multiply_convert_fusion.2
  11.4 1.3 dynamic-slice.20
  14.0 36.4 %all_gather.13 = f32[32,4,1,4,4,64]{5,4,3,2,1,0:T(4,128)S(1)} all-gather(f32[1,4,1,4,4,64]{5,4,3,2,1,0:T(4,128)S(1)} %fusion.30), channel_id=1, replica_groups=mesh['gx'=32,'gy'=16] {'gx'}, dimensions={0}, use_global_device_ids=true | all-gather | bytes 540672 | tf_op jit(solution)/shard_map/all_gather | solution.py:11
  50.4 55.5 %all-reduce.6 = f32[512]{0:T(512)S(1)} all-reduce(f32[512]{0:T(512)S(1)} %get-tuple-element.364), channel_id=2, replica_groups=mesh['gx'=32,'gy'=16] {'gx'}, use_global_device_ids=true, to_apply=%add.6 | all-reduce | flops 512 | bytes 4096
  105.9 4.9 %while.52 = (s32[]{:T(128)}, f32[4,1,4,4,64]{4,3,2,1,0:T(4,128)S(1)}, s32[]{:T(128)}, f32[32,16]{1,0:T(8,128)S(1)}, f32[32,4,1,4,4,64]{5,4,3,1,2,0:T(4,128)S(1)}, /*index=5*/s32[]{:T(128)}, s32[]{:T(128)}, s32[]{:T(128)}) while((s32[]{:T(128)}, f32[4,1,4,4,64]{4,3,2,1,0:T(4,128)S(1)}, s32[]{:T(128)}, f32[32,16]{1,0:T(8,128)S(1)}, ...), condition=%wide.region_7.10_spmd, body=%wide.region_6.9_spmd.sunk | while | flops 8197 | bytes 50495 | solution.py:19
  112.6 1.3 dynamic-slice.21
  115.3 41.2 %all_gather.15 = f32[16,4,1,4,4,64]{5,4,3,2,1,0:T(4,128)S(1)} all-gather(f32[1,4,1,4,4,64]{5,4,3,2,1,0:T(4,128)S(1)} %subtract_bitcast_fusion.1), channel_id=1, replica_groups=mesh['gx'=32,'gy'=16] {'gy'}, dimensions={0}, use_global_device_ids=true | all-gather | bytes 278528 | tf_op jit(solution)/shard_map/all_gather | solution.py:11
  156.5 24.0 %all-reduce.7 = f32[256]{0:T(256)S(1)} all-reduce(f32[256]{0:T(256)S(1)} %get-tuple-element.362), channel_id=3, replica_groups=mesh['gx'=32,'gy'=16] {'gy'}, use_global_device_ids=true, to_apply=%add.7 | all-reduce | flops 256 | bytes 2048
  180.6 2.6 while.53
  184.1 0.8 multiply_convert_fusion.1
  185.4 1.0 constant_dynamic-update-slice_fusion.13
  186.4 0.9 pad_slice_fusion
  187.2 0.8 constant_dynamic-update-slice_fusion.12
  188.0 0.7 constant_dynamic-update-slice_fusion.11
  188.8 0.7 constant_dynamic-update-slice_fusion.10
  189.5 0.8 constant_dynamic-update-slice_fusion.9
  190.3 0.7 constant_dynamic-update-slice_fusion.8
  191.0 0.8 constant_dynamic-update-slice_fusion.7
  191.8 2.9 multiply_convert_fusion
  196.3 35.7 %all_gather.32 = f32[32,4,1,4,4,64]{5,4,3,2,1,0:T(4,128)S(1)} all-gather(f32[1,4,1,4,4,64]{5,4,3,2,1,0:T(4,128)S(1)} %fusion.26), channel_id=1, replica_groups=mesh['gx'=32,'gy'=16] {'gx'}, dimensions={0}, use_global_device_ids=true | all-gather | bytes 540672 | tf_op jit(solution)/shard_map/all_gather | solution.py:11
  232.0 25.9 %while.54 = (s32[]{:T(128)}, f32[4,1,4,4,64]{4,3,2,1,0:T(4,128)S(1)}, s32[]{:T(128)}, f32[32,16]{1,0:T(8,128)}, f32[32,4,1,4,4,64]{5,4,3,1,2,0:T(4,128)S(1)}, /*index=5*/s32[]{:T(128)}, s32[]{:T(128)}, s32[]{:T(128)}) while((s32[]{:T(128)}, f32[4,1,4,4,64]{4,3,2,1,0:T(4,128)S(1)}, s32[]{:T(128)}, f32[32,16]{1,0:T(8,128)}, ...), condition=%wide.region_21.26_spmd, body=%wide.region_20.25_spmd.sunk | while | flops 8197 | bytes 50495 | solution.py:19
  232.9 0.7 dynamic-slice_bitcast_fusion.10
  233.7 0.7 dynamic-slice_bitcast_fusion.10
  234.5 0.7 dynamic-slice_bitcast_fusion.10
  235.4 0.7 dynamic-slice_bitcast_fusion.10
  259.3 27.0 %all_gather.33 = f32[16,4,1,4,4,64]{5,4,3,2,1,0:T(4,128)S(1)} all-gather(f32[1,4,1,4,4,64]{5,4,3,2,1,0:T(4,128)S(1)} %subtract_bitcast_fusion), channel_id=1, replica_groups=mesh['gx'=32,'gy'=16] {'gy'}, dimensions={0}, use_global_device_ids=true | all-gather | bytes 278528 | tf_op jit(solution)/shard_map/all_gather | solution.py:11
  286.3 12.4 %while.55 = (s32[]{:T(128)}, f32[4,1,4,4,64]{4,3,2,1,0:T(4,128)S(1)}, s32[]{:T(128)}, f32[16,16]{1,0:T(8,128)}, f32[16,4,1,4,4,64]{5,4,3,1,2,0:T(4,128)S(1)}, /*index=5*/s32[]{:T(128)}, s32[]{:T(128)}, s32[]{:T(128)}) while((s32[]{:T(128)}, f32[4,1,4,4,64]{4,3,2,1,0:T(4,128)S(1)}, s32[]{:T(128)}, f32[16,16]{1,0:T(8,128)}, ...), condition=%wide.region_27.32_spmd, body=%wide.region_26.31_spmd.sunk | while | flops 8197 | bytes 50495 | solution.py:19
  299.4 0.8 fusion.10
  (509 shorter events, 51.3 us)
Async XLA Ops:
  0.0 6.2 %copy-start = (bf16[7,128,128]{2,1,0:T(8,128)(2,1)S(1)}, bf16[7,128,128]{2,1,0:T(8,128)(2,1)}, u32[]{:S(2)}) copy-start(bf16[7,128,128]{2,1,0:T(8,128)(2,1)} %param.31) | copy-start | bytes 688132
  1.1 1.8 copy-start.1
  4.5 1.7 copy-start.15
  5.0 1.3 copy-start.3
  9.2 0.7 copy-start.10
  9.2 1.0 copy-start.17
  9.2 1.0 copy-start.2
  9.8 1.5 copy-start.13
  9.8 1.5 copy-start.14
  10.2 0.6 copy-start.11
  13.5 0.5 copy-start.6
  110.9 69.7 %copy-start.4 = (f32[32,16]{1,0:T(8,128)}, f32[32,16]{1,0:T(8,128)S(1)}, u32[]{:S(2)}) copy-start(f32[32,16]{1,0:T(8,128)S(1)} %get-tuple-element.601) | copy-start | bytes 6148
  114.7 0.6 copy-start.8
  183.2 0.9 copy-start.5
  187.2 4.5 %copy-start.16 = (bf16[128,512]{1,0:T(8,128)(2,1)S(1)}, bf16[128,512]{1,0:T(8,128)(2,1)}, u32[]{:S(2)}) copy-start(bf16[128,512]{1,0:T(8,128)(2,1)} %param.32) | copy-start | bytes 393220
  194.7 0.7 copy-start.12
  195.3 1.0 copy-start.7
  232.0 27.2 %copy-start.9 = (f32[64]{0:T(128)S(1)}, f32[64]{0:T(128)}, u32[]{:S(2)}) copy-start(f32[64]{0:T(128)} %copy-done.8) | copy-start | bytes 772
where the time goes:
time: 302 us; the launch traced here: 300 us
  blocking collectives  220 us (73%)
  local copies, waits for them, and re-layouts  56.8 us (19%)
  matrix products  10.3 us (3%)
  other arithmetic  7.92 us (3%)
  loops' own time  3.33 us (1%)
    all_gather x4, blocking collectives, prefix(): gathered = jax.tree.map(lambda a: lax.all_gather(a, axis), part)  140 us
    unnamed x2, blocking collectives  79.5 us
    another operation x184, local copies, waits for them, and re-layouts, compose(): jnp.tile(factor_late, 4) * term_early + term_late  32.7 us
    unnamed x53, local copies, waits for them, and re-layouts  9.29 us
    mul x92, local copies, waits for them, and re-layouts, compose(): jnp.tile(factor_late, 4) * term_early + term_late  7.72 us

commit v1 on v0

v1 whole, which is shorter than its diff:
```python
import functools

import jax
import jax.numpy as jnp
from jax import lax
from jax.experimental import pallas as pl
from jax.experimental.pallas import tpu as pltpu
from jax.sharding import PartitionSpec as P

STEPS = 2
F32 = jnp.float32
BF16 = jnp.bfloat16


def silu(v):
    half = 0.5 * v
    return half + half * jnp.tanh(half)


def iotas(rows):
    sub = lax.broadcasted_iota(jnp.int32, (rows, 128), 0)
    lane = lax.broadcasted_iota(jnp.int32, (rows, 128), 1)
    return sub, lane


def turn_lanes(x, by):
    return pltpu.roll(x, by % 128, x.ndim - 1)


def turn_rows(x, by):
    by = by % x.shape[0]
    return x if by == 0 else pltpu.roll(x, by, 0)


def swap_sy(x, lane):
    return jnp.where((lane // 32) % 2 == 0, turn_lanes(x, -32), turn_lanes(x, 32))


def edge_gain(logs):
    return sum(jnp.exp((p + 0.5) / 32.0 * logs) for p in range(24, 32)) * 0.125


def gain_at(place, logs):
    return jnp.exp(place.astype(F32) / 32.0 * logs + (0.5 / 32.0) * logs)


def widen(narrow, rows, cols):
    r = lax.broadcasted_iota(jnp.int32, (8 * rows, rows), 0) % rows
    k = lax.broadcasted_iota(jnp.int32, (8 * rows, rows), 1)
    tall = jnp.dot((r == k).astype(BF16), narrow, preferred_element_type=F32).astype(BF16)
    k = lax.broadcasted_iota(jnp.int32, (cols, 8 * cols), 0)
    c = lax.broadcasted_iota(jnp.int32, (cols, 8 * cols), 1) % cols
    both = jnp.dot(tall, (k == c).astype(BF16), preferred_element_type=F32)
    r = lax.broadcasted_iota(jnp.int32, (8 * rows, 8 * cols), 0) // rows
    c = lax.broadcasted_iota(jnp.int32, (8 * rows, 8 * cols), 1) // cols
    return jnp.where(r == c, both, 0.0).astype(BF16)


def net(state, aux, weights, scratch, pred_ref, outs):
    w_in, w_down, w_mid, w_up, w_out = weights
    first_ref, second_ref, wide_in_ref, wide_out_ref, line_ref = scratch
    msg_line, msg_x, msg_y, west_ref, south_ref, west_line_ref = outs
    log_x, log_y, col, row, occupied = aux
    wide_in_ref[...] = widen(w_in[...], 16, 64)
    wide_out_ref[...] = widen(w_out[...], 64, 16)
    for qx in range(4):
        rows = pl.ds(256 * qx, 256)
        first = silu(jnp.dot(state[rows, :], wide_in_ref[...], preferred_element_type=F32)).astype(BF16)
        first_ref[rows, :] = first
        pre = jnp.dot(first, w_down[...], preferred_element_type=F32)
        pre = pre * lax.rsqrt(jnp.mean(pre * pre, axis=-1, keepdims=True) + 1e-06)
        second_ref[rows, :] = silu(pre).astype(BF16)

    sub, lane = iotas(16)
    by, bx = sub % 4, sub // 4
    total_x = [[None] * 4 for _ in range(4)]
    south, north = [0.0] * 4, [0.0] * 4
    for qx in range(4):
        base = 256 * qx
        rows = pl.ds(base, 256)
        second = second_ref[rows, :]
        parts = [(0, second)]
        if qx > 0:
            parts.append((1, second_ref[pl.ds(base - 256, 256), :]))
        if qx < 3:
            parts.append((2, second_ref[pl.ds(base + 256, 256), :]))
        gap = jnp.zeros((64, 128), BF16)
        parts.append((3, jnp.concatenate([gap, second[:192]], axis=0)))
        parts.append((4, jnp.concatenate([second[64:], gap], axis=0)))
        gap = jnp.zeros((16, 128), BF16)
        below, above = [], []
        for qy in range(4):
            own = second[64 * qy : 64 * qy + 64]
            below += [gap, own[:48]]
            above += [own[16:], gap]
        parts.append((5, jnp.concatenate(below, axis=0)))
        parts.append((6, jnp.concatenate(above, axis=0)))
        stacked = jnp.concatenate([p for _, p in parts], axis=1)
        mids = jnp.concatenate([w_mid[k] for k, _ in parts], axis=0)
        mixed = jnp.dot(stacked, mids, preferred_element_type=F32)
        middle = (second.astype(F32) + silu(mixed)).astype(BF16)
        upper = jnp.dot(middle, w_up[...], preferred_element_type=F32) + first_ref[rows, :].astype(F32)
        upper = silu(upper).astype(BF16)
        update = jnp.dot(upper, wide_out_ref[...], preferred_element_type=F32)
        update = update.reshape(16, 16, 128) * occupied[None]
        pred = (state[rows, :].astype(F32).reshape(16, 16, 128) + update).astype(BF16)
        pred_ref[rows, :] = pred.reshape(256, 128)
        pred = pred.astype(F32)
        for qy in range(4):
            for qz in range(4):
                value = pred[4 * qy + qz]
                total_x[qy][qz] = value if qx == 0 else total_x[qy][qz] + value
        for qz in range(4):
            s = pred[qz] + pred[4 + qz] + pred[8 + qz] + pred[12 + qz]
            s = (s + swap_sy(s, lane)) * 0.125
            south[qx] = south[qx] + jnp.where(by == qz, turn_rows(s, qz), 0.0)
            north[qx] = north[qx] + jnp.where(by == qz, turn_rows(s, qz - 3), 0.0)

    west, east = [0.0] * 4, [0.0] * 4
    for qy in range(4):
        for qz in range(4):
            s = total_x[qy][qz]
            s = (s + turn_lanes(s, 64)) * 0.125
            west[qy] = west[qy] + jnp.where(bx == qz, turn_rows(s, 4 * qz), 0.0)
            east[qy] = east[qy] + jnp.where(bx == qz, turn_rows(s, 4 * qz + 4), 0.0)
    low_sx, low_sy = lane < 64, (lane // 32) % 2 == 0
    factor_x = jnp.where(col == 0.0, 0.0, edge_gain(log_x))
    factor_y = jnp.where(row == 0.0, 0.0, edge_gain(log_y))
    line_x, line_w = 0.0, 0.0
    for k in range(2):
        w = jnp.where(low_sx, west[k], west[2 + k])
        t = jnp.where(low_sx, east[k], east[2 + k]) - factor_x * w
        west_ref[k] = w
        line_x, line_w = line_x + t, line_w + w
        msg_x[:, pl.ds(16 * k, 16), :] = jnp.broadcast_to(t[None], (msg_x.shape[0], 16, 128))
        s = jnp.where(low_sy, south[k], south[2 + k])
        a = jnp.where(low_sy, north[k], north[2 + k]) - factor_y * s
        south_ref[k] = s
        msg_y[:, pl.ds(16 * k, 16), :] = jnp.broadcast_to(a[None], (msg_y.shape[0], 16, 128))
    part = lane // 32
    lines = []
    for slot, value in enumerate((line_x, line_w)):
        value = value + turn_lanes(value, 64)
        value = (value + turn_lanes(value, 32)) * 0.125
        value = jnp.where(((part == 0) & (by == 0)) | ((part == 3) & (by == 3)), value, 0.0)
        line_ref[slot] = value + turn_rows(value, -3)
        lines.append(line_ref[slot, pl.ds(0, 4, stride=4), :])
    part = iotas(4)[1] // 32
    line = jnp.where(part == 1, factor_x, lines[0])
    msg_line[...] = jnp.broadcast_to(line[None], msg_line.shape)
    west_line_ref[...] = lines[1]


def read_aux(aux_ref):
    logs = jnp.log(aux_ref[0:2, :])
    return logs[0:1], logs[1:2], aux_ref[2:3, :], aux_ref[3:4, :], aux_ref[8:24, :]


def everywhere(x, which):
    part = lax.broadcasted_iota(jnp.int32, x.shape, x.ndim - 1) // 32
    x = jnp.where(part == which, x, 0.0)
    x = x + turn_lanes(x, 32)
    return x + turn_lanes(x, 64)


def middle_kernel(aux_ref, got_line, west_line_ref, msg_v, south_line_ref):
    log_x, log_y, col, row, _ = read_aux(aux_ref)
    factor_y = jnp.where(row == 0.0, 0.0, edge_gain(log_y))
    before = jnp.zeros((4, 128), F32)
    for k in range(got_line.shape[0]):
        value = got_line[k]
        before = jnp.where(col > k, everywhere(value, 1) * before + value, before)
    drift = jnp.where(col == 0.0, 0.0, before - west_line_ref[...])
    south = everywhere(drift, 0)
    line = everywhere(drift, 3) - factor_y * south
    part = iotas(4)[1] // 32
    line = jnp.where(part == 1, factor_y, jnp.where(part == 2, log_x, line))
    msg_v[...] = jnp.broadcast_to(line[None], msg_v.shape)
    south_line_ref[...] = south


def four(line):
    return jnp.concatenate([line] * 4, axis=0)


def seams(aux, pred_ref, got_line, got_x, got_v, got_y, west_ref, south_ref, south_line_ref, put):
    log_x, log_y, col, row, _ = aux
    sub, lane = iotas(16)
    by, bx = sub % 4, sub // 4
    sx, sy = lane // 64, (lane // 32) % 2
    before = [jnp.zeros((16, 128), F32)] * 2
    for k in range(got_x.shape[0]):
        factor = everywhere(got_line[k, 0:1, :], 1)
        go = col > k
        before = [jnp.where(go, factor * before[h] + got_x[k, pl.ds(16 * h, 16), :], before[h]) for h in range(2)]
    drift_x = [jnp.where(col == 0.0, 0.0, before[h] - west_ref[h]) for h in range(2)]
    place = [8 * bx + 2 * (2 * sy + h) + sx for h in range(2)]
    before = [jnp.zeros((16, 128), F32)] * 2
    for k in range(got_y.shape[0]):
        line = got_v[k]
        factor = everywhere(line[0:1], 1)
        logs = everywhere(line[0:1], 2)
        line = four(everywhere(line, 0))
        go = row > k
        before = [
            jnp.where(
                go,
                factor * before[h] + got_y[k, pl.ds(16 * h, 16), :] + gain_at(place[h], logs) * line,
                before[h],
            )
            for h in range(2)
        ]
    south_line = four(south_line_ref[...])
    drift_y = [
        jnp.where(row == 0.0, 0.0, before[h] - south_ref[h] - gain_at(place[h], log_x) * south_line)
        for h in range(2)
    ]
    gain_x = [gain_at(8 * bx + 2 * q + sx, log_x) for q in range(4)]
    gain_y = [gain_at(8 * by + 2 * q + sy, log_y) for q in range(4)]
    spread_x = [[None] * 4 for _ in range(4)]
    spread_y = [[None] * 4 for _ in range(4)]
    for q in range(4):
        d = drift_x[q % 2]
        d = jnp.where(sx == q // 2, d, turn_lanes(d, 64))
        e = drift_y[q % 2]
        e = jnp.where(sy == q // 2, e, swap_sy(e, lane))
        for qz in range(4):
            m = jnp.where(bx == qz, d, 0.0)
            m = m + turn_rows(m, 8)
            spread_x[q][qz] = m + turn_rows(m, 4)
            m = turn_rows(jnp.where(by == qz, e, 0.0), -qz)
            m = m + turn_rows(m, 1)
            spread_y[q][qz] = m + turn_rows(m, 2)
    for qx in range(4):
        for qy in range(4):
            for qz in range(4):
                q = 16 * qx + 4 * qy + qz
                value = pred_ref[pl.ds(16 * q, 16), :].astype(F32)
                value = value + gain_x[qx] * spread_x[qy][qz] + gain_y[qy] * spread_y[qx][qz]
                put(q, value)


def first_kernel(aux_ref, latent, w_in, w_down, w_mid, w_up, w_out, *rest):
    pred_ref, *outs = rest[:7]
    state, *scratch = rest[7:]
    turned = jnp.swapaxes(latent[...].astype(F32), 0, 1)
    state[...] = turned.reshape(1024, 128).astype(BF16)
    net(state, read_aux(aux_ref), (w_in, w_down, w_mid, w_up, w_out), scratch, pred_ref, outs)


def next_kernel(aux_ref, *rest):
    seam_ins, weights, outs, (state, *scratch) = rest[:8], rest[8:13], rest[13:20], rest[20:]
    aux = read_aux(aux_ref)

    def put(q, value):
        state[pl.ds(16 * q, 16), :] = value.astype(BF16)

    seams(aux, *seam_ins, put)
    net(state, aux, weights, scratch, outs[0], outs[1:])


def last_kernel(aux_ref, *rest):
    seam_ins, out, state = rest[:8], rest[8], rest[9]

    def put(q, value):
        state[q] = value

    seams(read_aux(aux_ref), *seam_ins, put)
    out[...] = jnp.swapaxes(state[...], 0, 1).astype(BF16)


def call(kernel, out_shape, scratch, args, name):
    vmem = pl.BlockSpec(memory_space=pltpu.VMEM)
    return pl.pallas_call(
        kernel,
        out_shape=out_shape,
        in_specs=[vmem] * len(args),
        out_specs=jax.tree.map(lambda _: vmem, out_shape),
        scratch_shapes=scratch,
        compiler_params=pltpu.CompilerParams(vmem_limit_bytes=24 * 1024 * 1024),
        name=name,
    )(*args)


def per_device(columns, rows, latent, occupancy, carry_x, carry_y, w_in, w_down, w_mid, w_up, w_out):
    col, row = lax.axis_index("gx"), lax.axis_index("gy")
    aux = jnp.concatenate(
        [
            jnp.tile(carry_x[0, 0], 8)[None],
            jnp.tile(carry_y[0, 0], 8)[None],
            jnp.full((1, 128), col, F32),
            jnp.full((5, 128), row, F32),
            jnp.broadcast_to(occupancy[0, 0].astype(F32)[:, None], (16, 128)),
        ],
        axis=0,
    )
    weights = (w_in, w_down, w_mid, w_up, w_out)
    shape = jax.ShapeDtypeStruct
    net_out = (
        shape((1024, 128), BF16),
        shape((columns, 4, 128), F32),
        shape((columns, 32, 128), F32),
        shape((rows, 32, 128), F32),
        shape((2, 16, 128), F32),
        shape((2, 16, 128), F32),
        shape((4, 128), F32),
    )
    net_scratch = [
        pltpu.VMEM((1024, 128), BF16),
        pltpu.VMEM((1024, 512), BF16),
        pltpu.VMEM((1024, 128), BF16),
        pltpu.VMEM((128, 512), BF16),
        pltpu.VMEM((512, 128), BF16),
        pltpu.VMEM((2, 16, 128), F32),
    ]
    for step in range(STEPS):
        if step == 0:
            outs = call(first_kernel, net_out, net_scratch, (aux, latent[0, 0], *weights), "net_first")
        else:
            outs = call(next_kernel, net_out, net_scratch, (aux, *seam_ins, *weights), "seams_net")
        pred, msg_line, msg_x, msg_y, west, south, west_line = outs
        got_line = lax.all_to_all(msg_line, "gx", 0, 0)
        got_x = lax.all_to_all(msg_x, "gx", 0, 0)
        got_y = lax.all_to_all(msg_y, "gy", 0, 0)
        msg_v, south_line = call(
            middle_kernel,
            (shape((rows, 4, 128), F32), shape((4, 128), F32)),
            [],
            (aux, got_line, west_line),
            "lines",
        )
        got_v = lax.all_to_all(msg_v, "gy", 0, 0)
        seam_ins = (pred, got_line, got_x, got_v, got_y, west, south, south_line)
    out = call(
        last_kernel, shape((16, 64, 128), BF16), [pltpu.VMEM((64, 16, 128), F32)], (aux, *seam_ins), "seams_last"
    )
    return out[None, None]


def solution(mesh):
    in_specs = (
        P("gx", "gy", None, None, None),
        P("gx", "gy", None),
        P("gx", "gy", None),
        P("gx", "gy", None),
        P(),
        P(),
        P(),
        P(),
        P(),
    )
    out_specs = P("gx", "gy", None, None, None)
    return jax.shard_map(
        functools.partial(per_device, mesh.shape["gx"], mesh.shape["gy"]),
        mesh=mesh,
        in_specs=in_specs,
        out_specs=out_specs,
        check_vma=False,
    )
```

time: 302 us -> 152 us (0.50)
  the two profiles are of different devices: /device:TPU:511 before, /device:TPU:1 now
where the time goes in v1:
time: 152 us; the launch traced here: 151 us
  blocking collectives  134 us (88%)
  Pallas kernels  9.65 us (6%)
  local copies, waits for them, and re-layouts  7.31 us (5%)
    all_to_all x2, blocking collectives, per_device(): got_x = lax.all_to_all(msg_x, 'gx', 0, 0)  40 us
    all_to_all x2, blocking collectives, per_device(): got_line = lax.all_to_all(msg_line, 'gx', 0, 0)  33.6 us
    all_to_all x2, blocking collectives, per_device(): got_v = lax.all_to_all(msg_v, 'gy', 0, 0)  31.3 us
    all_to_all x2, blocking collectives, per_device(): got_y = lax.all_to_all(msg_y, 'gy', 0, 0)  29.3 us
    pallas_call x5, Pallas kernels, call(): pl.pallas_call(kernel, out_shape=out_shape, in_specs=[vmem] * len(args),...  9.65 us
    unnamed x25, local copies, waits for them, and re-layouts  7.04 us

profile of v1, /device:TPU:1, one launch (start us, length us, event | category | flops | bytes accessed | tf_op | source)
XLA Modules:
  0.0 151.2 jit_solution(16577137072596708626)
XLA Ops:
  0.0 0.0 copy-start.11
  0.0 0.7 copy-done.11
  0.7 0.0 copy-start.9
  0.7 0.7 copy-done.9
  1.3 0.1 broadcast_in_dim_tile.6
  1.4 0.0 copy-start.10
  1.4 0.7 copy-done.10
  2.1 0.1 broadcast_in_dim_tile.7
  2.1 0.6 copy-done.8
  2.7 0.1 copy.10.w_out.rest_12_
  2.9 0.1 broadcast_in_dim.17
  3.0 0.7 copy-done.7
  3.6 0.9 copy-done
  4.6 0.9 copy-done.2
  5.5 0.9 copy-done.4
  6.4 0.9 copy-done.6
  7.3 3.6 %net_first.1 = (bf16[1024,128]{1,0:T(8,128)(2,1)S(1)}, f32[32,4,128]{2,1,0:T(4,128)S(1)}, f32[32,32,128]{2,1,0:T(8,128)S(1)}, f32[16,32,128]{2,1,0:T(8,128)S(1)}...) custom-call(f32[24,128]{1,0:T(8,128)S(1)} %concatenate.3.aux_ref, ...), custom_call_target="tpu_custom_call" | custom-call | tf_op jit(solution)/shard_map/net_first/pallas_call | solution.py:274
  10.9 19.2 %all_to_all.40.got_line.rest_1_ = f32[32,4,128]{2,1,0:T(4,128)S(1)} all-to-all(f32[32,4,128]{2,1,0:T(4,128)S(1)} %get-tuple-element.24), channel_id=1, replica_groups=mesh['gx'=32,'gy'=16] {'gx'}, dimensions={0} | all-to-all | bytes 131072 | tf_op jit(solution)/shard_map/all_to_all | solution.py:322
  30.1 0.4 lines.2
  30.4 19.6 %all_to_all.41.rest_3_ = f32[16,4,128]{2,1,0:T(4,128)S(1)} all-to-all(f32[16,4,128]{2,1,0:T(4,128)S(1)} %get-tuple-element.27), channel_id=1, replica_groups=mesh['gx'=32,'gy'=16] {'gy'}, dimensions={0} | all-to-all | bytes 65536 | tf_op jit(solution)/shard_map/all_to_all | solution.py:332
  50.1 14.7 %all_to_all.42.rest_4_ = f32[16,32,128]{2,1,0:T(8,128)S(1)} all-to-all(f32[16,32,128]{2,1,0:T(8,128)S(1)} %get-tuple-element.28), channel_id=1, replica_groups=mesh['gx'=32,'gy'=16] {'gy'}, dimensions={0} | all-to-all | bytes 524288 | tf_op jit(solution)/shard_map/all_to_all | solution.py:324
  64.7 20.1 %all_to_all.43.rest_2_ = f32[32,32,128]{2,1,0:T(8,128)S(1)} all-to-all(f32[32,32,128]{2,1,0:T(8,128)S(1)} %get-tuple-element.25), channel_id=1, replica_groups=mesh['gx'=32,'gy'=16] {'gx'}, dimensions={0} | all-to-all | bytes 1048576 | tf_op jit(solution)/shard_map/all_to_all | solution.py:323
  84.8 0.0 copy-done.1
  84.8 0.0 copy-done.3
  84.8 0.0 copy-done.5
  84.8 4.0 %seams_net.1 = (bf16[1024,128]{1,0:T(8,128)(2,1)S(1)}, f32[32,4,128]{2,1,0:T(4,128)S(1)}, f32[32,32,128]{2,1,0:T(8,128)S(1)}, f32[16,32,128]{2,1,0:T(8,128)S(1)}...) custom-call(f32[24,128]{1,0:T(8,128)S(1)} %concatenate.3.aux_ref, ...), custom_call_target="tpu_custom_call" | custom-call | tf_op jit(solution)/shard_map/seams_net/pallas_call | solution.py:274
  88.8 14.4 %all_to_all.44.got_line.rest_1_ = f32[32,4,128]{2,1,0:T(4,128)S(1)} all-to-all(f32[32,4,128]{2,1,0:T(4,128)S(1)} %get-tuple-element.33), channel_id=1, replica_groups=mesh['gx'=32,'gy'=16] {'gx'}, dimensions={0} | all-to-all | bytes 131072 | tf_op jit(solution)/shard_map/all_to_all | solution.py:322
  103.2 0.4 lines.3
  103.6 11.7 %all_to_all.45.rest_3_ = f32[16,4,128]{2,1,0:T(4,128)S(1)} all-to-all(f32[16,4,128]{2,1,0:T(4,128)S(1)} %get-tuple-element.36), channel_id=1, replica_groups=mesh['gx'=32,'gy'=16] {'gy'}, dimensions={0} | all-to-all | bytes 65536 | tf_op jit(solution)/shard_map/all_to_all | solution.py:332
  115.3 14.7 %all_to_all.46.rest_4_ = f32[16,32,128]{2,1,0:T(8,128)S(1)} all-to-all(f32[16,32,128]{2,1,0:T(8,128)S(1)} %get-tuple-element.37), channel_id=1, replica_groups=mesh['gx'=32,'gy'=16] {'gy'}, dimensions={0} | all-to-all | bytes 524288 | tf_op jit(solution)/shard_map/all_to_all | solution.py:324
  129.9 19.9 %all_to_all.47.rest_2_ = f32[32,32,128]{2,1,0:T(8,128)S(1)} all-to-all(f32[32,32,128]{2,1,0:T(8,128)S(1)} %get-tuple-element.34), channel_id=1, replica_groups=mesh['gx'=32,'gy'=16] {'gx'}, dimensions={0} | all-to-all | bytes 1048576 | tf_op jit(solution)/shard_map/all_to_all | solution.py:323
  149.8 1.4 seams_last.1
  (15 shorter events, 0.1 us)
Async XLA Ops:
  0.0 0.7 copy-start.11
  0.7 0.7 copy-start.9
  1.4 0.7 copy-start.10
  2.1 0.7 copy-start.8
  2.9 0.7 copy-start.7
  3.6 0.9 copy-start
  4.6 0.9 copy-start.2
  5.5 0.9 copy-start.4
  6.4 0.9 copy-start.6
  64.7 20.1 %copy-start.1 = (bf16[7,128,128]{2,1,0:T(8,128)(2,1)S(1)}, bf16[7,128,128]{2,1,0:T(8,128)(2,1)}, u32[]{:S(2)}) copy-start(bf16[7,128,128]{2,1,0:T(8,128)(2,1)} %rest_10_.1) | copy-start | bytes 688132
  64.7 20.1 %copy-start.3 = (bf16[512,128]{1,0:T(8,128)(2,1)S(1)}, bf16[512,128]{1,0:T(8,128)(2,1)}, u32[]{:S(2)}) copy-start(bf16[512,128]{1,0:T(8,128)(2,1)} %rest_9_.1) | copy-start | bytes 393220
  64.7 20.1 %copy-start.5 = (bf16[128,512]{1,0:T(8,128)(2,1)S(1)}, bf16[128,512]{1,0:T(8,128)(2,1)}, u32[]{:S(2)}) copy-start(bf16[128,512]{1,0:T(8,128)(2,1)} %rest_11_.1) | copy-start | bytes 393220

commit v2 on v1

v2 whole, which is shorter than its diff:
```python
import functools

import jax
import jax.numpy as jnp
from jax import lax
from jax.experimental import pallas as pl
from jax.experimental.pallas import tpu as pltpu
from jax.sharding import PartitionSpec as P

STEPS = 2
F32 = jnp.float32
BF16 = jnp.bfloat16


def silu(v):
    half = 0.5 * v
    return half + half * jnp.tanh(half)


def iotas(rows):
    sub = lax.broadcasted_iota(jnp.int32, (rows, 128), 0)
    lane = lax.broadcasted_iota(jnp.int32, (rows, 128), 1)
    return sub, lane


def turn_lanes(x, by):
    return pltpu.roll(x, by % 128, x.ndim - 1)


def turn_rows(x, by):
    by = by % x.shape[0]
    return x if by == 0 else pltpu.roll(x, by, 0)


def swap_sy(x, lane):
    return jnp.where((lane // 32) % 2 == 0, turn_lanes(x, -32), turn_lanes(x, 32))


def edge_gain(logs):
    return sum(jnp.exp((p + 0.5) / 32.0 * logs) for p in range(24, 32)) * 0.125


def gain_at(place, logs):
    return jnp.exp(place.astype(F32) / 32.0 * logs + (0.5 / 32.0) * logs)


def widen(narrow, rows, cols):
    r = lax.broadcasted_iota(jnp.int32, (8 * rows, rows), 0) % rows
    k = lax.broadcasted_iota(jnp.int32, (8 * rows, rows), 1)
    tall = jnp.dot((r == k).astype(BF16), narrow, preferred_element_type=F32).astype(BF16)
    k = lax.broadcasted_iota(jnp.int32, (cols, 8 * cols), 0)
    c = lax.broadcasted_iota(jnp.int32, (cols, 8 * cols), 1) % cols
    both = jnp.dot(tall, (k == c).astype(BF16), preferred_element_type=F32)
    r = lax.broadcasted_iota(jnp.int32, (8 * rows, 8 * cols), 0) // rows
    c = lax.broadcasted_iota(jnp.int32, (8 * rows, 8 * cols), 1) // cols
    return jnp.where(r == c, both, 0.0)


def net(state, aux, weights, first_ref, second_ref, pred_ref, outs):
    wide_in, w_down, w_mid, w_up, wide_out = weights
    msg, west_ref, south_ref, north_ref = outs
    log_x, occupied, col = aux.log_x, aux.occupied, aux.col
    for qx in range(4):
        rows = pl.ds(256 * qx, 256)
        first = silu(jnp.dot(state[rows, :], wide_in[...], preferred_element_type=F32)).astype(BF16)
        first_ref[rows, :] = first
        pre = jnp.dot(first, w_down[...], preferred_element_type=F32)
        pre = pre * lax.rsqrt(jnp.mean(pre * pre, axis=-1, keepdims=True) + 1e-06)
        second_ref[rows, :] = silu(pre).astype(BF16)

    sub, lane = iotas(16)
    by, bx = sub % 4, sub // 4
    total_x = [[None] * 4 for _ in range(4)]
    south, north = [0.0] * 4, [0.0] * 4
    for qx in range(4):
        base = 256 * qx
        rows = pl.ds(base, 256)
        second = second_ref[rows, :]
        parts = [(0, second)]
        if qx > 0:
            parts.append((1, second_ref[pl.ds(base - 256, 256), :]))
        if qx < 3:
            parts.append((2, second_ref[pl.ds(base + 256, 256), :]))
        gap = jnp.zeros((64, 128), BF16)
        parts.append((3, jnp.concatenate([gap, second[:192]], axis=0)))
        parts.append((4, jnp.concatenate([second[64:], gap], axis=0)))
        gap = jnp.zeros((16, 128), BF16)
        below, above = [], []
        for qy in range(4):
            own = second[64 * qy : 64 * qy + 64]
            below += [gap, own[:48]]
            above += [own[16:], gap]
        parts.append((5, jnp.concatenate(below, axis=0)))
        parts.append((6, jnp.concatenate(above, axis=0)))
        stacked = jnp.concatenate([p for _, p in parts], axis=1)
        mids = jnp.concatenate([w_mid[k] for k, _ in parts], axis=0)
        mixed = jnp.dot(stacked, mids, preferred_element_type=F32)
        middle = (second.astype(F32) + silu(mixed)).astype(BF16)
        upper = jnp.dot(middle, w_up[...], preferred_element_type=F32) + first_ref[rows, :].astype(F32)
        upper = silu(upper).astype(BF16)
        update = jnp.dot(upper, wide_out[...], preferred_element_type=F32)
        update = update.reshape(16, 16, 128) * occupied[None]
        pred = (state[rows, :].astype(F32).reshape(16, 16, 128) + update).astype(BF16)
        pred_ref[rows, :] = pred.reshape(256, 128)
        pred = pred.astype(F32)
        for qy in range(4):
            for qz in range(4):
                value = pred[4 * qy + qz]
                total_x[qy][qz] = value if qx == 0 else total_x[qy][qz] + value
        for qz in range(4):
            s = pred[qz] + pred[4 + qz] + pred[8 + qz] + pred[12 + qz]
            s = (s + swap_sy(s, lane)) * 0.125
            south[qx] = south[qx] + jnp.where(by == qz, turn_rows(s, qz), 0.0)
            north[qx] = north[qx] + jnp.where(by == qz, turn_rows(s, qz - 3), 0.0)

    west, east = [0.0] * 4, [0.0] * 4
    for qy in range(4):
        for qz in range(4):
            s = total_x[qy][qz]
            s = (s + turn_lanes(s, 64)) * 0.125
            west[qy] = west[qy] + jnp.where(bx == qz, turn_rows(s, 4 * qz), 0.0)
            east[qy] = east[qy] + jnp.where(bx == qz, turn_rows(s, 4 * qz + 4), 0.0)
    low_sx, low_sy = lane < 64, (lane // 32) % 2 == 0
    factor = jnp.where(col == 0.0, 0.0, edge_gain(log_x))
    for h in range(2):
        w = jnp.where(low_sx, west[h], west[2 + h])
        t = jnp.where(low_sx, east[h], east[2 + h]) - factor * w
        west_ref[h] = w
        south_ref[h] = jnp.where(low_sy, south[h], south[2 + h])
        north_ref[h] = jnp.where(low_sy, north[h], north[2 + h])
        msg[:, pl.ds(16 * h, 16), :] = jnp.broadcast_to(t[None], (msg.shape[0], 16, 128))
    msg[:, 32:40, :] = jnp.broadcast_to(factor[None], (msg.shape[0], 8, 128))


class Aux:
    def __init__(self, ref):
        self.log_x, self.log_y = ref[0:1, :], ref[1:2, :]
        self.col, self.outer, self.inner, self.row = (ref[k : k + 1, :] for k in range(2, 6))
        self.occupied = ref[8:24, :]


def scan(got, place, planes, factor_row):
    zero, one = [jnp.zeros((16, 128), F32)] * 2, jnp.ones((1, 128), F32)
    before, before_f, total, total_f = zero, one, zero, one
    for k in range(got.shape[0]):
        f = got[k, factor_row : factor_row + 1, :]
        t = [got[k, pl.ds(16 * h, 16), :] for h in range(2)]
        go = place > k
        before = [jnp.where(go, f * before[h] + t[h], before[h]) for h in range(2)]
        before_f = jnp.where(go, f * before_f, before_f)
        total = [f * total[h] + t[h] for h in range(2)]
        total_f = f * total_f
    return before, before_f, total, total_f


def group_kernel(aux_ref, got, msg, prefix_ref, prefix_f_ref):
    before, before_f, total, total_f = scan(got, Aux(aux_ref).inner, 2, 32)
    for h in range(2):
        prefix_ref[h] = before[h]
        msg[:, pl.ds(16 * h, 16), :] = jnp.broadcast_to(total[h][None], (msg.shape[0], 16, 128))
    msg[:, 32:40, :] = jnp.broadcast_to(total_f[None], (msg.shape[0], 8, 128))
    prefix_f_ref[...] = jnp.broadcast_to(before_f, (8, 128))


def four(line):
    return jnp.concatenate([line] * 4, axis=0)


def place_y(lane, bx):
    return [8 * bx + 2 * (2 * ((lane // 32) % 2) + h) + lane // 64 for h in range(2)]


def turn_kernel(aux_ref, got, prefix_ref, prefix_f_ref, west_ref, south_ref, north_ref, msg, drift_ref, low_ref, line_ref):
    aux = Aux(aux_ref)
    sub, lane = iotas(16)
    start, _, _, _ = scan(got, aux.outer, 2, 32)
    line = 0.0
    for h in range(2):
        drift = prefix_f_ref[0:1, :] * start[h] + prefix_ref[h] - west_ref[h]
        drift = jnp.where(aux.col == 0.0, 0.0, drift)
        drift_ref[h] = drift
        line = line + drift
    line = line + turn_lanes(line, 64)
    line = (line + turn_lanes(line, 32)) * 0.125
    factor = jnp.where(aux.row == 0.0, 0.0, edge_gain(aux.log_y))
    line_ref[0] = line
    line_ref[1] = turn_rows(line, -3) - factor * line
    south_line = four(line_ref[0, pl.ds(0, 4, stride=4), :])
    term_line = four(line_ref[1, pl.ds(0, 4, stride=4), :])
    places = place_y(lane, sub // 4)
    for h in range(2):
        gain = gain_at(places[h], aux.log_x)
        low_ref[h] = south_ref[h] + gain * south_line
        term = north_ref[h] - factor * south_ref[h] + gain * term_line
        msg[:, pl.ds(16 * h, 16), :] = jnp.broadcast_to(term[None], (msg.shape[0], 16, 128))
    if msg.shape[1] > 32:
        msg[:, 32:40, :] = jnp.broadcast_to(factor[None], (msg.shape[0], 8, 128))


def seams(aux, pred_ref, got, factors, drift_ref, low_ref, put):
    sub, lane = iotas(16)
    by, bx = sub % 4, sub // 4
    sx, sy = lane // 64, (lane // 32) % 2
    before = [jnp.zeros((16, 128), F32)] * 2
    for k in range(got.shape[0]):
        f, go = factors(k), aux.row > k
        before = [jnp.where(go, f * before[h] + got[k, pl.ds(16 * h, 16), :], before[h]) for h in range(2)]
    drift_y = [jnp.where(aux.row == 0.0, 0.0, before[h] - low_ref[h]) for h in range(2)]
    drift_x = [drift_ref[h] for h in range(2)]
    gain_x = [gain_at(8 * bx + 2 * q + sx, aux.log_x) for q in range(4)]
    gain_y = [gain_at(8 * by + 2 * q + sy, aux.log_y) for q in range(4)]
    spread_x = [[None] * 4 for _ in range(4)]
    spread_y = [[None] * 4 for _ in range(4)]
    for q in range(4):
        d = drift_x[q % 2]
        d = jnp.where(sx == q // 2, d, turn_lanes(d, 64))
        e = drift_y[q % 2]
        e = jnp.where(sy == q // 2, e, swap_sy(e, lane))
        for qz in range(4):
            m = jnp.where(bx == qz, d, 0.0)
            m = m + turn_rows(m, 8)
            spread_x[q][qz] = m + turn_rows(m, 4)
            m = turn_rows(jnp.where(by == qz, e, 0.0), -qz)
            m = m + turn_rows(m, 1)
            spread_y[q][qz] = m + turn_rows(m, 2)
    for qx in range(4):
        for qy in range(4):
            for qz in range(4):
                q = 16 * qx + 4 * qy + qz
                value = pred_ref[pl.ds(16 * q, 16), :].astype(F32)
                value = value + gain_x[qx] * spread_x[qy][qz] + gain_y[qy] * spread_y[qx][qz]
                put(q, value)


def first_kernel(inner, latent, occupancy, carry_x, carry_y, w_in, w_down, w_mid, w_up, w_out, *rest):
    pred_ref, msg, west, south, north, aux_ref, wide_in, wide_out = rest[:8]
    latent_v, occupancy_v, carry_x_v, carry_y_v, w_in_v, w_down_v, w_mid_v, w_up_v, w_out_v = rest[8:17]
    state, first_ref, second_ref, sems = rest[17:]
    pairs = [
        (w_in, w_in_v),
        (w_out, w_out_v),
        (occupancy, occupancy_v),
        (carry_x, carry_x_v),
        (carry_y, carry_y_v),
        (latent, latent_v),
        (w_down, w_down_v),
        (w_mid, w_mid_v),
        (w_up, w_up_v),
    ]
    copies = [pltpu.make_async_copy(src, dst, sems.at[k]) for k, (src, dst) in enumerate(pairs)]
    for copy in copies:
        copy.start()
    col, row = lax.axis_index("gx"), lax.axis_index("gy")
    for copy in copies[:5]:
        copy.wait()
    wide_in[...] = widen(w_in_v[...], 16, 64).astype(BF16)
    wide_out[...] = widen(w_out_v[...], 16, 64).T.astype(BF16)
    rates = jnp.concatenate([carry_x_v[...], carry_y_v[...]], axis=0)
    rates = jnp.concatenate([rates] * 8, axis=1)
    aux_ref[0:2, :] = jnp.log(rates)
    for k, place in enumerate((col, col // inner, col % inner, row)):
        aux_ref[2 + k : 3 + k, :] = jnp.full((1, 128), place, jnp.int32).astype(F32)
    r, c = (lax.broadcasted_iota(jnp.int32, (16, 16), k) for k in (0, 1))
    occupied = jnp.where(r == c, occupancy_v[...].astype(F32), 0.0)
    aux_ref[8:24, :] = jnp.broadcast_to(jnp.sum(occupied, axis=1, keepdims=True), (16, 128))
    copies[5].wait()
    turned = jnp.swapaxes(latent_v[...].astype(F32), 0, 1)
    state[...] = turned.reshape(1024, 128).astype(BF16)
    for copy in copies[6:]:
        copy.wait()
    weights = (wide_in, w_down_v, w_mid_v, w_up_v, wide_out)
    net(state, Aux(aux_ref), weights, first_ref, second_ref, pred_ref, (msg, west, south, north))


def next_kernel(aux_ref, pred, got, drift, low, wide_in, w_down, w_mid, w_up, wide_out, *rest):
    outs, (factor_ref, state, first_ref, second_ref) = rest[:5], rest[5:]
    aux = Aux(aux_ref)
    for k in range(got.shape[0]):
        factor_ref[k : k + 1, :] = got[k, 32:33, :]

    def put(q, value):
        state[pl.ds(16 * q, 16), :] = value.astype(BF16)

    seams(aux, pred, got, lambda k: got[k, 32:33, :], drift, low, put)
    net(state, aux, (wide_in, w_down, w_mid, w_up, wide_out), first_ref, second_ref, outs[0], outs[1:])


def last_kernel(aux_ref, pred, got, drift, low, factor_ref, out, state):
    def put(q, value):
        state[q] = value

    seams(Aux(aux_ref), pred, got, lambda k: factor_ref[k : k + 1, :], drift, low, put)
    out[...] = jnp.swapaxes(state[...], 0, 1).astype(BF16)


def call(kernel, out_shape, scratch, args, name, space=pltpu.VMEM, limit=24):
    vmem = pl.BlockSpec(memory_space=pltpu.VMEM)
    return pl.pallas_call(
        kernel,
        out_shape=out_shape,
        in_specs=[pl.BlockSpec(memory_space=space)] * len(args),
        out_specs=jax.tree.map(lambda _: vmem, out_shape),
        scratch_shapes=scratch,
        compiler_params=pltpu.CompilerParams(vmem_limit_bytes=limit * 1024 * 1024),
        name=name,
    )(*args)


def per_device(columns, rows, latent, occupancy, carry_x, carry_y, w_in, w_down, w_mid, w_up, w_out):
    inner = 8 if columns % 8 == 0 else 2
    outer = columns // inner
    near = [[inner * a + b for b in range(inner)] for a in range(outer)]
    far = [[inner * a + b for a in range(outer)] for b in range(inner)]
    shape = jax.ShapeDtypeStruct
    plane = shape((2, 16, 128), F32)
    net_out = (shape((1024, 128), BF16), shape((inner, 40, 128), F32), plane, plane, plane)
    net_scratch = [
        pltpu.VMEM((1024, 128), BF16),
        pltpu.VMEM((1024, 512), BF16),
        pltpu.VMEM((1024, 128), BF16),
    ]
    for step in range(STEPS):
        if step == 0:
            args = (latent[0, 0], occupancy[0], carry_x[0], carry_y[0], w_in, w_down, w_mid, w_up, w_out.T)
            held = [pltpu.VMEM(a.shape, a.dtype) for a in args]
            *outs, aux, wide_in, wide_out = call(
                functools.partial(first_kernel, inner),
                (*net_out, shape((24, 128), F32), shape((128, 512), BF16), shape((512, 128), BF16)),
                held + net_scratch + [pltpu.SemaphoreType.DMA((len(args),))],
                args,
                "net_first",
                pl.ANY,
                60,
            )
        else:
            factors, *outs = call(
                next_kernel,
                (*net_out, shape((rows, 128), F32)),
                net_scratch,
                (aux, *seam_ins, wide_in, w_down, w_mid, w_up, wide_out),
                "seams_net",
            )[::-1]
            outs = outs[::-1]
        pred, msg, west, south, north = outs
        got = lax.all_to_all(msg, "gx", 0, 0, axis_index_groups=near)
        msg, prefix, prefix_f = call(
            group_kernel, (shape((outer, 40, 128), F32), plane, shape((8, 128), F32)), [], (aux, got), "group"
        )
        got = lax.all_to_all(msg, "gx", 0, 0, axis_index_groups=far)
        msg, drift, low = call(
            turn_kernel,
            (shape((rows, 40 if step == 0 else 32, 128), F32), plane, plane),
            [pltpu.VMEM((2, 16, 128), F32)],
            (aux, got, prefix, prefix_f, west, south, north),
            "turn",
        )
        got = lax.all_to_all(msg, "gy", 0, 0)
        seam_ins = (pred, got, drift, low)
    out = call(
        last_kernel,
        shape((16, 64, 128), BF16),
        [pltpu.VMEM((64, 16, 128), F32)],
        (aux, *seam_ins, factors),
        "seams_last",
    )
    return out[None, None]


def solution(mesh):
    in_specs = (
        P("gx", "gy", None, None, None),
        P("gx", "gy", None),
        P("gx", "gy", None),
        P("gx", "gy", None),
        P(),
        P(),
        P(),
        P(),
        P(),
    )
    out_specs = P("gx", "gy", None, None, None)
    return jax.shard_map(
        functools.partial(per_device, mesh.shape["gx"], mesh.shape["gy"]),
        mesh=mesh,
        in_specs=in_specs,
        out_specs=out_specs,
        check_vma=False,
    )
```

time: 152 us -> 97.6 us (0.64)
  blocking collectives: 134 us -> 86.9 us
  local copies, waits for them, and re-layouts: 7.31 us -> 0.05 us
    all_to_all x8 -> x6, blocking collectives: 134 us -> 86.9 us  [the longest x2 43 us: per_device(): got = lax.all_to_all(msg, 'gy', 0, 0)]
    unnamed x25 -> x20, local copies, waits for them, and re-layouts: 7.04 us -> 0.05 us
    pallas_call x5 -> x7, Pallas kernels: 9.65 us -> 10.1 us  [call(): pl.pallas_call(kernel, out_shape=out_shape, in_specs=[pl.BlockSpec(memory...]
where the time goes in v2:
time: 97.6 us; the launch traced here: 97.2 us
  blocking collectives  86.9 us (89%)
  Pallas kernels  10.1 us (10%)
    all_to_all x2, blocking collectives, per_device(): got = lax.all_to_all(msg, 'gy', 0, 0)  43 us
    all_to_all x2, blocking collectives, per_device(): got = lax.all_to_all(msg, 'gx', 0, 0, axis_index_groups=near)  28.6 us
    all_to_all x2, blocking collectives, per_device(): got = lax.all_to_all(msg, 'gx', 0, 0, axis_index_groups=far)  15.2 us
    pallas_call x7, Pallas kernels, call(): pl.pallas_call(kernel, out_shape=out_shape, in_specs=[pl.BlockSpec(memory...  10.1 us

profile of v2, /device:TPU:1, one launch (start us, length us, event | category | flops | bytes accessed | tf_op | source)
XLA Modules:
  0.0 97.2 jit_solution(1570239233097970265)
XLA Ops:
  0.0 5.3 %net_first.1 = (bf16[1024,128]{1,0:T(8,128)(2,1)}, f32[8,40,128]{2,1,0:T(8,128)}, f32[2,16,128]{2,1,0:T(8,128)}, f32[2,16,128]{2,1,0:T(8,128)}, f32[2,16,128]{2,...) custom-call(bf16[16,64,128]{2,1,0:T(8,128)(2,1)} %bitcast.6, ...), custom_call_target="tpu_custom_call" | custom-call | tf_op jit(solution)/shard_map/net_first/pallas_call | solution.py:298
  5.3 0.0 copy-start.3
  5.3 16.0 %all_to_all.30.got = f32[8,40,128]{2,1,0:T(8,128)S(1)} all-to-all(f32[8,40,128]{2,1,0:T(8,128)} %get-tuple-element.33), channel_id=1, replica_groups={{0,16,32,48,64,80,96,112},{128,144,160,176,192,208,224,240},{256,272,28..., dimensions={0} | all-to-all | bytes 327680 | tf_op jit(solution)/shard_map/all_to_all | solution.py:345
  21.4 0.0 copy-done.3
  21.4 0.0 copy-start.9
  21.4 0.0 copy-start.6
  21.4 0.0 copy-start.7
  21.4 0.0 copy-start.8
  21.4 0.0 copy-start.5
  21.4 8.3 %all_to_all.31.got = f32[4,40,128]{2,1,0:T(8,128)S(1)} all-to-all(f32[4,40,128]{2,1,0:T(8,128)S(1)} %get-tuple-element.34), channel_id=1, replica_groups={{0,128,256,384},{16,144,272,400},{32,160,288,416},{48,176,304,432},{64,..., dimensions={0} | all-to-all | bytes 163840 | tf_op jit(solution)/shard_map/all_to_all | solution.py:349
  29.7 0.0 copy-done.9
  29.7 0.0 copy-done.7
  29.7 0.0 copy-done.8
  29.7 0.0 copy-start.4
  29.8 0.2 turn.2
  30.0 0.0 copy-start
  30.0 0.0 copy-start.1
  30.0 0.0 copy-start.2
  30.0 27.3 %all_to_all.32.got = f32[16,40,128]{2,1,0:T(8,128)S(1)} all-to-all(f32[16,40,128]{2,1,0:T(8,128)S(1)} %get-tuple-element.40), channel_id=1, replica_groups=mesh['gx'=32,'gy'=16] {'gy'}, dimensions={0} | all-to-all | bytes 655360 | tf_op jit(solution)/shard_map/all_to_all | solution.py:357
  57.3 0.0 copy-done.6
  57.3 0.0 copy-done.5
  57.3 0.0 copy-done.4
  57.3 0.0 copy-done
  57.3 0.0 copy-done.1
  57.3 0.0 copy-done.2
  57.3 3.3 %seams_net.1 = (bf16[1024,128]{1,0:T(8,128)(2,1)S(1)}, f32[8,40,128]{2,1,0:T(8,128)S(1)}, f32[2,16,128]{2,1,0:T(8,128)S(1)}, f32[2,16,128]{2,1,0:T(8,128)S(1)}, ...) custom-call(f32[24,128]{1,0:T(8,128)S(1)} %copy-done.3, bf16[1024,128]{1,0:T(8,128)(2,1)S(1)} %copy-done.4, ...), custom_call_target="tpu_custom_call" | custom-call | tf_op jit(solution)/shard_map/seams_net/pallas_call | solution.py:298
  60.7 12.6 %all_to_all.33.got = f32[8,40,128]{2,1,0:T(8,128)S(1)} all-to-all(f32[8,40,128]{2,1,0:T(8,128)S(1)} %get-tuple-element.46), channel_id=1, replica_groups={{0,16,32,48,64,80,96,112},{128,144,160,176,192,208,224,240},{256,272,28..., dimensions={0} | all-to-all | bytes 327680 | tf_op jit(solution)/shard_map/all_to_all | solution.py:345
  73.3 6.9 %all_to_all.34.got = f32[4,40,128]{2,1,0:T(8,128)S(1)} all-to-all(f32[4,40,128]{2,1,0:T(8,128)S(1)} %get-tuple-element.47), channel_id=1, replica_groups={{0,128,256,384},{16,144,272,400},{32,160,288,416},{48,176,304,432},{64,..., dimensions={0} | all-to-all | bytes 163840 | tf_op jit(solution)/shard_map/all_to_all | solution.py:349
  80.2 0.2 turn.3
  80.4 15.7 %all_to_all.35.got = f32[16,32,128]{2,1,0:T(8,128)S(1)} all-to-all(f32[16,32,128]{2,1,0:T(8,128)S(1)} %get-tuple-element.53), channel_id=1, replica_groups=mesh['gx'=32,'gy'=16] {'gy'}, dimensions={0} | all-to-all | bytes 524288 | tf_op jit(solution)/shard_map/all_to_all | solution.py:357
  96.1 1.1 %seams_last.1 = bf16[16,64,128]{2,1,0:T(8,128)(2,1)} custom-call(f32[24,128]{1,0:T(8,128)S(1)} %copy-done.3, bf16[1024,128]{1,0:T(8,128)(2,1)S(1)} %get-tuple-element.45.pred, f32[16,32,128]{2,1,0:T(8,128)S(1)} %all_to_all.35.got, f32[2,16,128]{2,1,0:T(8,128)S(1)} %get-tuple-element.54.drift, f32[2,16,128]{2,1,0:T(8,128)S(1)} %get-tuple-element.55.low, ...), custom_call_target="tpu_custom_call" | custom-call | tf_op jit(solution)/shard_map/seams_last/pallas_call | solution.py:298
  (2 shorter events, 0.1 us)
Async XLA Ops:
  5.3 16.1 %copy-start.3 = (f32[24,128]{1,0:T(8,128)S(1)}, f32[24,128]{1,0:T(8,128)}, u32[]{:S(2)}) copy-start(f32[24,128]{1,0:T(8,128)} %get-tuple-element.31.aux_ref) | copy-start | bytes 36868
  21.4 8.4 %copy-start.9 = (f32[2,16,128]{2,1,0:T(8,128)S(1)}, f32[2,16,128]{2,1,0:T(8,128)}, u32[]{:S(2)}) copy-start(f32[2,16,128]{2,1,0:T(8,128)} %get-tuple-element.39.north_ref) | copy-start | bytes 49156
  21.4 35.9 %copy-start.6 = (bf16[512,128]{1,0:T(8,128)(2,1)S(1)}, bf16[512,128]{1,0:T(8,128)(2,1)}, u32[]{:S(2)}) copy-start(bf16[512,128]{1,0:T(8,128)(2,1)} %get-tuple-element.44.wide_out) | copy-start | bytes 393220
  21.4 8.3 %copy-start.7 = (f32[2,16,128]{2,1,0:T(8,128)S(1)}, f32[2,16,128]{2,1,0:T(8,128)}, u32[]{:S(2)}) copy-start(f32[2,16,128]{2,1,0:T(8,128)} %get-tuple-element.37.west_ref) | copy-start | bytes 49156
  21.4 8.3 %copy-start.8 = (f32[2,16,128]{2,1,0:T(8,128)S(1)}, f32[2,16,128]{2,1,0:T(8,128)}, u32[]{:S(2)}) copy-start(f32[2,16,128]{2,1,0:T(8,128)} %get-tuple-element.38.south_ref) | copy-start | bytes 49156
  21.4 35.9 %copy-start.5 = (bf16[128,512]{1,0:T(8,128)(2,1)S(1)}, bf16[128,512]{1,0:T(8,128)(2,1)}, u32[]{:S(2)}) copy-start(bf16[128,512]{1,0:T(8,128)(2,1)} %get-tuple-element.43.wide_in) | copy-start | bytes 393220
  29.7 27.6 %copy-start.4 = (bf16[1024,128]{1,0:T(8,128)(2,1)S(1)}, bf16[1024,128]{1,0:T(8,128)(2,1)}, u32[]{:S(2)}) copy-start(bf16[1024,128]{1,0:T(8,128)(2,1)} %get-tuple-element.32.pred) | copy-start | bytes 786436
  30.0 27.4 %copy-start = (bf16[7,128,128]{2,1,0:T(8,128)(2,1)S(1)}, bf16[7,128,128]{2,1,0:T(8,128)(2,1)}, u32[]{:S(2)}) copy-start(bf16[7,128,128]{2,1,0:T(8,128)(2,1)} %w_mid.3) | copy-start | bytes 688132
  30.0 27.4 %copy-start.1 = (bf16[512,128]{1,0:T(8,128)(2,1)S(1)}, bf16[512,128]{1,0:T(8,128)(2,1)}, u32[]{:S(2)}) copy-start(bf16[512,128]{1,0:T(8,128)(2,1)} %w_down.3) | copy-start | bytes 393220
  30.0 27.4 %copy-start.2 = (bf16[128,512]{1,0:T(8,128)(2,1)S(1)}, bf16[128,512]{1,0:T(8,128)(2,1)}, u32[]{:S(2)}) copy-start(bf16[128,512]{1,0:T(8,128)(2,1)} %w_up.3) | copy-start | bytes 393220

commit v3 on v2

--- a/solution.py
+++ b/solution.py
@@ -122,89 +122,152 @@
             east[qy] = east[qy] + jnp.where(bx == qz, turn_rows(s, 4 * qz + 4), 0.0)
     low_sx, low_sy = lane < 64, (lane // 32) % 2 == 0
     factor = jnp.where(col == 0.0, 0.0, edge_gain(log_x))
+    terms = []
     for h in range(2):
         w = jnp.where(low_sx, west[h], west[2 + h])
-        t = jnp.where(low_sx, east[h], east[2 + h]) - factor * w
+        terms.append(jnp.where(low_sx, east[h], east[2 + h]) - factor * w)
         west_ref[h] = w
         south_ref[h] = jnp.where(low_sy, south[h], south[2 + h])
         north_ref[h] = jnp.where(low_sy, north[h], north[2 + h])
-        msg[:, pl.ds(16 * h, 16), :] = jnp.broadcast_to(t[None], (msg.shape[0], 16, 128))
-    msg[:, 32:40, :] = jnp.broadcast_to(factor[None], (msg.shape[0], 8, 128))
+    fill(msg, terms, [jnp.broadcast_to(factor, (8, 128))] if msg.shape[1] > 32 else [])
 
 
 class Aux:
     def __init__(self, ref):
         self.log_x, self.log_y = ref[0:1, :], ref[1:2, :]
-        self.col, self.outer, self.inner, self.row = (ref[k : k + 1, :] for k in range(2, 6))
+        self.col, self.x, self.y, self.row, self.z, self.core = (ref[k : k + 1, :] for k in range(2, 8))
         self.occupied = ref[8:24, :]
 
 
-def scan(got, place, planes, factor_row):
+def halves(ref, k):
+    return [ref[k, pl.ds(16 * h, 16), :] for h in range(2)]
+
+
+def fill(msg, planes, rows=()):
+    for k, value in enumerate([*planes, *rows]):
+        size = 16 if k < 2 else 8
+        at = 16 * k if k < 2 else 32 + 8 * (k - 2)
+        msg[:, pl.ds(at, size), :] = jnp.broadcast_to(value[None], (msg.shape[0], size, 128))
+
+
+def line_of(planes, ref):
+    sub, lane = iotas(16)
+    value = planes[0] + planes[1]
+    value = value + turn_lanes(value, 64)
+    value = (value + turn_lanes(value, 32)) * 0.125
+    by, part = sub % 4, lane // 32
+    value = jnp.where(((part == 0) & (by == 0)) | ((part == 3) & (by == 3)), value, 0.0)
+    ref[...] = value + turn_rows(value, -3)
+    return ref[pl.ds(0, 4, stride=4), :]
+
+
+def everywhere(x, which):
+    part = lax.broadcasted_iota(jnp.int32, x.shape, x.ndim - 1) // 32
+    x = jnp.where(part == which, x, 0.0)
+    x = x + turn_lanes(x, 32)
+    return x + turn_lanes(x, 64)
+
+
+def four(line):
+    return jnp.concatenate([line] * 4, axis=0)
+
+
+def place_y(sub, lane):
+    return [8 * (sub // 4) + 2 * (2 * ((lane // 32) % 2) + h) + lane // 64 for h in range(2)]
+
+
+def edge_y(aux):
+    return jnp.where(aux.row == 0.0, 0.0, edge_gain(aux.log_y))
+
+
+def group_kernel(aux_ref, got, *rest):
+    if got.shape[1] > 32:
+        west, south, north, msg, start_ref, start_f_ref, factor_ref, line_ref, line2_ref = rest
+        for k in range(got.shape[0]):
+            factor_ref[k : k + 1, :] = got[k, 32:33, :]
+    else:
+        factor_ref, west, south, north, msg, start_ref, start_f_ref, line_ref, line2_ref = rest
+    aux = Aux(aux_ref)
     zero, one = [jnp.zeros((16, 128), F32)] * 2, jnp.ones((1, 128), F32)
     before, before_f, total, total_f = zero, one, zero, one
     for k in range(got.shape[0]):
-        f = got[k, factor_row : factor_row + 1, :]
-        t = [got[k, pl.ds(16 * h, 16), :] for h in range(2)]
-        go = place > k
+        f, t, go = factor_ref[k : k + 1, :], halves(got, k), aux.y > k
         before = [jnp.where(go, f * before[h] + t[h], before[h]) for h in range(2)]
         before_f = jnp.where(go, f * before_f, before_f)
         total = [f * total[h] + t[h] for h in range(2)]
         total_f = f * total_f
-    return before, before_f, total, total_f
-
-
-def group_kernel(aux_ref, got, msg, prefix_ref, prefix_f_ref):
-    before, before_f, total, total_f = scan(got, Aux(aux_ref).inner, 2, 32)
+    start = [before[h] - west[h] for h in range(2)]
+    factor_y = edge_y(aux)
+    term_y = [north[h] - factor_y * south[h] for h in range(2)]
+    line_start, line_total = line_of(start, line_ref), line_of(total, line2_ref)
     for h in range(2):
-        prefix_ref[h] = before[h]
-        msg[:, pl.ds(16 * h, 16), :] = jnp.broadcast_to(total[h][None], (msg.shape[0], 16, 128))
-    msg[:, 32:40, :] = jnp.broadcast_to(total_f[None], (msg.shape[0], 8, 128))
-    prefix_f_ref[...] = jnp.broadcast_to(before_f, (8, 128))
-
-
-def four(line):
-    return jnp.concatenate([line] * 4, axis=0)
-
-
-def place_y(lane, bx):
-    return [8 * bx + 2 * (2 * ((lane // 32) % 2) + h) + lane // 64 for h in range(2)]
-
-
-def turn_kernel(aux_ref, got, prefix_ref, prefix_f_ref, west_ref, south_ref, north_ref, msg, drift_ref, low_ref, line_ref):
+        start_ref[h] = start[h]
+    start_f_ref[...] = jnp.broadcast_to(before_f, (8, 128))
+    for x in range(msg.shape[0] // 2):
+        mine = aux.x == x
+        tail = [
+            jnp.where(mine, line_start, line_total),
+            jnp.where(mine, before_f, total_f),
+            factor_y,
+            aux.log_x,
+            factor_y,
+        ]
+        tail = jnp.concatenate(tail, axis=0)
+        for core in range(2):
+            for h in range(2):
+                msg[2 * x + core, pl.ds(16 * h, 16), :] = jnp.where(aux.core == core, total[h], term_y[h])
+            msg[2 * x + core, 32:40, :] = tail
+
+
+def turn_kernel(aux_ref, got, start_ref, start_f_ref, south, north, msg, drift_ref, low_ref, pair_ref, pair_f_ref, line_ref):
     aux = Aux(aux_ref)
-    sub, lane = iotas(16)
-    start, _, _, _ = scan(got, aux.outer, 2, 32)
-    line = 0.0
-    for h in range(2):
-        drift = prefix_f_ref[0:1, :] * start[h] + prefix_ref[h] - west_ref[h]
-        drift = jnp.where(aux.col == 0.0, 0.0, drift)
-        drift_ref[h] = drift
-        line = line + drift
-    line = line + turn_lanes(line, 64)
-    line = (line + turn_lanes(line, 32)) * 0.125
-    factor = jnp.where(aux.row == 0.0, 0.0, edge_gain(aux.log_y))
-    line_ref[0] = line
-    line_ref[1] = turn_rows(line, -3) - factor * line
-    south_line = four(line_ref[0, pl.ds(0, 4, stride=4), :])
-    term_line = four(line_ref[1, pl.ds(0, 4, stride=4), :])
-    places = place_y(lane, sub // 4)
+    first = aux.core == 0.0
+    begin = [jnp.zeros((16, 128), F32)] * 2
+    begin_line = jnp.zeros((4, 128), F32)
+    term, tail = [0.0, 0.0], 0.0
+    for x in range(got.shape[0] // 2):
+        one, two = halves(got, 2 * x), halves(got, 2 * x + 1)
+        tails = got[2 * x, 32:40, :], got[2 * x + 1, 32:40, :]
+        own_tail, other_tail = jnp.where(first, *tails), jnp.where(first, *tails[::-1])
+        go, mine = aux.x > x, aux.x == x
+        own = [jnp.where(first, one[h], two[h]) for h in range(2)]
+        begin = [jnp.where(go, own_tail[4:5] * begin[h] + own[h], begin[h]) for h in range(2)]
+        begin_line = jnp.where(go, other_tail[4:5] * begin_line + other_tail[0:4], begin_line)
+        term = [jnp.where(mine, jnp.where(first, two[h], one[h]), term[h]) for h in range(2)]
+        tail = jnp.where(mine, other_tail, tail)
+    away = aux.col == 0.0
+    drift = [jnp.where(away, 0.0, start_f_ref[0:1, :] * begin[h] + start_ref[h]) for h in range(2)]
+    line = line_of(drift, line_ref)
+    other_line = jnp.where(away, 0.0, tail[4:5] * begin_line + tail[0:4])
+    factor, other_factor = edge_y(aux), tail[5:6]
+    south_line = everywhere(line, 0)
+    term_line = four(everywhere(line, 3) - factor * south_line)
+    other_line = four(everywhere(other_line, 3) - other_factor * everywhere(other_line, 0))
+    south_line = four(south_line)
+    places = place_y(*iotas(16))
+    pairs = []
     for h in range(2):
         gain = gain_at(places[h], aux.log_x)
-        low_ref[h] = south_ref[h] + gain * south_line
-        term = north_ref[h] - factor * south_ref[h] + gain * term_line
-        msg[:, pl.ds(16 * h, 16), :] = jnp.broadcast_to(term[None], (msg.shape[0], 16, 128))
-    if msg.shape[1] > 32:
-        msg[:, 32:40, :] = jnp.broadcast_to(factor[None], (msg.shape[0], 8, 128))
-
-
-def seams(aux, pred_ref, got, factors, drift_ref, low_ref, put):
+        drift_ref[h] = drift[h]
+        low_ref[h] = south[h] + gain * south_line
+        own = north[h] - factor * south[h] + gain * term_line
+        other = term[h] + gain_at(places[h], tail[6:7]) * other_line
+        pair_ref[h] = jnp.where(first, 0.0, other)
+        pairs.append(jnp.where(first, other_factor * own + other, factor * other + own))
+    pair_f_ref[...] = jnp.broadcast_to(jnp.where(first, 1.0, other_factor), (8, 128))
+    rows = [jnp.broadcast_to(factor * other_factor, (8, 128))] if msg.shape[1] > 32 else []
+    fill(msg, pairs, rows)
+
+
+def seams(aux, pred_ref, got, factors, drift_ref, low_ref, pair_ref, pair_f_ref, put):
     sub, lane = iotas(16)
     by, bx = sub % 4, sub // 4
     sx, sy = lane // 64, (lane // 32) % 2
     before = [jnp.zeros((16, 128), F32)] * 2
     for k in range(got.shape[0]):
-        f, go = factors(k), aux.row > k
-        before = [jnp.where(go, f * before[h] + got[k, pl.ds(16 * h, 16), :], before[h]) for h in range(2)]
+        f, t, go = factors(k), halves(got, k), aux.z > k
+        before = [jnp.where(go, f * before[h] + t[h], before[h]) for h in range(2)]
+    before = [pair_f_ref[0:1, :] * before[h] + pair_ref[h] for h in range(2)]
     drift_y = [jnp.where(aux.row == 0.0, 0.0, before[h] - low_ref[h]) for h in range(2)]
     drift_x = [drift_ref[h] for h in range(2)]
     gain_x = [gain_at(8 * bx + 2 * q + sx, aux.log_x) for q in range(4)]
@@ -232,7 +295,7 @@
                 put(q, value)
 
 
-def first_kernel(inner, latent, occupancy, carry_x, carry_y, w_in, w_down, w_mid, w_up, w_out, *rest):
+def first_kernel(latent, occupancy, carry_x, carry_y, w_in, w_down, w_mid, w_up, w_out, *rest):
     pred_ref, msg, west, south, north, aux_ref, wide_in, wide_out = rest[:8]
     latent_v, occupancy_v, carry_x_v, carry_y_v, w_in_v, w_down_v, w_mid_v, w_up_v, w_out_v = rest[8:17]
     state, first_ref, second_ref, sems = rest[17:]
@@ -250,7 +313,8 @@
     copies = [pltpu.make_async_copy(src, dst, sems.at[k]) for k, (src, dst) in enumerate(pairs)]
     for copy in copies:
         copy.start()
-    col, row = lax.axis_index("gx"), lax.axis_index("gy")
+    x, y, z, core = (lax.axis_index(name) for name in ("x", "y", "z", "core"))
+    columns = lax.axis_size("y")
     for copy in copies[:5]:
         copy.wait()
     wide_in[...] = widen(w_in_v[...], 16, 64).astype(BF16)
@@ -258,7 +322,7 @@
     rates = jnp.concatenate([carry_x_v[...], carry_y_v[...]], axis=0)
     rates = jnp.concatenate([rates] * 8, axis=1)
     aux_ref[0:2, :] = jnp.log(rates)
-    for k, place in enumerate((col, col // inner, col % inner, row)):
+    for k, place in enumerate((x * columns + y, x, y, 2 * z + core, z, core)):
         aux_ref[2 + k : 3 + k, :] = jnp.full((1, 128), place, jnp.int32).astype(F32)
     r, c = (lax.broadcasted_iota(jnp.int32, (16, 16), k) for k in (0, 1))
     occupied = jnp.where(r == c, occupancy_v[...].astype(F32), 0.0)
@@ -272,7 +336,7 @@
     net(state, Aux(aux_ref), weights, first_ref, second_ref, pred_ref, (msg, west, south, north))
 
 
-def next_kernel(aux_ref, pred, got, drift, low, wide_in, w_down, w_mid, w_up, wide_out, *rest):
+def next_kernel(aux_ref, pred, got, drift, low, pair, pair_f, wide_in, w_down, w_mid, w_up, wide_out, *rest):
     outs, (factor_ref, state, first_ref, second_ref) = rest[:5], rest[5:]
     aux = Aux(aux_ref)
     for k in range(got.shape[0]):
@@ -281,15 +345,15 @@
     def put(q, value):
         state[pl.ds(16 * q, 16), :] = value.astype(BF16)
 
-    seams(aux, pred, got, lambda k: got[k, 32:33, :], drift, low, put)
+    seams(aux, pred, got, lambda k: got[k, 32:33, :], drift, low, pair, pair_f, put)
     net(state, aux, (wide_in, w_down, w_mid, w_up, wide_out), first_ref, second_ref, outs[0], outs[1:])
 
 
-def last_kernel(aux_ref, pred, got, drift, low, factor_ref, out, state):
+def last_kernel(aux_ref, pred, got, drift, low, pair, pair_f, factor_ref, out, state):
     def put(q, value):
         state[q] = value
 
-    seams(Aux(aux_ref), pred, got, lambda k: factor_ref[k : k + 1, :], drift, low, put)
+    seams(Aux(aux_ref), pred, got, lambda k: factor_ref[k : k + 1, :], drift, low, pair, pair_f, put)
     out[...] = jnp.swapaxes(state[...], 0, 1).astype(BF16)
 
 
@@ -306,25 +370,24 @@
     )(*args)
 
 
-def per_device(columns, rows, latent, occupancy, carry_x, carry_y, w_in, w_down, w_mid, w_up, w_out):
-    inner = 8 if columns % 8 == 0 else 2
-    outer = columns // inner
-    near = [[inner * a + b for b in range(inner)] for a in range(outer)]
-    far = [[inner * a + b for a in range(outer)] for b in range(inner)]
+def per_device(sizes, latent, occupancy, carry_x, carry_y, w_in, w_down, w_mid, w_up, w_out):
+    xs, ys, zs, _ = sizes
     shape = jax.ShapeDtypeStruct
-    plane = shape((2, 16, 128), F32)
-    net_out = (shape((1024, 128), BF16), shape((inner, 40, 128), F32), plane, plane, plane)
+    plane, row = shape((2, 16, 128), F32), shape((8, 128), F32)
+    lines = pltpu.VMEM((16, 128), F32)
     net_scratch = [
         pltpu.VMEM((1024, 128), BF16),
         pltpu.VMEM((1024, 512), BF16),
         pltpu.VMEM((1024, 128), BF16),
     ]
     for step in range(STEPS):
+        tall = 40 if step == 0 else 32
+        net_out = (shape((1024, 128), BF16), shape((ys, tall, 128), F32), plane, plane, plane)
         if step == 0:
             args = (latent[0, 0], occupancy[0], carry_x[0], carry_y[0], w_in, w_down, w_mid, w_up, w_out.T)
             held = [pltpu.VMEM(a.shape, a.dtype) for a in args]
-            *outs, aux, wide_in, wide_out = call(
-                functools.partial(first_kernel, inner),
+            pred, msg, west, south, north, aux, wide_in, wide_out = call(
+                first_kernel,
                 (*net_out, shape((24, 128), F32), shape((128, 512), BF16), shape((512, 128), BF16)),
                 held + net_scratch + [pltpu.SemaphoreType.DMA((len(args),))],
                 args,
@@ -333,56 +396,68 @@
                 60,
             )
         else:
-            factors, *outs = call(
+            pred, msg, west, south, north, factors_z = call(
                 next_kernel,
-                (*net_out, shape((rows, 128), F32)),
+                (*net_out, shape((zs, 128), F32)),
                 net_scratch,
                 (aux, *seam_ins, wide_in, w_down, w_mid, w_up, wide_out),
                 "seams_net",
-            )[::-1]
-            outs = outs[::-1]
-        pred, msg, west, south, north = outs
-        got = lax.all_to_all(msg, "gx", 0, 0, axis_index_groups=near)
-        msg, prefix, prefix_f = call(
-            group_kernel, (shape((outer, 40, 128), F32), plane, shape((8, 128), F32)), [], (aux, got), "group"
-        )
-        got = lax.all_to_all(msg, "gx", 0, 0, axis_index_groups=far)
-        msg, drift, low = call(
+            )
+        got = lax.all_to_all(msg, "y", 0, 0)
+        group_out = (shape((2 * xs, 40, 128), F32), plane, row)
+        if step == 0:
+            msg, start, start_f, factors_y = call(
+                group_kernel,
+                (*group_out, shape((ys, 128), F32)),
+                [lines, lines],
+                (aux, got, west, south, north),
+                "group",
+            )
+        else:
+            msg, start, start_f = call(
+                group_kernel, group_out, [lines, lines], (aux, got, factors_y, west, south, north), "group"
+            )
+        got = lax.all_to_all(msg, ("x", "core"), 0, 0)
+        msg, *seam_ins = call(
             turn_kernel,
-            (shape((rows, 40 if step == 0 else 32, 128), F32), plane, plane),
-            [pltpu.VMEM((2, 16, 128), F32)],
-            (aux, got, prefix, prefix_f, west, south, north),
+            (shape((zs, tall, 128), F32), plane, plane, plane, row),
+            [lines],
+            (aux, got, start, start_f, south, north),
             "turn",
         )
-        got = lax.all_to_all(msg, "gy", 0, 0)
-        seam_ins = (pred, got, drift, low)
+        got = lax.all_to_all(msg, "z", 0, 0)
+        seam_ins = (pred, got, *seam_ins)
     out = call(
         last_kernel,
         shape((16, 64, 128), BF16),
         [pltpu.VMEM((64, 16, 128), F32)],
-        (aux, *seam_ins, factors),
+        (aux, *seam_ins, factors_z),
         "seams_last",
     )
     return out[None, None]
 
 
 def solution(mesh):
+    columns, rows = mesh.shape["gx"], mesh.shape["gy"]
+    inner = 8 if columns % 8 == 0 else 2
+    sizes = (columns // inner, inner, rows // 2, 2)
+    parts = jax.sharding.Mesh(mesh.devices.reshape(sizes), ("x", "y", "z", "core"))
+    gx, gy = ("x", "y"), ("z", "core")
     in_specs = (
-        P("gx", "gy", None, None, None),
-        P("gx", "gy", None),
-        P("gx", "gy", None),
-        P("gx", "gy", None),
+        P(gx, gy, None, None, None),
+        P(gx, gy, None),
+        P(gx, gy, None),
+        P(gx, gy, None),
         P(),
         P(),
         P(),
         P(),
         P(),
     )
-    out_specs = P("gx", "gy", None, None, None)
     return jax.shard_map(
-        functools.partial(per_device, mesh.shape["gx"], mesh.shape["gy"]),
-        mesh=mesh,
+        functools.partial(per_device, sizes),
+        mesh=parts,
         in_specs=in_specs,
-        out_specs=out_specs,
+        out_specs=P(gx, gy, None, None, None),
         check_vma=False,
     )

time: 97.6 us -> 89.9 us (0.921)
  blocking collectives: 86.9 us -> 78.6 us
    all_to_all x6, blocking collectives: 86.9 us -> 78.6 us  [the longest x2 28.2 us: per_device(): got = lax.all_to_all(msg, 'z', 0, 0)]
where the time goes in v3:
time: 89.9 us; the launch traced here: 89.5 us
  blocking collectives  78.6 us (87%)
  Pallas kernels  10.7 us (12%)
    all_to_all x2, blocking collectives, per_device(): got = lax.all_to_all(msg, 'z', 0, 0)  28.2 us
    all_to_all x2, blocking collectives, per_device(): got = lax.all_to_all(msg, 'y', 0, 0)  26.5 us
    all_to_all x2, blocking collectives, per_device(): got = lax.all_to_all(msg, ('x', 'core'), 0, 0)  23.9 us
    pallas_call x7, Pallas kernels, call(): pl.pallas_call(kernel, out_shape=out_shape, in_specs=[pl.BlockSpec(memory...  10.7 us

profile of v3, /device:TPU:1, one launch (start us, length us, event | category | flops | bytes accessed | tf_op | source)
XLA Modules:
  0.0 89.5 jit_solution(7608030898063190698)
XLA Ops:
  0.0 5.3 %net_first.1 = (bf16[1024,128]{1,0:T(8,128)(2,1)}, f32[8,40,128]{2,1,0:T(8,128)}, f32[2,16,128]{2,1,0:T(8,128)}, f32[2,16,128]{2,1,0:T(8,128)}, f32[2,16,128]{2,...) custom-call(bf16[16,64,128]{2,1,0:T(8,128)(2,1)} %bitcast.6, ...), custom_call_target="tpu_custom_call" | custom-call | tf_op jit(solution)/shard_map/net_first/pallas_call | solution.py:362
  5.3 0.0 copy-start.3
  5.3 0.0 copy-start.7
  5.3 0.0 copy-start.8
  5.3 0.0 copy-start.9
  5.4 16.2 %all_to_all.30.got = f32[8,40,128]{2,1,0:T(8,128)S(1)} all-to-all(f32[8,40,128]{2,1,0:T(8,128)} %get-tuple-element.38), channel_id=1, replica_groups=mesh['x'=4,'y'=8,'z'=8,'core'=2] {'y'}, dimensions={0} | all-to-all | bytes 327680 | tf_op jit(solution)/shard_map/all_to_all | solution.py:406
  21.5 0.0 copy-done.3
  21.5 0.0 copy-done.7
  21.5 0.0 copy-done.8
  21.5 0.0 copy-done.9
  21.6 0.0 copy-start.6
  21.6 0.2 group.2
  21.8 0.0 copy-start.4
  21.8 0.0 copy-start.5
  21.8 12.1 %all_to_all.31.got = f32[8,40,128]{2,1,0:T(8,128)S(1)} all-to-all(f32[8,40,128]{2,1,0:T(8,128)S(1)} %get-tuple-element.42), channel_id=1, replica_groups=mesh['x'=4,'y'=8,'z'=8,'core'=2] {'x','core'}, dimensions={0} | all-to-all | bytes 327680 | tf_op jit(solution)/shard_map/all_to_all | solution.py:420
  33.9 0.3 turn.2
  34.3 0.0 copy-start.1
  34.3 0.0 copy-start.2
  34.3 18.0 %all_to_all.32.got = f32[8,40,128]{2,1,0:T(8,128)S(1)} all-to-all(f32[8,40,128]{2,1,0:T(8,128)S(1)} %get-tuple-element.45), channel_id=1, replica_groups=mesh['x'=4,'y'=8,'z'=8,'core'=2] {'z'}, dimensions={0} | all-to-all | bytes 327680 | tf_op jit(solution)/shard_map/all_to_all | solution.py:428
  52.3 0.0 copy-done.6
  52.3 0.0 copy-done.4
  52.3 0.0 copy-done.5
  52.3 0.0 copy-done
  52.4 0.0 copy-done.1
  52.4 0.0 copy-done.2
  52.4 3.3 %seams_net.1 = (bf16[1024,128]{1,0:T(8,128)(2,1)S(1)}, f32[8,32,128]{2,1,0:T(8,128)S(1)}, f32[2,16,128]{2,1,0:T(8,128)S(1)}, f32[2,16,128]{2,1,0:T(8,128)S(1)}, ...) custom-call(f32[24,128]{1,0:T(8,128)S(1)} %copy-done.3, bf16[1024,128]{1,0:T(8,128)(2,1)S(1)} %copy-done.4, ...), custom_call_target="tpu_custom_call" | custom-call | tf_op jit(solution)/shard_map/seams_net/pallas_call | solution.py:362
  55.7 10.3 %all_to_all.33.got = f32[8,32,128]{2,1,0:T(8,128)S(1)} all-to-all(f32[8,32,128]{2,1,0:T(8,128)S(1)} %get-tuple-element.53), channel_id=1, replica_groups=mesh['x'=4,'y'=8,'z'=8,'core'=2] {'y'}, dimensions={0} | all-to-all | bytes 262144 | tf_op jit(solution)/shard_map/all_to_all | solution.py:406
  66.0 0.2 group.3
  66.2 11.8 %all_to_all.34.got = f32[8,40,128]{2,1,0:T(8,128)S(1)} all-to-all(f32[8,40,128]{2,1,0:T(8,128)S(1)} %get-tuple-element.58), channel_id=1, replica_groups=mesh['x'=4,'y'=8,'z'=8,'core'=2] {'x','core'}, dimensions={0} | all-to-all | bytes 327680 | tf_op jit(solution)/shard_map/all_to_all | solution.py:420
  77.9 0.3 turn.3
  78.3 10.1 %all_to_all.35.got = f32[8,32,128]{2,1,0:T(8,128)S(1)} all-to-all(f32[8,32,128]{2,1,0:T(8,128)S(1)} %get-tuple-element.61), channel_id=1, replica_groups=mesh['x'=4,'y'=8,'z'=8,'core'=2] {'z'}, dimensions={0} | all-to-all | bytes 262144 | tf_op jit(solution)/shard_map/all_to_all | solution.py:428
  88.4 1.0 %seams_last.1 = bf16[16,64,128]{2,1,0:T(8,128)(2,1)} custom-call(f32[24,128]{1,0:T(8,128)S(1)} %copy-done.3, bf16[1024,128]{1,0:T(8,128)(2,1)S(1)} %get-tuple-element.52.pred, f32[8,32,128]{2,1,0:T(8,128)S(1)} %all_to_all.35.got, f32[2,16,128]{2,1,0:T(8,128)S(1)} %get-tuple-element.62.drift, f32[2,16,128]{2,1,0:T(8,128)S(1)} %get-tuple-element.63.low, ...), custom_call_target="tpu_custom_call" | custom-call | tf_op jit(solution)/shard_map/seams_last/pallas_call | solution.py:362
  (1 shorter events, 0.0 us)
Async XLA Ops:
  5.3 16.2 %copy-start.3 = (f32[24,128]{1,0:T(8,128)S(1)}, f32[24,128]{1,0:T(8,128)}, u32[]{:S(2)}) copy-start(f32[24,128]{1,0:T(8,128)} %get-tuple-element.36.aux_ref) | copy-start | bytes 36868
  5.3 16.2 %copy-start.7 = (f32[2,16,128]{2,1,0:T(8,128)S(1)}, f32[2,16,128]{2,1,0:T(8,128)}, u32[]{:S(2)}) copy-start(f32[2,16,128]{2,1,0:T(8,128)} %get-tuple-element.40.rest_1_.south) | copy-start | bytes 49156
  5.3 16.2 %copy-start.8 = (f32[2,16,128]{2,1,0:T(8,128)S(1)}, f32[2,16,128]{2,1,0:T(8,128)}, u32[]{:S(2)}) copy-start(f32[2,16,128]{2,1,0:T(8,128)} %get-tuple-element.41.rest_2_.north) | copy-start | bytes 49156
  5.3 16.2 %copy-start.9 = (f32[2,16,128]{2,1,0:T(8,128)S(1)}, f32[2,16,128]{2,1,0:T(8,128)}, u32[]{:S(2)}) copy-start(f32[2,16,128]{2,1,0:T(8,128)} %get-tuple-element.39.rest_0_) | copy-start | bytes 49156
  21.6 30.8 %copy-start.6 = (bf16[512,128]{1,0:T(8,128)(2,1)S(1)}, bf16[512,128]{1,0:T(8,128)(2,1)}, u32[]{:S(2)}) copy-start(bf16[512,128]{1,0:T(8,128)(2,1)} %get-tuple-element.51.wide_out) | copy-start | bytes 393220
  21.8 30.6 %copy-start.4 = (bf16[1024,128]{1,0:T(8,128)(2,1)S(1)}, bf16[1024,128]{1,0:T(8,128)(2,1)}, u32[]{:S(2)}) copy-start(bf16[1024,128]{1,0:T(8,128)(2,1)} %get-tuple-element.37.pred) | copy-start | bytes 786436
  21.8 30.6 %copy-start.5 = (bf16[128,512]{1,0:T(8,128)(2,1)S(1)}, bf16[128,512]{1,0:T(8,128)(2,1)}, u32[]{:S(2)}) copy-start(bf16[128,512]{1,0:T(8,128)(2,1)} %get-tuple-element.50.wide_in) | copy-start | bytes 393220
  33.9 18.4 %copy-start = (bf16[7,128,128]{2,1,0:T(8,128)(2,1)S(1)}, bf16[7,128,128]{2,1,0:T(8,128)(2,1)}, u32[]{:S(2)}) copy-start(bf16[7,128,128]{2,1,0:T(8,128)(2,1)} %w_mid.3) | copy-start | bytes 688132
  34.3 18.1 %copy-start.1 = (bf16[512,128]{1,0:T(8,128)(2,1)S(1)}, bf16[512,128]{1,0:T(8,128)(2,1)}, u32[]{:S(2)}) copy-start(bf16[512,128]{1,0:T(8,128)(2,1)} %w_down.3) | copy-start | bytes 393220
  34.3 18.1 %copy-start.2 = (bf16[128,512]{1,0:T(8,128)(2,1)S(1)}, bf16[128,512]{1,0:T(8,128)(2,1)}, u32[]{:S(2)}) copy-start(bf16[128,512]{1,0:T(8,128)(2,1)} %w_up.3) | copy-start | bytes 393220

commit v4 on v3

--- a/solution.py
+++ b/solution.py
@@ -56,62 +56,64 @@
     return jnp.where(r == c, both, 0.0)
 
 
-def net(state, aux, weights, first_ref, second_ref, pred_ref, outs):
+def net(state, ready, weights, first_ref, second_ref, pred_ref, outs):
     wide_in, w_down, w_mid, w_up, wide_out = weights
     msg, west_ref, south_ref, north_ref = outs
-    log_x, occupied, col = aux.log_x, aux.occupied, aux.col
-    for qx in range(4):
-        rows = pl.ds(256 * qx, 256)
+    for qx in range(2):
+        rows = pl.ds(512 * qx, 512)
         first = silu(jnp.dot(state[rows, :], wide_in[...], preferred_element_type=F32)).astype(BF16)
         first_ref[rows, :] = first
         pre = jnp.dot(first, w_down[...], preferred_element_type=F32)
         pre = pre * lax.rsqrt(jnp.mean(pre * pre, axis=-1, keepdims=True) + 1e-06)
-        second_ref[rows, :] = silu(pre).astype(BF16)
+        second_ref[pl.ds(256 + 512 * qx, 512), :] = silu(pre).astype(BF16)
 
     sub, lane = iotas(16)
     by, bx = sub % 4, sub // 4
     total_x = [[None] * 4 for _ in range(4)]
     south, north = [0.0] * 4, [0.0] * 4
-    for qx in range(4):
-        base = 256 * qx
-        rows = pl.ds(base, 256)
-        second = second_ref[rows, :]
-        parts = [(0, second)]
-        if qx > 0:
-            parts.append((1, second_ref[pl.ds(base - 256, 256), :]))
-        if qx < 3:
-            parts.append((2, second_ref[pl.ds(base + 256, 256), :]))
+    aux = ready()
+    log_x, occupied, col = aux.log_x, aux.occupied, aux.col
+    second_ref[pl.ds(0, 256), :] = jnp.zeros((256, 128), BF16)
+    second_ref[pl.ds(1280, 256), :] = jnp.zeros((256, 128), BF16)
+    mids = jnp.concatenate([w_mid[k] for k in range(7)], axis=0)
+    for group in range(2):
+        base = 512 * group
+        rows = pl.ds(base, 512)
+        second = second_ref[pl.ds(base + 256, 512), :]
+        parts = [second, second_ref[pl.ds(base, 512), :], second_ref[pl.ds(base + 512, 512), :]]
         gap = jnp.zeros((64, 128), BF16)
-        parts.append((3, jnp.concatenate([gap, second[:192]], axis=0)))
-        parts.append((4, jnp.concatenate([second[64:], gap], axis=0)))
-        gap = jnp.zeros((16, 128), BF16)
-        below, above = [], []
-        for qy in range(4):
-            own = second[64 * qy : 64 * qy + 64]
-            below += [gap, own[:48]]
-            above += [own[16:], gap]
-        parts.append((5, jnp.concatenate(below, axis=0)))
-        parts.append((6, jnp.concatenate(above, axis=0)))
-        stacked = jnp.concatenate([p for _, p in parts], axis=1)
-        mids = jnp.concatenate([w_mid[k] for k, _ in parts], axis=0)
+        gap16 = jnp.zeros((16, 128), BF16)
+        left, right, below, above = [], [], [], []
+        for plane in range(2):
+            own = second[256 * plane : 256 * plane + 256]
+            left += [gap, own[:192]]
+            right += [own[64:], gap]
+            for qy in range(4):
+                o = own[64 * qy : 64 * qy + 64]
+                below += [gap16, o[:48]]
+                above += [o[16:], gap16]
+        parts += [jnp.concatenate(p, axis=0) for p in (left, right, below, above)]
+        stacked = jnp.concatenate(parts, axis=1)
         mixed = jnp.dot(stacked, mids, preferred_element_type=F32)
         middle = (second.astype(F32) + silu(mixed)).astype(BF16)
         upper = jnp.dot(middle, w_up[...], preferred_element_type=F32) + first_ref[rows, :].astype(F32)
         upper = silu(upper).astype(BF16)
         update = jnp.dot(upper, wide_out[...], preferred_element_type=F32)
-        update = update.reshape(16, 16, 128) * occupied[None]
-        pred = (state[rows, :].astype(F32).reshape(16, 16, 128) + update).astype(BF16)
-        pred_ref[rows, :] = pred.reshape(256, 128)
-        pred = pred.astype(F32)
-        for qy in range(4):
+        update = update.reshape(32, 16, 128) * occupied[None]
+        preds = (state[rows, :].astype(F32).reshape(32, 16, 128) + update).astype(BF16)
+        pred_ref[rows, :] = preds.reshape(512, 128)
+        for plane in range(2):
+            qx = 2 * group + plane
+            pred = preds[16 * plane : 16 * plane + 16].astype(F32)
+            for qy in range(4):
+                for qz in range(4):
+                    value = pred[4 * qy + qz]
+                    total_x[qy][qz] = value if qx == 0 else total_x[qy][qz] + value
             for qz in range(4):
-                value = pred[4 * qy + qz]
-                total_x[qy][qz] = value if qx == 0 else total_x[qy][qz] + value
-        for qz in range(4):
-            s = pred[qz] + pred[4 + qz] + pred[8 + qz] + pred[12 + qz]
-            s = (s + swap_sy(s, lane)) * 0.125
-            south[qx] = south[qx] + jnp.where(by == qz, turn_rows(s, qz), 0.0)
-            north[qx] = north[qx] + jnp.where(by == qz, turn_rows(s, qz - 3), 0.0)
+                s = pred[qz] + pred[4 + qz] + pred[8 + qz] + pred[12 + qz]
+                s = (s + swap_sy(s, lane)) * 0.125
+                south[qx] = south[qx] + jnp.where(by == qz, turn_rows(s, qz), 0.0)
+                north[qx] = north[qx] + jnp.where(by == qz, turn_rows(s, qz - 3), 0.0)
 
     west, east = [0.0] * 4, [0.0] * 4
     for qy in range(4):
@@ -301,39 +303,43 @@
     state, first_ref, second_ref, sems = rest[17:]
     pairs = [
         (w_in, w_in_v),
+        (latent, latent_v),
+        (w_down, w_down_v),
+        (w_mid, w_mid_v),
+        (w_up, w_up_v),
         (w_out, w_out_v),
         (occupancy, occupancy_v),
         (carry_x, carry_x_v),
         (carry_y, carry_y_v),
-        (latent, latent_v),
-        (w_down, w_down_v),
-        (w_mid, w_mid_v),
-        (w_up, w_up_v),
     ]
     copies = [pltpu.make_async_copy(src, dst, sems.at[k]) for k, (src, dst) in enumerate(pairs)]
     for copy in copies:
         copy.start()
     x, y, z, core = (lax.axis_index(name) for name in ("x", "y", "z", "core"))
     columns = lax.axis_size("y")
-    for copy in copies[:5]:
-        copy.wait()
+    copies[0].wait()
     wide_in[...] = widen(w_in_v[...], 16, 64).astype(BF16)
-    wide_out[...] = widen(w_out_v[...], 16, 64).T.astype(BF16)
-    rates = jnp.concatenate([carry_x_v[...], carry_y_v[...]], axis=0)
-    rates = jnp.concatenate([rates] * 8, axis=1)
-    aux_ref[0:2, :] = jnp.log(rates)
-    for k, place in enumerate((x * columns + y, x, y, 2 * z + core, z, core)):
-        aux_ref[2 + k : 3 + k, :] = jnp.full((1, 128), place, jnp.int32).astype(F32)
-    r, c = (lax.broadcasted_iota(jnp.int32, (16, 16), k) for k in (0, 1))
-    occupied = jnp.where(r == c, occupancy_v[...].astype(F32), 0.0)
-    aux_ref[8:24, :] = jnp.broadcast_to(jnp.sum(occupied, axis=1, keepdims=True), (16, 128))
-    copies[5].wait()
+    copies[1].wait()
     turned = jnp.swapaxes(latent_v[...].astype(F32), 0, 1)
     state[...] = turned.reshape(1024, 128).astype(BF16)
-    for copy in copies[6:]:
-        copy.wait()
+    copies[2].wait()
+
+    def ready():
+        for copy in copies[3:]:
+            copy.wait()
+        wide_out[...] = widen(w_out_v[...], 16, 64).T.astype(BF16)
+        rates = jnp.concatenate([carry_x_v[...], carry_y_v[...]], axis=0)
+        rates = jnp.concatenate([rates] * 8, axis=1)
+        aux_ref[0:2, :] = jnp.log(rates)
+        for k, place in enumerate((x * columns + y, x, y, 2 * z + core, z, core)):
+            aux_ref[2 + k : 3 + k, :] = jnp.full((1, 128), place, jnp.int32).astype(F32)
+        r, c = (lax.broadcasted_iota(jnp.int32, (16, 16), k) for k in (0, 1))
+        occupied = jnp.where(r == c, occupancy_v[...].astype(F32), 0.0)
+        aux_ref[8:24, :] = jnp.broadcast_to(jnp.sum(occupied, axis=1, keepdims=True), (16, 128))
+        return Aux(aux_ref)
+
     weights = (wide_in, w_down_v, w_mid_v, w_up_v, wide_out)
-    net(state, Aux(aux_ref), weights, first_ref, second_ref, pred_ref, (msg, west, south, north))
+    net(state, ready, weights, first_ref, second_ref, pred_ref, (msg, west, south, north))
 
 
 def next_kernel(aux_ref, pred, got, drift, low, pair, pair_f, wide_in, w_down, w_mid, w_up, wide_out, *rest):
@@ -346,19 +352,27 @@
         state[pl.ds(16 * q, 16), :] = value.astype(BF16)
 
     seams(aux, pred, got, lambda k: got[k, 32:33, :], drift, low, pair, pair_f, put)
-    net(state, aux, (wide_in, w_down, w_mid, w_up, wide_out), first_ref, second_ref, outs[0], outs[1:])
-
-
-def last_kernel(aux_ref, pred, got, drift, low, pair, pair_f, factor_ref, out, state):
+    net(state, lambda: aux, (wide_in, w_down, w_mid, w_up, wide_out), first_ref, second_ref, outs[0], outs[1:])
+
+
+def last_kernel(aux_ref, pred, got, drift, low, pair, pair_f, factor_ref, out, state, turned, sems):
+    copies = []
+
     def put(q, value):
         state[q] = value
+        if q % 16 == 15:
+            rows = pl.ds(q - 15, 16)
+            turned[:, rows, :] = jnp.swapaxes(state[rows], 0, 1).astype(BF16)
+            copies.append(pltpu.make_async_copy(turned.at[:, rows, :], out.at[:, rows, :], sems.at[q // 16]))
+            copies[-1].start()
 
     seams(Aux(aux_ref), pred, got, lambda k: factor_ref[k : k + 1, :], drift, low, pair, pair_f, put)
-    out[...] = jnp.swapaxes(state[...], 0, 1).astype(BF16)
-
-
-def call(kernel, out_shape, scratch, args, name, space=pltpu.VMEM, limit=24):
-    vmem = pl.BlockSpec(memory_space=pltpu.VMEM)
+    for copy in copies:
+        copy.wait()
+
+
+def call(kernel, out_shape, scratch, args, name, space=pltpu.VMEM, limit=24, out_space=pltpu.VMEM):
+    vmem = pl.BlockSpec(memory_space=out_space)
     return pl.pallas_call(
         kernel,
         out_shape=out_shape,
@@ -378,7 +392,7 @@
     net_scratch = [
         pltpu.VMEM((1024, 128), BF16),
         pltpu.VMEM((1024, 512), BF16),
-        pltpu.VMEM((1024, 128), BF16),
+        pltpu.VMEM((1536, 128), BF16),
     ]
     for step in range(STEPS):
         tall = 40 if step == 0 else 32
@@ -430,9 +444,10 @@
     out = call(
         last_kernel,
         shape((16, 64, 128), BF16),
-        [pltpu.VMEM((64, 16, 128), F32)],
+        [pltpu.VMEM((64, 16, 128), F32), pltpu.VMEM((16, 64, 128), BF16), pltpu.SemaphoreType.DMA((4,))],
         (aux, *seam_ins, factors_z),
         "seams_last",
+        out_space=pl.ANY,
     )
     return out[None, None]
 

time: 89.9 us -> 88.8 us (0.988)
  Pallas kernels: 10.7 us -> 9.55 us
    pallas_call x7, Pallas kernels: 10.7 us -> 9.55 us  [call(): pl.pallas_call(kernel, out_shape=out_shape, in_specs=[pl.BlockSpec(memory...]
where the time goes in v4:
time: 88.8 us; the launch traced here: 88.3 us
  blocking collectives  78.6 us (89%)
  Pallas kernels  9.55 us (11%)
    all_to_all x2, blocking collectives, per_device(): got = lax.all_to_all(msg, 'z', 0, 0)  28.2 us
    all_to_all x2, blocking collectives, per_device(): got = lax.all_to_all(msg, 'y', 0, 0)  26.5 us
    all_to_all x2, blocking collectives, per_device(): got = lax.all_to_all(msg, ('x', 'core'), 0, 0)  23.9 us
    pallas_call x7, Pallas kernels, call(): pl.pallas_call(kernel, out_shape=out_shape, in_specs=[pl.BlockSpec(memory...  9.55 us

profile of v4, /device:TPU:1, one launch (start us, length us, event | category | flops | bytes accessed | tf_op | source)
XLA Modules:
  0.0 88.3 jit_solution(7123291736290063982)
XLA Ops:
  0.0 4.8 %net_first.1 = (bf16[1024,128]{1,0:T(8,128)(2,1)}, f32[8,40,128]{2,1,0:T(8,128)}, f32[2,16,128]{2,1,0:T(8,128)}, f32[2,16,128]{2,1,0:T(8,128)}, f32[2,16,128]{2,...) custom-call(bf16[16,64,128]{2,1,0:T(8,128)(2,1)} %bitcast.6, ...), custom_call_target="tpu_custom_call" | custom-call | tf_op jit(solution)/shard_map/net_first/pallas_call | solution.py:376
  4.8 0.0 copy-start.3
  4.9 0.0 copy-start.7
  4.9 0.0 copy-start.8
  4.9 0.0 copy-start.9
  4.9 16.2 %all_to_all.30.got = f32[8,40,128]{2,1,0:T(8,128)S(1)} all-to-all(f32[8,40,128]{2,1,0:T(8,128)} %get-tuple-element.38), channel_id=1, replica_groups=mesh['x'=4,'y'=8,'z'=8,'core'=2] {'y'}, dimensions={0} | all-to-all | bytes 327680 | tf_op jit(solution)/shard_map/all_to_all | solution.py:420
  21.1 0.0 copy-done.3
  21.1 0.0 copy-done.7
  21.1 0.0 copy-done.8
  21.1 0.0 copy-done.9
  21.1 0.0 copy-start.6
  21.1 0.2 group.2
  21.3 0.0 copy-start.4
  21.3 0.0 copy-start.5
  21.3 12.1 %all_to_all.31.got = f32[8,40,128]{2,1,0:T(8,128)S(1)} all-to-all(f32[8,40,128]{2,1,0:T(8,128)S(1)} %get-tuple-element.42), channel_id=1, replica_groups=mesh['x'=4,'y'=8,'z'=8,'core'=2] {'x','core'}, dimensions={0} | all-to-all | bytes 327680 | tf_op jit(solution)/shard_map/all_to_all | solution.py:434
  33.5 0.3 turn.2
  33.8 0.0 copy-start.1
  33.8 0.0 copy-start.2
  33.8 18.0 %all_to_all.32.got = f32[8,40,128]{2,1,0:T(8,128)S(1)} all-to-all(f32[8,40,128]{2,1,0:T(8,128)S(1)} %get-tuple-element.45), channel_id=1, replica_groups=mesh['x'=4,'y'=8,'z'=8,'core'=2] {'z'}, dimensions={0} | all-to-all | bytes 327680 | tf_op jit(solution)/shard_map/all_to_all | solution.py:442
  51.9 0.0 copy-done.6
  51.9 0.0 copy-done.4
  51.9 0.0 copy-done.5
  51.9 0.0 copy-done
  51.9 0.0 copy-done.1
  51.9 0.0 copy-done.2
  51.9 2.7 %seams_net.1 = (bf16[1024,128]{1,0:T(8,128)(2,1)S(1)}, f32[8,32,128]{2,1,0:T(8,128)S(1)}, f32[2,16,128]{2,1,0:T(8,128)S(1)}, f32[2,16,128]{2,1,0:T(8,128)S(1)}, ...) custom-call(f32[24,128]{1,0:T(8,128)S(1)} %copy-done.3, bf16[1024,128]{1,0:T(8,128)(2,1)S(1)} %copy-done.4, ...), custom_call_target="tpu_custom_call" | custom-call | tf_op jit(solution)/shard_map/seams_net/pallas_call | solution.py:376
  54.6 10.3 %all_to_all.33.got = f32[8,32,128]{2,1,0:T(8,128)S(1)} all-to-all(f32[8,32,128]{2,1,0:T(8,128)S(1)} %get-tuple-element.53), channel_id=1, replica_groups=mesh['x'=4,'y'=8,'z'=8,'core'=2] {'y'}, dimensions={0} | all-to-all | bytes 262144 | tf_op jit(solution)/shard_map/all_to_all | solution.py:420
  64.9 0.2 group.3
  65.1 11.8 %all_to_all.34.got = f32[8,40,128]{2,1,0:T(8,128)S(1)} all-to-all(f32[8,40,128]{2,1,0:T(8,128)S(1)} %get-tuple-element.58), channel_id=1, replica_groups=mesh['x'=4,'y'=8,'z'=8,'core'=2] {'x','core'}, dimensions={0} | all-to-all | bytes 327680 | tf_op jit(solution)/shard_map/all_to_all | solution.py:434
  76.9 0.3 turn.3
  77.2 10.1 %all_to_all.35.got = f32[8,32,128]{2,1,0:T(8,128)S(1)} all-to-all(f32[8,32,128]{2,1,0:T(8,128)S(1)} %get-tuple-element.61), channel_id=1, replica_groups=mesh['x'=4,'y'=8,'z'=8,'core'=2] {'z'}, dimensions={0} | all-to-all | bytes 262144 | tf_op jit(solution)/shard_map/all_to_all | solution.py:442
  87.4 1.0 %seams_last.1 = bf16[16,64,128]{2,1,0:T(8,128)(2,1)} custom-call(f32[24,128]{1,0:T(8,128)S(1)} %copy-done.3, bf16[1024,128]{1,0:T(8,128)(2,1)S(1)} %get-tuple-element.52.pred, f32[8,32,128]{2,1,0:T(8,128)S(1)} %all_to_all.35.got, f32[2,16,128]{2,1,0:T(8,128)S(1)} %get-tuple-element.62.drift, f32[2,16,128]{2,1,0:T(8,128)S(1)} %get-tuple-element.63.low, ...), custom_call_target="tpu_custom_call" | custom-call | tf_op jit(solution)/shard_map/seams_last/pallas_call | solution.py:376
  (1 shorter events, 0.0 us)
Async XLA Ops:
  4.8 16.2 %copy-start.3 = (f32[24,128]{1,0:T(8,128)S(1)}, f32[24,128]{1,0:T(8,128)}, u32[]{:S(2)}) copy-start(f32[24,128]{1,0:T(8,128)} %get-tuple-element.36.aux_ref) | copy-start | bytes 36868
  4.9 16.2 %copy-start.7 = (f32[2,16,128]{2,1,0:T(8,128)S(1)}, f32[2,16,128]{2,1,0:T(8,128)}, u32[]{:S(2)}) copy-start(f32[2,16,128]{2,1,0:T(8,128)} %get-tuple-element.40.rest_1_.south) | copy-start | bytes 49156
  4.9 16.2 %copy-start.8 = (f32[2,16,128]{2,1,0:T(8,128)S(1)}, f32[2,16,128]{2,1,0:T(8,128)}, u32[]{:S(2)}) copy-start(f32[2,16,128]{2,1,0:T(8,128)} %get-tuple-element.41.rest_2_.north) | copy-start | bytes 49156
  4.9 16.2 %copy-start.9 = (f32[2,16,128]{2,1,0:T(8,128)S(1)}, f32[2,16,128]{2,1,0:T(8,128)}, u32[]{:S(2)}) copy-start(f32[2,16,128]{2,1,0:T(8,128)} %get-tuple-element.39.rest_0_) | copy-start | bytes 49156
  21.1 30.8 %copy-start.6 = (bf16[512,128]{1,0:T(8,128)(2,1)S(1)}, bf16[512,128]{1,0:T(8,128)(2,1)}, u32[]{:S(2)}) copy-start(bf16[512,128]{1,0:T(8,128)(2,1)} %get-tuple-element.51.wide_out) | copy-start | bytes 393220
  21.3 30.6 %copy-start.4 = (bf16[1024,128]{1,0:T(8,128)(2,1)S(1)}, bf16[1024,128]{1,0:T(8,128)(2,1)}, u32[]{:S(2)}) copy-start(bf16[1024,128]{1,0:T(8,128)(2,1)} %get-tuple-element.37.pred) | copy-start | bytes 786436
  21.3 30.6 %copy-start.5 = (bf16[128,512]{1,0:T(8,128)(2,1)S(1)}, bf16[128,512]{1,0:T(8,128)(2,1)}, u32[]{:S(2)}) copy-start(bf16[128,512]{1,0:T(8,128)(2,1)} %get-tuple-element.50.wide_in) | copy-start | bytes 393220
  33.5 18.4 %copy-start = (bf16[7,128,128]{2,1,0:T(8,128)(2,1)S(1)}, bf16[7,128,128]{2,1,0:T(8,128)(2,1)}, u32[]{:S(2)}) copy-start(bf16[7,128,128]{2,1,0:T(8,128)(2,1)} %w_mid.3) | copy-start | bytes 688132
  33.8 18.1 %copy-start.1 = (bf16[512,128]{1,0:T(8,128)(2,1)S(1)}, bf16[512,128]{1,0:T(8,128)(2,1)}, u32[]{:S(2)}) copy-start(bf16[512,128]{1,0:T(8,128)(2,1)} %w_down.3) | copy-start | bytes 393220
  33.8 18.1 %copy-start.2 = (bf16[128,512]{1,0:T(8,128)(2,1)S(1)}, bf16[128,512]{1,0:T(8,128)(2,1)}, u32[]{:S(2)}) copy-start(bf16[128,512]{1,0:T(8,128)(2,1)} %w_up.3) | copy-start | bytes 393220

commit v5 on v4

--- a/solution.py
+++ b/solution.py
@@ -44,15 +44,11 @@
     return jnp.exp(place.astype(F32) / 32.0 * logs + (0.5 / 32.0) * logs)
 
 
-def widen(narrow, rows, cols):
-    r = lax.broadcasted_iota(jnp.int32, (8 * rows, rows), 0) % rows
-    k = lax.broadcasted_iota(jnp.int32, (8 * rows, rows), 1)
-    tall = jnp.dot((r == k).astype(BF16), narrow, preferred_element_type=F32).astype(BF16)
-    k = lax.broadcasted_iota(jnp.int32, (cols, 8 * cols), 0)
-    c = lax.broadcasted_iota(jnp.int32, (cols, 8 * cols), 1) % cols
-    both = jnp.dot(tall, (k == c).astype(BF16), preferred_element_type=F32)
-    r = lax.broadcasted_iota(jnp.int32, (8 * rows, 8 * cols), 0) // rows
-    c = lax.broadcasted_iota(jnp.int32, (8 * rows, 8 * cols), 1) // cols
+def widen(narrow):
+    row = jnp.concatenate([narrow.astype(F32)] * 8, axis=1)
+    both = jnp.concatenate([row] * 8, axis=0)
+    r = lax.broadcasted_iota(jnp.int32, both.shape, 0) // 16
+    c = lax.broadcasted_iota(jnp.int32, both.shape, 1) // 64
     return jnp.where(r == c, both, 0.0)
 
 
@@ -184,11 +180,11 @@
 
 def group_kernel(aux_ref, got, *rest):
     if got.shape[1] > 32:
-        west, south, north, msg, start_ref, start_f_ref, factor_ref, line_ref, line2_ref = rest
+        west, term, msg, start_ref, start_f_ref, factor_ref, line_ref, line2_ref = rest
         for k in range(got.shape[0]):
             factor_ref[k : k + 1, :] = got[k, 32:33, :]
     else:
-        factor_ref, west, south, north, msg, start_ref, start_f_ref, line_ref, line2_ref = rest
+        factor_ref, west, term, msg, start_ref, start_f_ref, line_ref, line2_ref = rest
     aux = Aux(aux_ref)
     zero, one = [jnp.zeros((16, 128), F32)] * 2, jnp.ones((1, 128), F32)
     before, before_f, total, total_f = zero, one, zero, one
@@ -200,7 +196,7 @@
         total_f = f * total_f
     start = [before[h] - west[h] for h in range(2)]
     factor_y = edge_y(aux)
-    term_y = [north[h] - factor_y * south[h] for h in range(2)]
+    term_y = [term[h] for h in range(2)]
     line_start, line_total = line_of(start, line_ref), line_of(total, line2_ref)
     for h in range(2):
         start_ref[h] = start[h]
@@ -219,6 +215,12 @@
             for h in range(2):
                 msg[2 * x + core, pl.ds(16 * h, 16), :] = jnp.where(aux.core == core, total[h], term_y[h])
             msg[2 * x + core, 32:40, :] = tail
+
+
+def term_kernel(aux_ref, south, north, term_ref):
+    factor = edge_y(Aux(aux_ref))
+    for h in range(2):
+        term_ref[h] = north[h] - factor * south[h]
 
 
 def turn_kernel(aux_ref, got, start_ref, start_f_ref, south, north, msg, drift_ref, low_ref, pair_ref, pair_f_ref, line_ref):
@@ -302,8 +304,8 @@
     latent_v, occupancy_v, carry_x_v, carry_y_v, w_in_v, w_down_v, w_mid_v, w_up_v, w_out_v = rest[8:17]
     state, first_ref, second_ref, sems = rest[17:]
     pairs = [
+        (latent, latent_v),
         (w_in, w_in_v),
-        (latent, latent_v),
         (w_down, w_down_v),
         (w_mid, w_mid_v),
         (w_up, w_up_v),
@@ -318,16 +320,15 @@
     x, y, z, core = (lax.axis_index(name) for name in ("x", "y", "z", "core"))
     columns = lax.axis_size("y")
     copies[0].wait()
-    wide_in[...] = widen(w_in_v[...], 16, 64).astype(BF16)
     copies[1].wait()
+    wide_in[...] = widen(w_in_v[...]).astype(BF16)
     turned = jnp.swapaxes(latent_v[...].astype(F32), 0, 1)
     state[...] = turned.reshape(1024, 128).astype(BF16)
-    copies[2].wait()
+    for copy in copies[2:]:
+        copy.wait()
 
     def ready():
-        for copy in copies[3:]:
-            copy.wait()
-        wide_out[...] = widen(w_out_v[...], 16, 64).T.astype(BF16)
+        wide_out[...] = widen(w_out_v[...]).T.astype(BF16)
         rates = jnp.concatenate([carry_x_v[...], carry_y_v[...]], axis=0)
         rates = jnp.concatenate([rates] * 8, axis=1)
         aux_ref[0:2, :] = jnp.log(rates)
@@ -371,7 +372,7 @@
         copy.wait()
 
 
-def call(kernel, out_shape, scratch, args, name, space=pltpu.VMEM, limit=24, out_space=pltpu.VMEM):
+def call(kernel, out_shape, scratch, args, name, space=pltpu.VMEM, limit=24, out_space=pltpu.VMEM, cost=0):
     vmem = pl.BlockSpec(memory_space=out_space)
     return pl.pallas_call(
         kernel,
@@ -380,6 +381,7 @@
         out_specs=jax.tree.map(lambda _: vmem, out_shape),
         scratch_shapes=scratch,
         compiler_params=pltpu.CompilerParams(vmem_limit_bytes=limit * 1024 * 1024),
+        cost_estimate=pl.CostEstimate(flops=cost, bytes_accessed=cost // 500, transcendentals=0) if cost else None,
         name=name,
     )(*args)
 
@@ -417,6 +419,7 @@
                 (aux, *seam_ins, wide_in, w_down, w_mid, w_up, wide_out),
                 "seams_net",
             )
+        term = call(term_kernel, plane, [], (aux, south, north), "terms", cost=2 * 10**9)
         got = lax.all_to_all(msg, "y", 0, 0)
         group_out = (shape((2 * xs, 40, 128), F32), plane, row)
         if step == 0:
@@ -424,12 +427,12 @@
                 group_kernel,
                 (*group_out, shape((ys, 128), F32)),
                 [lines, lines],
-                (aux, got, west, south, north),
+                (aux, got, west, term),
                 "group",
             )
         else:
             msg, start, start_f = call(
-                group_kernel, group_out, [lines, lines], (aux, got, factors_y, west, south, north), "group"
+                group_kernel, group_out, [lines, lines], (aux, got, factors_y, west, term), "group"
             )
         got = lax.all_to_all(msg, ("x", "core"), 0, 0)
         msg, *seam_ins = call(

time: 88.8 us -> 90 us (1.014)
  blocking collectives: 78.6 us -> 52.1 us
  waiting for transfers between devices: 0 us -> 16.1 us
  starting transfers between devices: 0 us -> 11.2 us
    all_to_all x2 -> x0, blocking collectives: 26.5 us -> none  [per_device(): got = lax.all_to_all(msg, 'y', 0, 0)]
    all_to_all x0 -> x2, waiting for transfers between devices: none -> 16.1 us  [per_device(): got = lax.all_to_all(msg, 'y', 0, 0)]
    all_to_all x0 -> x2, starting transfers between devices: none -> 11.2 us  [per_device(): got = lax.all_to_all(msg, 'y', 0, 0)]
    pallas_call x7 -> x9, Pallas kernels: 9.55 us -> 9.9 us  [call(): pl.pallas_call(kernel, out_shape=out_shape, in_specs=[pl.BlockSpec(memory...]
  transfers between devices with their start and end apart: 0 -> 2, of which waited for: 0 -> 2; matrix products, arithmetic and copies ran while one was open for 0% -> 0% of each run, Pallas kernels for 0% -> 0%
where the time goes in v5:
time: 90 us; the launch traced here: 89.5 us
  blocking collectives  52.1 us (58%)
  waiting for transfers between devices  16.1 us (18%)
  starting transfers between devices  11.2 us (12%)
  Pallas kernels  9.9 us (11%)
    all_to_all x2, blocking collectives, per_device(): got = lax.all_to_all(msg, 'z', 0, 0)  28.2 us
    all_to_all x2, blocking collectives, per_device(): got = lax.all_to_all(msg, ('x', 'core'), 0, 0)  23.9 us
    all_to_all x2, waiting for transfers between devices, per_device(): got = lax.all_to_all(msg, 'y', 0, 0)  16.1 us
    all_to_all x2, starting transfers between devices, per_device(): got = lax.all_to_all(msg, 'y', 0, 0)  11.2 us
    pallas_call x9, Pallas kernels, call(): pl.pallas_call(kernel, out_shape=out_shape, in_specs=[pl.BlockSpec(memory...  9.9 us
  transfers between devices with their start and end apart: 2, of which 2 were waited for; matrix products, arithmetic and copies ran while one was open for 0% of the time, Pallas kernels for 0%

profile of v5, /device:TPU:1, one launch (start us, length us, event | category | flops | bytes accessed | tf_op | source)
XLA Modules:
  0.0 89.5 jit_solution(5003052473743667081)
XLA Ops:
  0.0 4.5 %net_first.1 = (bf16[1024,128]{1,0:T(8,128)(2,1)}, f32[8,40,128]{2,1,0:T(8,128)}, f32[2,16,128]{2,1,0:T(8,128)}, f32[2,16,128]{2,1,0:T(8,128)}, f32[2,16,128]{2,...) custom-call(bf16[16,64,128]{2,1,0:T(8,128)(2,1)} %bitcast.6, ...), custom_call_target="tpu_custom_call" | custom-call | tf_op jit(solution)/shard_map/net_first/pallas_call | solution.py:377
  4.5 0.0 copy-start.3
  4.5 0.0 copy-start.7
  4.5 0.0 copy-start.8
  4.5 7.8 %all-to-all-start = ((f32[8,40,128]{2,1,0:T(8,128)}), f32[8,40,128]{2,1,0:T(8,128)S(1)}, u32[]{:S(2)}, u32[]{:S(2)}) async-start(f32[8,40,128]{2,1,0:T(8,128)} %get-tuple-element.38), calls=%async_computation | async-start | bytes 327680 | tf_op jit(solution)/shard_map/all_to_all | solution.py:423
  12.3 0.0 copy-done.3
  12.3 0.0 copy-done.7
  12.4 0.0 copy-done.8
  12.4 0.0 copy-start.9
  12.4 8.3 %all-to-all-done.got = f32[8,40,128]{2,1,0:T(8,128)S(1)} async-done(((f32[8,40,128]{2,1,0:T(8,128)}), f32[8,40,128]{2,1,0:T(8,128)S(1)}, u32[]{:S(2)}, u32[]{:S(2)}) %all-to-all-start) | async-done | bytes 163872 | tf_op jit(solution)/shard_map/all_to_all | solution.py:423
  20.7 0.0 copy-done.9
  20.7 0.2 group.2
  20.9 0.0 copy-start.4
  20.9 0.0 copy-start.5
  20.9 12.2 %all_to_all.30.got = f32[8,40,128]{2,1,0:T(8,128)S(1)} all-to-all(f32[8,40,128]{2,1,0:T(8,128)S(1)} %get-tuple-element.42), channel_id=1, replica_groups=mesh['x'=4,'y'=8,'z'=8,'core'=2] {'x','core'}, dimensions={0} | all-to-all | bytes 327680 | tf_op jit(solution)/shard_map/all_to_all | solution.py:437
  33.1 0.3 turn.2
  33.4 0.0 copy-start.1
  33.4 0.0 copy-start.2
  33.5 18.0 %all_to_all.31.got = f32[8,40,128]{2,1,0:T(8,128)S(1)} all-to-all(f32[8,40,128]{2,1,0:T(8,128)S(1)} %get-tuple-element.45), channel_id=1, replica_groups=mesh['x'=4,'y'=8,'z'=8,'core'=2] {'z'}, dimensions={0} | all-to-all | bytes 327680 | tf_op jit(solution)/shard_map/all_to_all | solution.py:445
  51.5 0.0 copy-done.6
  51.5 0.0 copy-done.4
  51.5 0.0 copy-done
  51.5 0.0 copy-done.1
  51.5 0.0 copy-done.2
  51.5 3.3 %seams_net.1 = (bf16[1024,128]{1,0:T(8,128)(2,1)S(1)}, f32[8,32,128]{2,1,0:T(8,128)}, f32[2,16,128]{2,1,0:T(8,128)S(1)}, f32[2,16,128]{2,1,0:T(8,128)S(1)}, f32[...) custom-call(f32[24,128]{1,0:T(8,128)S(1)} %copy-done.3, bf16[1024,128]{1,0:T(8,128)(2,1)S(1)} %copy-done.4, ...), custom_call_target="tpu_custom_call" | custom-call | tf_op jit(solution)/shard_map/seams_net/pallas_call | solution.py:377
  54.9 3.4 %all-to-all-start.3 = ((f32[8,32,128]{2,1,0:T(8,128)}), f32[8,32,128]{2,1,0:T(8,128)S(1)}, u32[]{:S(2)}, u32[]{:S(2)}) async-start(f32[8,32,128]{2,1,0:T(8,128)} %get-tuple-element.53), calls=%async_computation.3 | async-start | bytes 262144 | tf_op jit(solution)/shard_map/all_to_all | solution.py:423
  58.3 7.8 %all-to-all-done.3.got = f32[8,32,128]{2,1,0:T(8,128)S(1)} async-done(((f32[8,32,128]{2,1,0:T(8,128)}), f32[8,32,128]{2,1,0:T(8,128)S(1)}, u32[]{:S(2)}, u32[]{:S(2)}) %all-to-all-start.3) | async-done | bytes 131104 | tf_op jit(solution)/shard_map/all_to_all | solution.py:423
  66.1 0.2 group.3
  66.3 11.8 %all_to_all.32.got = f32[8,40,128]{2,1,0:T(8,128)S(1)} all-to-all(f32[8,40,128]{2,1,0:T(8,128)S(1)} %get-tuple-element.58), channel_id=1, replica_groups=mesh['x'=4,'y'=8,'z'=8,'core'=2] {'x','core'}, dimensions={0} | all-to-all | bytes 327680 | tf_op jit(solution)/shard_map/all_to_all | solution.py:437
  78.1 0.3 turn.3
  78.4 10.1 %all_to_all.33.got = f32[8,32,128]{2,1,0:T(8,128)S(1)} all-to-all(f32[8,32,128]{2,1,0:T(8,128)S(1)} %get-tuple-element.61), channel_id=1, replica_groups=mesh['x'=4,'y'=8,'z'=8,'core'=2] {'z'}, dimensions={0} | all-to-all | bytes 262144 | tf_op jit(solution)/shard_map/all_to_all | solution.py:445
  88.6 1.0 %seams_last.1 = bf16[16,64,128]{2,1,0:T(8,128)(2,1)} custom-call(f32[24,128]{1,0:T(8,128)S(1)} %copy-done.3, bf16[1024,128]{1,0:T(8,128)(2,1)S(1)} %get-tuple-element.52.pred, f32[8,32,128]{2,1,0:T(8,128)S(1)} %all_to_all.33.got, f32[2,16,128]{2,1,0:T(8,128)S(1)} %get-tuple-element.62.drift, f32[2,16,128]{2,1,0:T(8,128)S(1)} %get-tuple-element.63.low, ...), custom_call_target="tpu_custom_call" | custom-call | tf_op jit(solution)/shard_map/seams_last/pallas_call | solution.py:377
  (5 shorter events, 0.1 us)
Async XLA Ops:
  4.5 7.8 %copy-start.3 = (f32[24,128]{1,0:T(8,128)S(1)}, f32[24,128]{1,0:T(8,128)}, u32[]{:S(2)}) copy-start(f32[24,128]{1,0:T(8,128)} %get-tuple-element.36.aux_ref) | copy-start | bytes 36868
  4.5 7.8 %copy-start.7 = (f32[2,16,128]{2,1,0:T(8,128)S(1)}, f32[2,16,128]{2,1,0:T(8,128)}, u32[]{:S(2)}) copy-start(f32[2,16,128]{2,1,0:T(8,128)} %get-tuple-element.40.south) | copy-start | bytes 49156
  4.5 7.8 %copy-start.8 = (f32[2,16,128]{2,1,0:T(8,128)S(1)}, f32[2,16,128]{2,1,0:T(8,128)}, u32[]{:S(2)}) copy-start(f32[2,16,128]{2,1,0:T(8,128)} %get-tuple-element.41.north) | copy-start | bytes 49156
  4.5 16.2 %all-to-all-start = ((f32[8,40,128]{2,1,0:T(8,128)}), f32[8,40,128]{2,1,0:T(8,128)S(1)}, u32[]{:S(2)}, u32[]{:S(2)}) async-start(f32[8,40,128]{2,1,0:T(8,128)} %get-tuple-element.38), calls=%async_computation | async-start | bytes 327680 | tf_op jit(solution)/shard_map/all_to_all | solution.py:423
  12.4 8.4 %copy-start.9 = (f32[2,16,128]{2,1,0:T(8,128)S(1)}, f32[2,16,128]{2,1,0:T(8,128)}, u32[]{:S(2)}) copy-start(f32[2,16,128]{2,1,0:T(8,128)} %get-tuple-element.39.rest_0_) | copy-start | bytes 49156
  20.7 30.8 %copy-start.6 = (bf16[512,128]{1,0:T(8,128)(2,1)S(1)}, bf16[512,128]{1,0:T(8,128)(2,1)}, u32[]{:S(2)}) copy-start(bf16[512,128]{1,0:T(8,128)(2,1)} %get-tuple-element.51.wide_out) | copy-start | bytes 393220
  20.9 30.6 %copy-start.4 = (bf16[1024,128]{1,0:T(8,128)(2,1)S(1)}, bf16[1024,128]{1,0:T(8,128)(2,1)}, u32[]{:S(2)}) copy-start(bf16[1024,128]{1,0:T(8,128)(2,1)} %get-tuple-element.37.pred) | copy-start | bytes 786436
  20.9 30.6 %copy-start.5 = (bf16[128,512]{1,0:T(8,128)(2,1)S(1)}, bf16[128,512]{1,0:T(8,128)(2,1)}, u32[]{:S(2)}) copy-start(bf16[128,512]{1,0:T(8,128)(2,1)} %get-tuple-element.50.wide_in) | copy-start | bytes 393220
  33.1 18.4 %copy-start = (bf16[7,128,128]{2,1,0:T(8,128)(2,1)S(1)}, bf16[7,128,128]{2,1,0:T(8,128)(2,1)}, u32[]{:S(2)}) copy-start(bf16[7,128,128]{2,1,0:T(8,128)(2,1)} %w_mid.3) | copy-start | bytes 688132
  33.4 18.1 %copy-start.1 = (bf16[512,128]{1,0:T(8,128)(2,1)S(1)}, bf16[512,128]{1,0:T(8,128)(2,1)}, u32[]{:S(2)}) copy-start(bf16[512,128]{1,0:T(8,128)(2,1)} %w_down.3) | copy-start | bytes 393220
  33.4 18.1 %copy-start.2 = (bf16[128,512]{1,0:T(8,128)(2,1)S(1)}, bf16[128,512]{1,0:T(8,128)(2,1)}, u32[]{:S(2)}) copy-start(bf16[128,512]{1,0:T(8,128)(2,1)} %w_up.3) | copy-start | bytes 393220
  54.9 11.2 %all-to-all-start.3 = ((f32[8,32,128]{2,1,0:T(8,128)}), f32[8,32,128]{2,1,0:T(8,128)S(1)}, u32[]{:S(2)}, u32[]{:S(2)}) async-start(f32[8,32,128]{2,1,0:T(8,128)} %get-tuple-element.53), calls=%async_computation.3 | async-start | bytes 262144 | tf_op jit(solution)/shard_map/all_to_all | solution.py:423

commit v6 on v5

--- a/solution.py
+++ b/solution.py
@@ -12,9 +12,12 @@
 BF16 = jnp.bfloat16
 
 
+def silu_of_half(half):
+    return half + half * jnp.tanh(half)
+
+
 def silu(v):
-    half = 0.5 * v
-    return half + half * jnp.tanh(half)
+    return silu_of_half(0.5 * v)
 
 
 def iotas(rows):
@@ -57,11 +60,11 @@
     msg, west_ref, south_ref, north_ref = outs
     for qx in range(2):
         rows = pl.ds(512 * qx, 512)
-        first = silu(jnp.dot(state[rows, :], wide_in[...], preferred_element_type=F32)).astype(BF16)
+        first = silu_of_half(jnp.dot(state[rows, :], wide_in[...], preferred_element_type=F32)).astype(BF16)
         first_ref[rows, :] = first
         pre = jnp.dot(first, w_down[...], preferred_element_type=F32)
-        pre = pre * lax.rsqrt(jnp.mean(pre * pre, axis=-1, keepdims=True) + 1e-06)
-        second_ref[pl.ds(256 + 512 * qx, 512), :] = silu(pre).astype(BF16)
+        half = pre * (0.5 * lax.rsqrt(jnp.mean(pre * pre, axis=-1, keepdims=True) + 1e-06))
+        second_ref[pl.ds(256 + 512 * qx, 512), :] = silu_of_half(half).astype(BF16)
 
     sub, lane = iotas(16)
     by, bx = sub % 4, sub // 4
@@ -71,7 +74,7 @@
     log_x, occupied, col = aux.log_x, aux.occupied, aux.col
     second_ref[pl.ds(0, 256), :] = jnp.zeros((256, 128), BF16)
     second_ref[pl.ds(1280, 256), :] = jnp.zeros((256, 128), BF16)
-    mids = jnp.concatenate([w_mid[k] for k in range(7)], axis=0)
+    mids = jnp.concatenate([0.5 * w_mid[k] for k in range(7)], axis=0)
     for group in range(2):
         base = 512 * group
         rows = pl.ds(base, 512)
@@ -91,7 +94,7 @@
         parts += [jnp.concatenate(p, axis=0) for p in (left, right, below, above)]
         stacked = jnp.concatenate(parts, axis=1)
         mixed = jnp.dot(stacked, mids, preferred_element_type=F32)
-        middle = (second.astype(F32) + silu(mixed)).astype(BF16)
+        middle = (second.astype(F32) + silu_of_half(mixed)).astype(BF16)
         upper = jnp.dot(middle, w_up[...], preferred_element_type=F32) + first_ref[rows, :].astype(F32)
         upper = silu(upper).astype(BF16)
         update = jnp.dot(upper, wide_out[...], preferred_element_type=F32)
@@ -148,22 +151,21 @@
         msg[:, pl.ds(at, size), :] = jnp.broadcast_to(value[None], (msg.shape[0], size, 128))
 
 
-def line_of(planes, ref):
+def line_of(planes):
     sub, lane = iotas(16)
     value = planes[0] + planes[1]
-    value = value + turn_lanes(value, 64)
-    value = (value + turn_lanes(value, 32)) * 0.125
-    by, part = sub % 4, lane // 32
-    value = jnp.where(((part == 0) & (by == 0)) | ((part == 3) & (by == 3)), value, 0.0)
-    ref[...] = value + turn_rows(value, -3)
-    return ref[pl.ds(0, 4, stride=4), :]
-
-
-def everywhere(x, which):
-    part = lax.broadcasted_iota(jnp.int32, x.shape, x.ndim - 1) // 32
-    x = jnp.where(part == which, x, 0.0)
-    x = x + turn_lanes(x, 32)
-    return x + turn_lanes(x, 64)
+    value = ((value + turn_lanes(value, 32)) + (turn_lanes(value, 64) + turn_lanes(value, 96))) * 0.125
+    low, line = lane < 64, value
+    for qz in range(4):
+        line = jnp.where(low & (sub == qz), turn_rows(value, -3 * qz), line)
+        line = jnp.where(~low & (sub == qz), turn_rows(value, -3 * qz - 3), line)
+    return line[0:4]
+
+
+def both_strips(line):
+    low = iotas(4)[1] < 64
+    other = turn_lanes(line, 64)
+    return jnp.where(low, line, other), jnp.where(low, other, line)
 
 
 def four(line):
@@ -180,11 +182,11 @@
 
 def group_kernel(aux_ref, got, *rest):
     if got.shape[1] > 32:
-        west, term, msg, start_ref, start_f_ref, factor_ref, line_ref, line2_ref = rest
+        west, south, north, msg, start_ref, start_f_ref, factor_ref = rest
         for k in range(got.shape[0]):
             factor_ref[k : k + 1, :] = got[k, 32:33, :]
     else:
-        factor_ref, west, term, msg, start_ref, start_f_ref, line_ref, line2_ref = rest
+        factor_ref, west, south, north, msg, start_ref, start_f_ref = rest
     aux = Aux(aux_ref)
     zero, one = [jnp.zeros((16, 128), F32)] * 2, jnp.ones((1, 128), F32)
     before, before_f, total, total_f = zero, one, zero, one
@@ -196,8 +198,8 @@
         total_f = f * total_f
     start = [before[h] - west[h] for h in range(2)]
     factor_y = edge_y(aux)
-    term_y = [term[h] for h in range(2)]
-    line_start, line_total = line_of(start, line_ref), line_of(total, line2_ref)
+    term_y = [north[h] - factor_y * south[h] for h in range(2)]
+    line_start, line_total = line_of(start), line_of(total)
     for h in range(2):
         start_ref[h] = start[h]
     start_f_ref[...] = jnp.broadcast_to(before_f, (8, 128))
@@ -217,45 +219,37 @@
             msg[2 * x + core, 32:40, :] = tail
 
 
-def term_kernel(aux_ref, south, north, term_ref):
-    factor = edge_y(Aux(aux_ref))
-    for h in range(2):
-        term_ref[h] = north[h] - factor * south[h]
-
-
-def turn_kernel(aux_ref, got, start_ref, start_f_ref, south, north, msg, drift_ref, low_ref, pair_ref, pair_f_ref, line_ref):
+def turn_kernel(aux_ref, got, start_ref, start_f_ref, south, north, msg, drift_ref, low_ref, pair_ref, pair_f_ref):
     aux = Aux(aux_ref)
     first = aux.core == 0.0
     begin = [jnp.zeros((16, 128), F32)] * 2
-    begin_line = jnp.zeros((4, 128), F32)
-    term, tail = [0.0, 0.0], 0.0
+    lines = [jnp.zeros((4, 128), F32)] * 2
+    term, mine_tails = [0.0, 0.0], [0.0, 0.0]
     for x in range(got.shape[0] // 2):
         one, two = halves(got, 2 * x), halves(got, 2 * x + 1)
         tails = got[2 * x, 32:40, :], got[2 * x + 1, 32:40, :]
-        own_tail, other_tail = jnp.where(first, *tails), jnp.where(first, *tails[::-1])
+        tails = [jnp.where(first, *tails), jnp.where(first, *tails[::-1])]
         go, mine = aux.x > x, aux.x == x
         own = [jnp.where(first, one[h], two[h]) for h in range(2)]
-        begin = [jnp.where(go, own_tail[4:5] * begin[h] + own[h], begin[h]) for h in range(2)]
-        begin_line = jnp.where(go, other_tail[4:5] * begin_line + other_tail[0:4], begin_line)
+        begin = [jnp.where(go, tails[0][4:5] * begin[h] + own[h], begin[h]) for h in range(2)]
+        lines = [jnp.where(go, t[4:5] * line + t[0:4], line) for t, line in zip(tails, lines)]
         term = [jnp.where(mine, jnp.where(first, two[h], one[h]), term[h]) for h in range(2)]
-        tail = jnp.where(mine, other_tail, tail)
+        mine_tails = [jnp.where(mine, t, kept) for t, kept in zip(tails, mine_tails)]
     away = aux.col == 0.0
-    drift = [jnp.where(away, 0.0, start_f_ref[0:1, :] * begin[h] + start_ref[h]) for h in range(2)]
-    line = line_of(drift, line_ref)
-    other_line = jnp.where(away, 0.0, tail[4:5] * begin_line + tail[0:4])
-    factor, other_factor = edge_y(aux), tail[5:6]
-    south_line = everywhere(line, 0)
-    term_line = four(everywhere(line, 3) - factor * south_line)
-    other_line = four(everywhere(other_line, 3) - other_factor * everywhere(other_line, 0))
-    south_line = four(south_line)
+    lines = [jnp.where(away, 0.0, t[4:5] * line + t[0:4]) for t, line in zip(mine_tails, lines)]
+    factor, other_factor = (t[5:6] for t in mine_tails)
+    strips = [both_strips(line) for line in lines]
+    south_line = four(strips[0][0])
+    term_line = four(strips[0][1] - factor * strips[0][0])
+    other_line = four(strips[1][1] - other_factor * strips[1][0])
     places = place_y(*iotas(16))
     pairs = []
     for h in range(2):
         gain = gain_at(places[h], aux.log_x)
-        drift_ref[h] = drift[h]
+        drift_ref[h] = jnp.where(away, 0.0, start_f_ref[0:1, :] * begin[h] + start_ref[h])
         low_ref[h] = south[h] + gain * south_line
         own = north[h] - factor * south[h] + gain * term_line
-        other = term[h] + gain_at(places[h], tail[6:7]) * other_line
+        other = term[h] + gain_at(places[h], mine_tails[1][6:7]) * other_line
         pair_ref[h] = jnp.where(first, 0.0, other)
         pairs.append(jnp.where(first, other_factor * own + other, factor * other + own))
     pair_f_ref[...] = jnp.broadcast_to(jnp.where(first, 1.0, other_factor), (8, 128))
@@ -284,12 +278,14 @@
         e = drift_y[q % 2]
         e = jnp.where(sy == q // 2, e, swap_sy(e, lane))
         for qz in range(4):
-            m = jnp.where(bx == qz, d, 0.0)
-            m = m + turn_rows(m, 8)
-            spread_x[q][qz] = m + turn_rows(m, 4)
-            m = turn_rows(jnp.where(by == qz, e, 0.0), -qz)
-            m = m + turn_rows(m, 1)
-            spread_y[q][qz] = m + turn_rows(m, 2)
+            m = d
+            for k in range(4):
+                m = jnp.where(bx == k, turn_rows(d, 4 * (k - qz)), m)
+            spread_x[q][qz] = m
+            m = e
+            for k in range(4):
+                m = jnp.where(by == k, turn_rows(e, k - qz), m)
+            spread_y[q][qz] = m
     for qx in range(4):
         for qy in range(4):
             for qz in range(4):
@@ -321,7 +317,7 @@
     columns = lax.axis_size("y")
     copies[0].wait()
     copies[1].wait()
-    wide_in[...] = widen(w_in_v[...]).astype(BF16)
+    wide_in[...] = (0.5 * widen(w_in_v[...])).astype(BF16)
     turned = jnp.swapaxes(latent_v[...].astype(F32), 0, 1)
     state[...] = turned.reshape(1024, 128).astype(BF16)
     for copy in copies[2:]:
@@ -372,7 +368,7 @@
         copy.wait()
 
 
-def call(kernel, out_shape, scratch, args, name, space=pltpu.VMEM, limit=24, out_space=pltpu.VMEM, cost=0):
+def call(kernel, out_shape, scratch, args, name, space=pltpu.VMEM, limit=24, out_space=pltpu.VMEM):
     vmem = pl.BlockSpec(memory_space=out_space)
     return pl.pallas_call(
         kernel,
@@ -381,7 +377,6 @@
         out_specs=jax.tree.map(lambda _: vmem, out_shape),
         scratch_shapes=scratch,
         compiler_params=pltpu.CompilerParams(vmem_limit_bytes=limit * 1024 * 1024),
-        cost_estimate=pl.CostEstimate(flops=cost, bytes_accessed=cost // 500, transcendentals=0) if cost else None,
         name=name,
     )(*args)
 
@@ -390,7 +385,6 @@
     xs, ys, zs, _ = sizes
     shape = jax.ShapeDtypeStruct
     plane, row = shape((2, 16, 128), F32), shape((8, 128), F32)
-    lines = pltpu.VMEM((16, 128), F32)
     net_scratch = [
         pltpu.VMEM((1024, 128), BF16),
         pltpu.VMEM((1024, 512), BF16),
@@ -419,26 +413,25 @@
                 (aux, *seam_ins, wide_in, w_down, w_mid, w_up, wide_out),
                 "seams_net",
             )
-        term = call(term_kernel, plane, [], (aux, south, north), "terms", cost=2 * 10**9)
         got = lax.all_to_all(msg, "y", 0, 0)
         group_out = (shape((2 * xs, 40, 128), F32), plane, row)
         if step == 0:
             msg, start, start_f, factors_y = call(
                 group_kernel,
                 (*group_out, shape((ys, 128), F32)),
-                [lines, lines],
-                (aux, got, west, term),
+                [],
+                (aux, got, west, south, north),
                 "group",
             )
         else:
             msg, start, start_f = call(
-                group_kernel, group_out, [lines, lines], (aux, got, factors_y, west, term), "group"
+                group_kernel, group_out, [], (aux, got, factors_y, west, south, north), "group"
             )
         got = lax.all_to_all(msg, ("x", "core"), 0, 0)
         msg, *seam_ins = call(
             turn_kernel,
             (shape((zs, tall, 128), F32), plane, plane, plane, row),
-            [lines],
+            [],
             (aux, got, start, start_f, south, north),
             "turn",
         )

time: 90 us -> 87.7 us (0.974)
  blocking collectives: 52.1 us -> 78.6 us
  waiting for transfers between devices: 16.1 us -> 0 us
  starting transfers between devices: 11.2 us -> 0 us
  Pallas kernels: 9.9 us -> 8.46 us
    all_to_all x0 -> x2, blocking collectives: none -> 26.5 us  [per_device(): got = lax.all_to_all(msg, 'y', 0, 0)]
    all_to_all x2 -> x0, waiting for transfers between devices: 16.1 us -> none  [per_device(): got = lax.all_to_all(msg, 'y', 0, 0)]
    all_to_all x2 -> x0, starting transfers between devices: 11.2 us -> none  [per_device(): got = lax.all_to_all(msg, 'y', 0, 0)]
    pallas_call x9 -> x7, Pallas kernels: 9.9 us -> 8.46 us  [call(): pl.pallas_call(kernel, out_shape=out_shape, in_specs=[pl.BlockSpec(memory...]
  transfers between devices with their start and end apart: 2 -> 0, of which waited for: 2 -> 0; matrix products, arithmetic and copies ran while one was open for 0% -> 0% of each run, Pallas kernels for 0% -> 0%
where the time goes in v6:
time: 87.7 us; the launch traced here: 87.3 us
  blocking collectives  78.6 us (90%)
  Pallas kernels  8.46 us (10%)
    all_to_all x2, blocking collectives, per_device(): got = lax.all_to_all(msg, 'z', 0, 0)  28.2 us
    all_to_all x2, blocking collectives, per_device(): got = lax.all_to_all(msg, 'y', 0, 0)  26.5 us
    all_to_all x2, blocking collectives, per_device(): got = lax.all_to_all(msg, ('x', 'core'), 0, 0)  23.9 us
    pallas_call x7, Pallas kernels, call(): pl.pallas_call(kernel, out_shape=out_shape, in_specs=[pl.BlockSpec(memory...  8.46 us

profile of v6, /device:TPU:1, one launch (start us, length us, event | category | flops | bytes accessed | tf_op | source)
XLA Modules:
  0.0 87.3 jit_solution(13098637664640391008)
XLA Ops:
  0.0 4.4 %net_first.1 = (bf16[1024,128]{1,0:T(8,128)(2,1)}, f32[8,40,128]{2,1,0:T(8,128)}, f32[2,16,128]{2,1,0:T(8,128)}, f32[2,16,128]{2,1,0:T(8,128)}, f32[2,16,128]{2,...) custom-call(bf16[16,64,128]{2,1,0:T(8,128)(2,1)} %bitcast.6, ...), custom_call_target="tpu_custom_call" | custom-call | tf_op jit(solution)/shard_map/net_first/pallas_call | solution.py:373
  4.4 0.0 copy-start.3
  4.4 0.0 copy-start.7
  4.4 0.0 copy-start.8
  4.5 0.0 copy-start.9
  4.5 16.2 %all_to_all.30.got = f32[8,40,128]{2,1,0:T(8,128)S(1)} all-to-all(f32[8,40,128]{2,1,0:T(8,128)} %get-tuple-element.38), channel_id=1, replica_groups=mesh['x'=4,'y'=8,'z'=8,'core'=2] {'y'}, dimensions={0} | all-to-all | bytes 327680 | tf_op jit(solution)/shard_map/all_to_all | solution.py:416
  20.6 0.0 copy-done.3
  20.6 0.0 copy-done.7
  20.6 0.0 copy-done.8
  20.6 0.0 copy-done.9
  20.7 0.0 copy-start.6
  20.7 0.1 group.2
  20.8 0.0 copy-start.4
  20.8 0.0 copy-start.5
  20.8 12.1 %all_to_all.31.got = f32[8,40,128]{2,1,0:T(8,128)S(1)} all-to-all(f32[8,40,128]{2,1,0:T(8,128)S(1)} %get-tuple-element.42), channel_id=1, replica_groups=mesh['x'=4,'y'=8,'z'=8,'core'=2] {'x','core'}, dimensions={0} | all-to-all | bytes 327680 | tf_op jit(solution)/shard_map/all_to_all | solution.py:430
  33.0 0.1 turn.2
  33.1 0.0 copy-start.1
  33.1 0.0 copy-start.2
  33.1 18.0 %all_to_all.32.got = f32[8,40,128]{2,1,0:T(8,128)S(1)} all-to-all(f32[8,40,128]{2,1,0:T(8,128)S(1)} %get-tuple-element.45), channel_id=1, replica_groups=mesh['x'=4,'y'=8,'z'=8,'core'=2] {'z'}, dimensions={0} | all-to-all | bytes 327680 | tf_op jit(solution)/shard_map/all_to_all | solution.py:438
  51.2 0.0 copy-done.6
  51.2 0.0 copy-done.4
  51.2 0.0 copy-done.5
  51.2 0.0 copy-done
  51.2 0.0 copy-done.1
  51.2 0.0 copy-done.2
  51.2 2.6 %seams_net.1 = (bf16[1024,128]{1,0:T(8,128)(2,1)S(1)}, f32[8,32,128]{2,1,0:T(8,128)S(1)}, f32[2,16,128]{2,1,0:T(8,128)S(1)}, f32[2,16,128]{2,1,0:T(8,128)S(1)}, ...) custom-call(f32[24,128]{1,0:T(8,128)S(1)} %copy-done.3, bf16[1024,128]{1,0:T(8,128)(2,1)S(1)} %copy-done.4, ...), custom_call_target="tpu_custom_call" | custom-call | tf_op jit(solution)/shard_map/seams_net/pallas_call | solution.py:373
  53.8 10.3 %all_to_all.33.got = f32[8,32,128]{2,1,0:T(8,128)S(1)} all-to-all(f32[8,32,128]{2,1,0:T(8,128)S(1)} %get-tuple-element.53), channel_id=1, replica_groups=mesh['x'=4,'y'=8,'z'=8,'core'=2] {'y'}, dimensions={0} | all-to-all | bytes 262144 | tf_op jit(solution)/shard_map/all_to_all | solution.py:416
  64.1 0.1 group.3
  64.2 11.8 %all_to_all.34.got = f32[8,40,128]{2,1,0:T(8,128)S(1)} all-to-all(f32[8,40,128]{2,1,0:T(8,128)S(1)} %get-tuple-element.58), channel_id=1, replica_groups=mesh['x'=4,'y'=8,'z'=8,'core'=2] {'x','core'}, dimensions={0} | all-to-all | bytes 327680 | tf_op jit(solution)/shard_map/all_to_all | solution.py:430
  76.0 0.1 turn.3
  76.1 10.1 %all_to_all.35.got = f32[8,32,128]{2,1,0:T(8,128)S(1)} all-to-all(f32[8,32,128]{2,1,0:T(8,128)S(1)} %get-tuple-element.61), channel_id=1, replica_groups=mesh['x'=4,'y'=8,'z'=8,'core'=2] {'z'}, dimensions={0} | all-to-all | bytes 262144 | tf_op jit(solution)/shard_map/all_to_all | solution.py:438
  86.3 1.0 %seams_last.1 = bf16[16,64,128]{2,1,0:T(8,128)(2,1)} custom-call(f32[24,128]{1,0:T(8,128)S(1)} %copy-done.3, bf16[1024,128]{1,0:T(8,128)(2,1)S(1)} %get-tuple-element.52.pred, f32[8,32,128]{2,1,0:T(8,128)S(1)} %all_to_all.35.got, f32[2,16,128]{2,1,0:T(8,128)S(1)} %get-tuple-element.62.drift, f32[2,16,128]{2,1,0:T(8,128)S(1)} %get-tuple-element.63.low, ...), custom_call_target="tpu_custom_call" | custom-call | tf_op jit(solution)/shard_map/seams_last/pallas_call | solution.py:373
  (1 shorter events, 0.0 us)
Async XLA Ops:
  4.4 16.2 %copy-start.3 = (f32[24,128]{1,0:T(8,128)S(1)}, f32[24,128]{1,0:T(8,128)}, u32[]{:S(2)}) copy-start(f32[24,128]{1,0:T(8,128)} %get-tuple-element.36.aux_ref) | copy-start | bytes 36868
  4.4 16.2 %copy-start.7 = (f32[2,16,128]{2,1,0:T(8,128)S(1)}, f32[2,16,128]{2,1,0:T(8,128)}, u32[]{:S(2)}) copy-start(f32[2,16,128]{2,1,0:T(8,128)} %get-tuple-element.40.rest_1_.south) | copy-start | bytes 49156
  4.4 16.2 %copy-start.8 = (f32[2,16,128]{2,1,0:T(8,128)S(1)}, f32[2,16,128]{2,1,0:T(8,128)}, u32[]{:S(2)}) copy-start(f32[2,16,128]{2,1,0:T(8,128)} %get-tuple-element.41.rest_2_.north) | copy-start | bytes 49156
  4.5 16.2 %copy-start.9 = (f32[2,16,128]{2,1,0:T(8,128)S(1)}, f32[2,16,128]{2,1,0:T(8,128)}, u32[]{:S(2)}) copy-start(f32[2,16,128]{2,1,0:T(8,128)} %get-tuple-element.39.rest_0_) | copy-start | bytes 49156
  20.7 30.5 %copy-start.6 = (bf16[512,128]{1,0:T(8,128)(2,1)S(1)}, bf16[512,128]{1,0:T(8,128)(2,1)}, u32[]{:S(2)}) copy-start(bf16[512,128]{1,0:T(8,128)(2,1)} %get-tuple-element.51.wide_out) | copy-start | bytes 393220
  20.8 30.3 %copy-start.4 = (bf16[1024,128]{1,0:T(8,128)(2,1)S(1)}, bf16[1024,128]{1,0:T(8,128)(2,1)}, u32[]{:S(2)}) copy-start(bf16[1024,128]{1,0:T(8,128)(2,1)} %get-tuple-element.37.pred) | copy-start | bytes 786436
  20.8 30.3 %copy-start.5 = (bf16[128,512]{1,0:T(8,128)(2,1)S(1)}, bf16[128,512]{1,0:T(8,128)(2,1)}, u32[]{:S(2)}) copy-start(bf16[128,512]{1,0:T(8,128)(2,1)} %get-tuple-element.50.wide_in) | copy-start | bytes 393220
  33.0 18.2 %copy-start = (bf16[7,128,128]{2,1,0:T(8,128)(2,1)S(1)}, bf16[7,128,128]{2,1,0:T(8,128)(2,1)}, u32[]{:S(2)}) copy-start(bf16[7,128,128]{2,1,0:T(8,128)(2,1)} %w_mid.3) | copy-start | bytes 688132
  33.1 18.1 %copy-start.1 = (bf16[512,128]{1,0:T(8,128)(2,1)S(1)}, bf16[512,128]{1,0:T(8,128)(2,1)}, u32[]{:S(2)}) copy-start(bf16[512,128]{1,0:T(8,128)(2,1)} %w_down.3) | copy-start | bytes 393220
  33.1 18.1 %copy-start.2 = (bf16[128,512]{1,0:T(8,128)(2,1)S(1)}, bf16[128,512]{1,0:T(8,128)(2,1)}, u32[]{:S(2)}) copy-start(bf16[128,512]{1,0:T(8,128)(2,1)} %w_up.3) | copy-start | bytes 393220

commit v7 on v6

--- a/solution.py
+++ b/solution.py
@@ -58,14 +58,6 @@
 def net(state, ready, weights, first_ref, second_ref, pred_ref, outs):
     wide_in, w_down, w_mid, w_up, wide_out = weights
     msg, west_ref, south_ref, north_ref = outs
-    for qx in range(2):
-        rows = pl.ds(512 * qx, 512)
-        first = silu_of_half(jnp.dot(state[rows, :], wide_in[...], preferred_element_type=F32)).astype(BF16)
-        first_ref[rows, :] = first
-        pre = jnp.dot(first, w_down[...], preferred_element_type=F32)
-        half = pre * (0.5 * lax.rsqrt(jnp.mean(pre * pre, axis=-1, keepdims=True) + 1e-06))
-        second_ref[pl.ds(256 + 512 * qx, 512), :] = silu_of_half(half).astype(BF16)
-
     sub, lane = iotas(16)
     by, bx = sub % 4, sub // 4
     total_x = [[None] * 4 for _ in range(4)]
@@ -75,15 +67,27 @@
     second_ref[pl.ds(0, 256), :] = jnp.zeros((256, 128), BF16)
     second_ref[pl.ds(1280, 256), :] = jnp.zeros((256, 128), BF16)
     mids = jnp.concatenate([0.5 * w_mid[k] for k in range(7)], axis=0)
-    for group in range(2):
-        base = 512 * group
-        rows = pl.ds(base, 512)
-        second = second_ref[pl.ds(base + 256, 512), :]
-        parts = [second, second_ref[pl.ds(base, 512), :], second_ref[pl.ds(base + 512, 512), :]]
+    firsts, middles, uppers = {}, {}, {}
+
+    def lower(k, n):
+        rows = pl.ds(n * k, n)
+        first = silu_of_half(jnp.dot(state[rows, :], wide_in[...], preferred_element_type=F32)).astype(BF16)
+        first_ref[rows, :] = first
+        firsts[k] = first
+
+    def down(k, n):
+        pre = jnp.dot(firsts.pop(k), w_down[...], preferred_element_type=F32)
+        half = pre * (0.5 * lax.rsqrt(jnp.mean(pre * pre, axis=-1, keepdims=True) + 1e-06))
+        second_ref[pl.ds(256 + n * k, n), :] = silu_of_half(half).astype(BF16)
+
+    def stencil(k, n):
+        base = n * k
+        second = second_ref[pl.ds(base + 256, n), :]
+        parts = [second, second_ref[pl.ds(base, n), :], second_ref[pl.ds(base + 512, n), :]]
         gap = jnp.zeros((64, 128), BF16)
         gap16 = jnp.zeros((16, 128), BF16)
         left, right, below, above = [], [], [], []
-        for plane in range(2):
+        for plane in range(n // 256):
             own = second[256 * plane : 256 * plane + 256]
             left += [gap, own[:192]]
             right += [own[64:], gap]
@@ -94,15 +98,21 @@
         parts += [jnp.concatenate(p, axis=0) for p in (left, right, below, above)]
         stacked = jnp.concatenate(parts, axis=1)
         mixed = jnp.dot(stacked, mids, preferred_element_type=F32)
-        middle = (second.astype(F32) + silu_of_half(mixed)).astype(BF16)
-        upper = jnp.dot(middle, w_up[...], preferred_element_type=F32) + first_ref[rows, :].astype(F32)
-        upper = silu(upper).astype(BF16)
-        update = jnp.dot(upper, wide_out[...], preferred_element_type=F32)
-        update = update.reshape(32, 16, 128) * occupied[None]
-        preds = (state[rows, :].astype(F32).reshape(32, 16, 128) + update).astype(BF16)
-        pred_ref[rows, :] = preds.reshape(512, 128)
-        for plane in range(2):
-            qx = 2 * group + plane
+        middles[k] = (second.astype(F32) + silu_of_half(mixed)).astype(BF16)
+
+    def up(k, n):
+        rows = pl.ds(n * k, n)
+        upper = jnp.dot(middles.pop(k), w_up[...], preferred_element_type=F32) + first_ref[rows, :].astype(F32)
+        uppers[k] = silu(upper).astype(BF16)
+
+    def out(k, n):
+        rows = pl.ds(n * k, n)
+        update = jnp.dot(uppers.pop(k), wide_out[...], preferred_element_type=F32)
+        update = update.reshape(n // 16, 16, 128) * occupied[None]
+        preds = (state[rows, :].astype(F32).reshape(n // 16, 16, 128) + update).astype(BF16)
+        pred_ref[rows, :] = preds.reshape(n, 128)
+        for plane in range(n // 256):
+            qx = n // 256 * k + plane
             pred = preds[16 * plane : 16 * plane + 16].astype(F32)
             for qy in range(4):
                 for qz in range(4):
@@ -113,6 +123,17 @@
                 s = (s + swap_sy(s, lane)) * 0.125
                 south[qx] = south[qx] + jnp.where(by == qz, turn_rows(s, qz), 0.0)
                 north[qx] = north[qx] + jnp.where(by == qz, turn_rows(s, qz - 3), 0.0)
+
+    for k in range(4):
+        lower(k, 256)
+        if k > 0:
+            down(k - 1, 256)
+    down(3, 256)
+    for k in range(2):
+        stencil(k, 512)
+    for k in range(2):
+        up(k, 512)
+        out(k, 512)
 
     west, east = [0.0] * 4, [0.0] * 4
     for qy in range(4):

time: 87.7 us -> 87.1 us (level)
  no operation moved by 1% of the time
where the time goes in v7:
time: 87.1 us; the launch traced here: 86.7 us
  blocking collectives  78.6 us (90%)
  Pallas kernels  7.9 us (9%)
    all_to_all x2, blocking collectives, per_device(): got = lax.all_to_all(msg, 'z', 0, 0)  28.2 us
    all_to_all x2, blocking collectives, per_device(): got = lax.all_to_all(msg, 'y', 0, 0)  26.5 us
    all_to_all x2, blocking collectives, per_device(): got = lax.all_to_all(msg, ('x', 'core'), 0, 0)  23.9 us
    pallas_call x7, Pallas kernels, call(): pl.pallas_call(kernel, out_shape=out_shape, in_specs=[pl.BlockSpec(memory...  7.9 us

profile of v7, /device:TPU:1, one launch (start us, length us, event | category | flops | bytes accessed | tf_op | source)
XLA Modules:
  0.0 86.7 jit_solution(17601058274764411026)
XLA Ops:
  0.0 4.1 %net_first.1 = (bf16[1024,128]{1,0:T(8,128)(2,1)}, f32[8,40,128]{2,1,0:T(8,128)}, f32[2,16,128]{2,1,0:T(8,128)}, f32[2,16,128]{2,1,0:T(8,128)}, f32[2,16,128]{2,...) custom-call(bf16[16,64,128]{2,1,0:T(8,128)(2,1)} %bitcast.6, ...), custom_call_target="tpu_custom_call" | custom-call | tf_op jit(solution)/shard_map/net_first/pallas_call | solution.py:394
  4.2 0.0 copy-start.3
  4.2 0.0 copy-start.7
  4.2 0.0 copy-start.8
  4.2 0.0 copy-start.9
  4.2 16.2 %all_to_all.30.got = f32[8,40,128]{2,1,0:T(8,128)S(1)} all-to-all(f32[8,40,128]{2,1,0:T(8,128)} %get-tuple-element.38), channel_id=1, replica_groups=mesh['x'=4,'y'=8,'z'=8,'core'=2] {'y'}, dimensions={0} | all-to-all | bytes 327680 | tf_op jit(solution)/shard_map/all_to_all | solution.py:437
  20.4 0.0 copy-done.3
  20.4 0.0 copy-done.7
  20.4 0.0 copy-done.8
  20.4 0.0 copy-done.9
  20.4 0.0 copy-start.6
  20.4 0.1 group.2
  20.6 0.0 copy-start.4
  20.6 0.0 copy-start.5
  20.6 12.1 %all_to_all.31.got = f32[8,40,128]{2,1,0:T(8,128)S(1)} all-to-all(f32[8,40,128]{2,1,0:T(8,128)S(1)} %get-tuple-element.42), channel_id=1, replica_groups=mesh['x'=4,'y'=8,'z'=8,'core'=2] {'x','core'}, dimensions={0} | all-to-all | bytes 327680 | tf_op jit(solution)/shard_map/all_to_all | solution.py:451
  32.7 0.1 turn.2
  32.8 0.0 copy-start.1
  32.8 0.0 copy-start.2
  32.9 18.0 %all_to_all.32.got = f32[8,40,128]{2,1,0:T(8,128)S(1)} all-to-all(f32[8,40,128]{2,1,0:T(8,128)S(1)} %get-tuple-element.45), channel_id=1, replica_groups=mesh['x'=4,'y'=8,'z'=8,'core'=2] {'z'}, dimensions={0} | all-to-all | bytes 327680 | tf_op jit(solution)/shard_map/all_to_all | solution.py:459
  50.9 0.0 copy-done.6
  50.9 0.0 copy-done.4
  50.9 0.0 copy-done.5
  50.9 0.0 copy-done
  50.9 0.0 copy-done.1
  50.9 0.0 copy-done.2
  50.9 2.3 %seams_net.1 = (bf16[1024,128]{1,0:T(8,128)(2,1)S(1)}, f32[8,32,128]{2,1,0:T(8,128)S(1)}, f32[2,16,128]{2,1,0:T(8,128)S(1)}, f32[2,16,128]{2,1,0:T(8,128)S(1)}, ...) custom-call(f32[24,128]{1,0:T(8,128)S(1)} %copy-done.3, bf16[1024,128]{1,0:T(8,128)(2,1)S(1)} %copy-done.4, ...), custom_call_target="tpu_custom_call" | custom-call | tf_op jit(solution)/shard_map/seams_net/pallas_call | solution.py:394
  53.2 10.3 %all_to_all.33.got = f32[8,32,128]{2,1,0:T(8,128)S(1)} all-to-all(f32[8,32,128]{2,1,0:T(8,128)S(1)} %get-tuple-element.53), channel_id=1, replica_groups=mesh['x'=4,'y'=8,'z'=8,'core'=2] {'y'}, dimensions={0} | all-to-all | bytes 262144 | tf_op jit(solution)/shard_map/all_to_all | solution.py:437
  63.5 0.1 group.3
  63.7 11.8 %all_to_all.34.got = f32[8,40,128]{2,1,0:T(8,128)S(1)} all-to-all(f32[8,40,128]{2,1,0:T(8,128)S(1)} %get-tuple-element.58), channel_id=1, replica_groups=mesh['x'=4,'y'=8,'z'=8,'core'=2] {'x','core'}, dimensions={0} | all-to-all | bytes 327680 | tf_op jit(solution)/shard_map/all_to_all | solution.py:451
  75.5 0.1 turn.3
  75.6 10.1 %all_to_all.35.got = f32[8,32,128]{2,1,0:T(8,128)S(1)} all-to-all(f32[8,32,128]{2,1,0:T(8,128)S(1)} %get-tuple-element.61), channel_id=1, replica_groups=mesh['x'=4,'y'=8,'z'=8,'core'=2] {'z'}, dimensions={0} | all-to-all | bytes 262144 | tf_op jit(solution)/shard_map/all_to_all | solution.py:459
  85.7 1.0 %seams_last.1 = bf16[16,64,128]{2,1,0:T(8,128)(2,1)} custom-call(f32[24,128]{1,0:T(8,128)S(1)} %copy-done.3, bf16[1024,128]{1,0:T(8,128)(2,1)S(1)} %get-tuple-element.52.pred, f32[8,32,128]{2,1,0:T(8,128)S(1)} %all_to_all.35.got, f32[2,16,128]{2,1,0:T(8,128)S(1)} %get-tuple-element.62.drift, f32[2,16,128]{2,1,0:T(8,128)S(1)} %get-tuple-element.63.low, ...), custom_call_target="tpu_custom_call" | custom-call | tf_op jit(solution)/shard_map/seams_last/pallas_call | solution.py:394
  (1 shorter events, 0.0 us)
Async XLA Ops:
  4.2 16.2 %copy-start.3 = (f32[24,128]{1,0:T(8,128)S(1)}, f32[24,128]{1,0:T(8,128)}, u32[]{:S(2)}) copy-start(f32[24,128]{1,0:T(8,128)} %get-tuple-element.36.aux_ref) | copy-start | bytes 36868
  4.2 16.2 %copy-start.7 = (f32[2,16,128]{2,1,0:T(8,128)S(1)}, f32[2,16,128]{2,1,0:T(8,128)}, u32[]{:S(2)}) copy-start(f32[2,16,128]{2,1,0:T(8,128)} %get-tuple-element.40.rest_1_.south) | copy-start | bytes 49156
  4.2 16.2 %copy-start.8 = (f32[2,16,128]{2,1,0:T(8,128)S(1)}, f32[2,16,128]{2,1,0:T(8,128)}, u32[]{:S(2)}) copy-start(f32[2,16,128]{2,1,0:T(8,128)} %get-tuple-element.41.rest_2_.north) | copy-start | bytes 49156
  4.2 16.2 %copy-start.9 = (f32[2,16,128]{2,1,0:T(8,128)S(1)}, f32[2,16,128]{2,1,0:T(8,128)}, u32[]{:S(2)}) copy-start(f32[2,16,128]{2,1,0:T(8,128)} %get-tuple-element.39.rest_0_) | copy-start | bytes 49156
  20.4 30.5 %copy-start.6 = (bf16[512,128]{1,0:T(8,128)(2,1)S(1)}, bf16[512,128]{1,0:T(8,128)(2,1)}, u32[]{:S(2)}) copy-start(bf16[512,128]{1,0:T(8,128)(2,1)} %get-tuple-element.51.wide_out) | copy-start | bytes 393220
  20.6 30.3 %copy-start.4 = (bf16[1024,128]{1,0:T(8,128)(2,1)S(1)}, bf16[1024,128]{1,0:T(8,128)(2,1)}, u32[]{:S(2)}) copy-start(bf16[1024,128]{1,0:T(8,128)(2,1)} %get-tuple-element.37.pred) | copy-start | bytes 786436
  20.6 30.3 %copy-start.5 = (bf16[128,512]{1,0:T(8,128)(2,1)S(1)}, bf16[128,512]{1,0:T(8,128)(2,1)}, u32[]{:S(2)}) copy-start(bf16[128,512]{1,0:T(8,128)(2,1)} %get-tuple-element.50.wide_in) | copy-start | bytes 393220
  32.7 18.2 %copy-start = (bf16[7,128,128]{2,1,0:T(8,128)(2,1)S(1)}, bf16[7,128,128]{2,1,0:T(8,128)(2,1)}, u32[]{:S(2)}) copy-start(bf16[7,128,128]{2,1,0:T(8,128)(2,1)} %w_mid.3) | copy-start | bytes 688132
  32.8 18.1 %copy-start.1 = (bf16[512,128]{1,0:T(8,128)(2,1)S(1)}, bf16[512,128]{1,0:T(8,128)(2,1)}, u32[]{:S(2)}) copy-start(bf16[512,128]{1,0:T(8,128)(2,1)} %w_down.3) | copy-start | bytes 393220
  32.8 18.1 %copy-start.2 = (bf16[128,512]{1,0:T(8,128)(2,1)S(1)}, bf16[128,512]{1,0:T(8,128)(2,1)}, u32[]{:S(2)}) copy-start(bf16[128,512]{1,0:T(8,128)(2,1)} %w_up.3) | copy-start | bytes 393220

commit v8 on v7

--- a/solution.py
+++ b/solution.py
@@ -417,6 +417,7 @@
         if step == 0:
             args = (latent[0, 0], occupancy[0], carry_x[0], carry_y[0], w_in, w_down, w_mid, w_up, w_out.T)
             held = [pltpu.VMEM(a.shape, a.dtype) for a in args]
+            args = [pltpu.with_memory_space_constraint(a, pltpu.HBM) for a in args]
             pred, msg, west, south, north, aux, wide_in, wide_out = call(
                 first_kernel,
                 (*net_out, shape((24, 128), F32), shape((128, 512), BF16), shape((512, 128), BF16)),
@@ -424,7 +425,6 @@
                 args,
                 "net_first",
                 pl.ANY,
-                60,
             )
         else:
             pred, msg, west, south, north, factors_z = call(

time: 87.1 us -> 85.7 us (0.984)
  no operation moved by 1% of the time
where the time goes in v8:
time: 85.7 us; the launch traced here: 85.4 us
  blocking collectives  78.1 us (91%)
  Pallas kernels  7.15 us (8%)
    all_to_all x2, blocking collectives, per_device(): got = lax.all_to_all(msg, 'z', 0, 0)  28.2 us
    all_to_all x2, blocking collectives, per_device(): got = lax.all_to_all(msg, 'y', 0, 0)  26.1 us
    all_to_all x2, blocking collectives, per_device(): got = lax.all_to_all(msg, ('x', 'core'), 0, 0)  23.9 us
    pallas_call x7, Pallas kernels, call(): pl.pallas_call(kernel, out_shape=out_shape, in_specs=[pl.BlockSpec(memory...  7.15 us

profile of v8, /device:TPU:1, one launch (start us, length us, event | category | flops | bytes accessed | tf_op | source)
XLA Modules:
  0.0 85.4 jit_solution(13652576906303435832)
XLA Ops:
  0.0 3.4 %net_first.1 = (bf16[1024,128]{1,0:T(8,128)(2,1)S(1)}, f32[8,40,128]{2,1,0:T(8,128)S(1)}, f32[2,16,128]{2,1,0:T(8,128)S(1)}, f32[2,16,128]{2,1,0:T(8,128)S(1)}, ...) custom-call(bf16[16,64,128]{2,1,0:T(8,128)(2,1)} %bitcast.6, ...), custom_call_target="tpu_custom_call" | custom-call | tf_op jit(solution)/shard_map/net_first/pallas_call | solution.py:394
  3.4 15.8 %all_to_all.30.got = f32[8,40,128]{2,1,0:T(8,128)S(1)} all-to-all(f32[8,40,128]{2,1,0:T(8,128)S(1)} %get-tuple-element.38), channel_id=1, replica_groups=mesh['x'=4,'y'=8,'z'=8,'core'=2] {'y'}, dimensions={0} | all-to-all | bytes 327680 | tf_op jit(solution)/shard_map/all_to_all | solution.py:437
  19.2 0.1 group.2
  19.3 12.1 %all_to_all.31.got = f32[8,40,128]{2,1,0:T(8,128)S(1)} all-to-all(f32[8,40,128]{2,1,0:T(8,128)S(1)} %get-tuple-element.42), channel_id=1, replica_groups=mesh['x'=4,'y'=8,'z'=8,'core'=2] {'x','core'}, dimensions={0} | all-to-all | bytes 327680 | tf_op jit(solution)/shard_map/all_to_all | solution.py:451
  31.4 0.0 copy-start
  31.4 0.1 turn.2
  31.5 0.0 copy-start.1
  31.5 0.0 copy-start.2
  31.5 18.0 %all_to_all.32.got = f32[8,40,128]{2,1,0:T(8,128)S(1)} all-to-all(f32[8,40,128]{2,1,0:T(8,128)S(1)} %get-tuple-element.45), channel_id=1, replica_groups=mesh['x'=4,'y'=8,'z'=8,'core'=2] {'z'}, dimensions={0} | all-to-all | bytes 327680 | tf_op jit(solution)/shard_map/all_to_all | solution.py:459
  49.6 0.0 copy-done
  49.6 0.0 copy-done.1
  49.6 0.0 copy-done.2
  49.6 2.3 %seams_net.1 = (bf16[1024,128]{1,0:T(8,128)(2,1)S(1)}, f32[8,32,128]{2,1,0:T(8,128)S(1)}, f32[2,16,128]{2,1,0:T(8,128)S(1)}, f32[2,16,128]{2,1,0:T(8,128)S(1)}, ...) custom-call(f32[24,128]{1,0:T(8,128)S(1)} %get-tuple-element.36.aux_ref, bf16[1024,128]{1,0:T(8,128)(2,1)S(1)} %get-tuple-element.37.pred, ...), custom_call_target="tpu_custom_call" | custom-call | tf_op jit(solution)/shard_map/seams_net/pallas_call | solution.py:394
  51.9 10.3 %all_to_all.33.got = f32[8,32,128]{2,1,0:T(8,128)S(1)} all-to-all(f32[8,32,128]{2,1,0:T(8,128)S(1)} %get-tuple-element.53), channel_id=1, replica_groups=mesh['x'=4,'y'=8,'z'=8,'core'=2] {'y'}, dimensions={0} | all-to-all | bytes 262144 | tf_op jit(solution)/shard_map/all_to_all | solution.py:437
  62.2 0.1 group.3
  62.3 11.8 %all_to_all.34.got = f32[8,40,128]{2,1,0:T(8,128)S(1)} all-to-all(f32[8,40,128]{2,1,0:T(8,128)S(1)} %get-tuple-element.58), channel_id=1, replica_groups=mesh['x'=4,'y'=8,'z'=8,'core'=2] {'x','core'}, dimensions={0} | all-to-all | bytes 327680 | tf_op jit(solution)/shard_map/all_to_all | solution.py:451
  74.1 0.1 turn.3
  74.2 10.1 %all_to_all.35.got = f32[8,32,128]{2,1,0:T(8,128)S(1)} all-to-all(f32[8,32,128]{2,1,0:T(8,128)S(1)} %get-tuple-element.61), channel_id=1, replica_groups=mesh['x'=4,'y'=8,'z'=8,'core'=2] {'z'}, dimensions={0} | all-to-all | bytes 262144 | tf_op jit(solution)/shard_map/all_to_all | solution.py:459
  84.4 1.0 %seams_last.1 = bf16[16,64,128]{2,1,0:T(8,128)(2,1)} custom-call(f32[24,128]{1,0:T(8,128)S(1)} %get-tuple-element.36.aux_ref, bf16[1024,128]{1,0:T(8,128)(2,1)S(1)} %get-tuple-element.52.pred, f32[8,32,128]{2,1,0:T(8,128)S(1)} %all_to_all.35.got, f32[2,16,128]{2,1,0:T(8,128)S(1)} %get-tuple-element.62.drift, f32[2,16,128]{2,1,0:T(8,128)S(1)} %get-tuple-element.63.low, ...), custom_call_target="tpu_custom_call" | custom-call | tf_op jit(solution)/shard_map/seams_last/pallas_call | solution.py:394
Async XLA Ops:
  31.4 18.2 %copy-start = (bf16[7,128,128]{2,1,0:T(8,128)(2,1)S(1)}, bf16[7,128,128]{2,1,0:T(8,128)(2,1)}, u32[]{:S(2)}) copy-start(bf16[7,128,128]{2,1,0:T(8,128)(2,1)} %w_mid.3) | copy-start | bytes 688132
  31.5 18.1 %copy-start.1 = (bf16[512,128]{1,0:T(8,128)(2,1)S(1)}, bf16[512,128]{1,0:T(8,128)(2,1)}, u32[]{:S(2)}) copy-start(bf16[512,128]{1,0:T(8,128)(2,1)} %w_down.3) | copy-start | bytes 393220
  31.5 18.1 %copy-start.2 = (bf16[128,512]{1,0:T(8,128)(2,1)S(1)}, bf16[128,512]{1,0:T(8,128)(2,1)}, u32[]{:S(2)}) copy-start(bf16[128,512]{1,0:T(8,128)(2,1)} %w_up.3) | copy-start | bytes 393220

commit v9 on v8

--- a/solution.py
+++ b/solution.py
@@ -72,7 +72,7 @@
     def lower(k, n):
         rows = pl.ds(n * k, n)
         first = silu_of_half(jnp.dot(state[rows, :], wide_in[...], preferred_element_type=F32)).astype(BF16)
-        first_ref[rows, :] = first
+        first_ref[rows, :] = 0.5 * first
         firsts[k] = first
 
     def down(k, n):
@@ -102,8 +102,8 @@
 
     def up(k, n):
         rows = pl.ds(n * k, n)
-        upper = jnp.dot(middles.pop(k), w_up[...], preferred_element_type=F32) + first_ref[rows, :].astype(F32)
-        uppers[k] = silu(upper).astype(BF16)
+        upper = jnp.dot(middles.pop(k), 0.5 * w_up[...], preferred_element_type=F32) + first_ref[rows, :].astype(F32)
+        uppers[k] = silu_of_half(upper).astype(BF16)
 
     def out(k, n):
         rows = pl.ds(n * k, n)
@@ -124,10 +124,12 @@
                 south[qx] = south[qx] + jnp.where(by == qz, turn_rows(s, qz), 0.0)
                 north[qx] = north[qx] + jnp.where(by == qz, turn_rows(s, qz - 3), 0.0)
 
-    for k in range(4):
+    lower(0, 256)
+    lower(1, 256)
+    for k in range(2, 4):
         lower(k, 256)
-        if k > 0:
-            down(k - 1, 256)
+        down(k - 2, 256)
+    down(2, 256)
     down(3, 256)
     for k in range(2):
         stencil(k, 512)

time: 85.7 us -> 85.5 us (level)
  no operation moved by 1% of the time
where the time goes in v9:
time: 85.5 us; the launch traced here: 85.2 us
  blocking collectives  78.1 us (91%)
  Pallas kernels  6.98 us (8%)
    all_to_all x2, blocking collectives, per_device(): got = lax.all_to_all(msg, 'z', 0, 0)  28.2 us
    all_to_all x2, blocking collectives, per_device(): got = lax.all_to_all(msg, 'y', 0, 0)  26.1 us
    all_to_all x2, blocking collectives, per_device(): got = lax.all_to_all(msg, ('x', 'core'), 0, 0)  23.9 us
    pallas_call x7, Pallas kernels, call(): pl.pallas_call(kernel, out_shape=out_shape, in_specs=[pl.BlockSpec(memory...  6.98 us

profile of v9, /device:TPU:1, one launch (start us, length us, event | category | flops | bytes accessed | tf_op | source)
XLA Modules:
  0.0 85.2 jit_solution(15935907361672876761)
XLA Ops:
  0.0 3.3 %net_first.1 = (bf16[1024,128]{1,0:T(8,128)(2,1)S(1)}, f32[8,40,128]{2,1,0:T(8,128)S(1)}, f32[2,16,128]{2,1,0:T(8,128)S(1)}, f32[2,16,128]{2,1,0:T(8,128)S(1)}, ...) custom-call(bf16[16,64,128]{2,1,0:T(8,128)(2,1)} %bitcast.6, ...), custom_call_target="tpu_custom_call" | custom-call | tf_op jit(solution)/shard_map/net_first/pallas_call | solution.py:396
  3.3 15.8 %all_to_all.30.got = f32[8,40,128]{2,1,0:T(8,128)S(1)} all-to-all(f32[8,40,128]{2,1,0:T(8,128)S(1)} %get-tuple-element.38), channel_id=1, replica_groups=mesh['x'=4,'y'=8,'z'=8,'core'=2] {'y'}, dimensions={0} | all-to-all | bytes 327680 | tf_op jit(solution)/shard_map/all_to_all | solution.py:439
  19.1 0.1 group.2
  19.2 12.1 %all_to_all.31.got = f32[8,40,128]{2,1,0:T(8,128)S(1)} all-to-all(f32[8,40,128]{2,1,0:T(8,128)S(1)} %get-tuple-element.42), channel_id=1, replica_groups=mesh['x'=4,'y'=8,'z'=8,'core'=2] {'x','core'}, dimensions={0} | all-to-all | bytes 327680 | tf_op jit(solution)/shard_map/all_to_all | solution.py:453
  31.3 0.0 copy-start
  31.3 0.1 turn.2
  31.4 0.0 copy-start.1
  31.4 0.0 copy-start.2
  31.4 18.0 %all_to_all.32.got = f32[8,40,128]{2,1,0:T(8,128)S(1)} all-to-all(f32[8,40,128]{2,1,0:T(8,128)S(1)} %get-tuple-element.45), channel_id=1, replica_groups=mesh['x'=4,'y'=8,'z'=8,'core'=2] {'z'}, dimensions={0} | all-to-all | bytes 327680 | tf_op jit(solution)/shard_map/all_to_all | solution.py:461
  49.5 0.0 copy-done
  49.5 0.0 copy-done.1
  49.5 0.0 copy-done.2
  49.5 2.2 %seams_net.1 = (bf16[1024,128]{1,0:T(8,128)(2,1)S(1)}, f32[8,32,128]{2,1,0:T(8,128)S(1)}, f32[2,16,128]{2,1,0:T(8,128)S(1)}, f32[2,16,128]{2,1,0:T(8,128)S(1)}, ...) custom-call(f32[24,128]{1,0:T(8,128)S(1)} %get-tuple-element.36.aux_ref, bf16[1024,128]{1,0:T(8,128)(2,1)S(1)} %get-tuple-element.37.pred, ...), custom_call_target="tpu_custom_call" | custom-call | tf_op jit(solution)/shard_map/seams_net/pallas_call | solution.py:396
  51.7 10.3 %all_to_all.33.got = f32[8,32,128]{2,1,0:T(8,128)S(1)} all-to-all(f32[8,32,128]{2,1,0:T(8,128)S(1)} %get-tuple-element.53), channel_id=1, replica_groups=mesh['x'=4,'y'=8,'z'=8,'core'=2] {'y'}, dimensions={0} | all-to-all | bytes 262144 | tf_op jit(solution)/shard_map/all_to_all | solution.py:439
  62.0 0.1 group.3
  62.2 11.8 %all_to_all.34.got = f32[8,40,128]{2,1,0:T(8,128)S(1)} all-to-all(f32[8,40,128]{2,1,0:T(8,128)S(1)} %get-tuple-element.58), channel_id=1, replica_groups=mesh['x'=4,'y'=8,'z'=8,'core'=2] {'x','core'}, dimensions={0} | all-to-all | bytes 327680 | tf_op jit(solution)/shard_map/all_to_all | solution.py:453
  73.9 0.1 turn.3
  74.1 10.1 %all_to_all.35.got = f32[8,32,128]{2,1,0:T(8,128)S(1)} all-to-all(f32[8,32,128]{2,1,0:T(8,128)S(1)} %get-tuple-element.61), channel_id=1, replica_groups=mesh['x'=4,'y'=8,'z'=8,'core'=2] {'z'}, dimensions={0} | all-to-all | bytes 262144 | tf_op jit(solution)/shard_map/all_to_all | solution.py:461
  84.2 1.0 %seams_last.1 = bf16[16,64,128]{2,1,0:T(8,128)(2,1)} custom-call(f32[24,128]{1,0:T(8,128)S(1)} %get-tuple-element.36.aux_ref, bf16[1024,128]{1,0:T(8,128)(2,1)S(1)} %get-tuple-element.52.pred, f32[8,32,128]{2,1,0:T(8,128)S(1)} %all_to_all.35.got, f32[2,16,128]{2,1,0:T(8,128)S(1)} %get-tuple-element.62.drift, f32[2,16,128]{2,1,0:T(8,128)S(1)} %get-tuple-element.63.low, ...), custom_call_target="tpu_custom_call" | custom-call | tf_op jit(solution)/shard_map/seams_last/pallas_call | solution.py:396
Async XLA Ops:
  31.3 18.2 %copy-start = (bf16[7,128,128]{2,1,0:T(8,128)(2,1)S(1)}, bf16[7,128,128]{2,1,0:T(8,128)(2,1)}, u32[]{:S(2)}) copy-start(bf16[7,128,128]{2,1,0:T(8,128)(2,1)} %w_mid.3) | copy-start | bytes 688132
  31.4 18.1 %copy-start.1 = (bf16[512,128]{1,0:T(8,128)(2,1)S(1)}, bf16[512,128]{1,0:T(8,128)(2,1)}, u32[]{:S(2)}) copy-start(bf16[512,128]{1,0:T(8,128)(2,1)} %w_down.3) | copy-start | bytes 393220
  31.4 18.1 %copy-start.2 = (bf16[128,512]{1,0:T(8,128)(2,1)S(1)}, bf16[128,512]{1,0:T(8,128)(2,1)}, u32[]{:S(2)}) copy-start(bf16[128,512]{1,0:T(8,128)(2,1)} %w_up.3) | copy-start | bytes 393220

commit v10 on v9

--- a/solution.py
+++ b/solution.py
@@ -153,7 +153,7 @@
         west_ref[h] = w
         south_ref[h] = jnp.where(low_sy, south[h], south[2 + h])
         north_ref[h] = jnp.where(low_sy, north[h], north[2 + h])
-    fill(msg, terms, [jnp.broadcast_to(factor, (8, 128))] if msg.shape[1] > 32 else [])
+    fill(msg, terms, factor)
 
 
 class Aux:
@@ -163,15 +163,25 @@
         self.occupied = ref[8:24, :]
 
 
+def has_factor(ref):
+    return len(ref.shape) == 4
+
+
 def halves(ref, k):
+    if has_factor(ref):
+        return [ref[k, pl.ds(4 * h, 4)].reshape(16, 128) for h in range(2)]
     return [ref[k, pl.ds(16 * h, 16), :] for h in range(2)]
 
 
-def fill(msg, planes, rows=()):
-    for k, value in enumerate([*planes, *rows]):
-        size = 16 if k < 2 else 8
-        at = 16 * k if k < 2 else 32 + 8 * (k - 2)
-        msg[:, pl.ds(at, size), :] = jnp.broadcast_to(value[None], (msg.shape[0], size, 128))
+def fill(msg, planes, factor):
+    n = msg.shape[0]
+    for h, value in enumerate(planes):
+        if has_factor(msg):
+            msg[:, pl.ds(4 * h, 4)] = jnp.broadcast_to(value.reshape(1, 4, 4, 128), (n, 4, 4, 128))
+        else:
+            msg[:, pl.ds(16 * h, 16), :] = jnp.broadcast_to(value[None], (n, 16, 128))
+    if has_factor(msg):
+        msg[:, 8] = jnp.broadcast_to(factor[None], (n, 4, 128))
 
 
 def line_of(planes):
@@ -204,10 +214,10 @@
 
 
 def group_kernel(aux_ref, got, *rest):
-    if got.shape[1] > 32:
+    if has_factor(got):
         west, south, north, msg, start_ref, start_f_ref, factor_ref = rest
         for k in range(got.shape[0]):
-            factor_ref[k : k + 1, :] = got[k, 32:33, :]
+            factor_ref[k : k + 1, :] = got[k, 8, 0:1, :]
     else:
         factor_ref, west, south, north, msg, start_ref, start_f_ref = rest
     aux = Aux(aux_ref)
@@ -276,8 +286,7 @@
         pair_ref[h] = jnp.where(first, 0.0, other)
         pairs.append(jnp.where(first, other_factor * own + other, factor * other + own))
     pair_f_ref[...] = jnp.broadcast_to(jnp.where(first, 1.0, other_factor), (8, 128))
-    rows = [jnp.broadcast_to(factor * other_factor, (8, 128))] if msg.shape[1] > 32 else []
-    fill(msg, pairs, rows)
+    fill(msg, pairs, factor * other_factor)
 
 
 def seams(aux, pred_ref, got, factors, drift_ref, low_ref, pair_ref, pair_f_ref, put):
@@ -366,12 +375,12 @@
     outs, (factor_ref, state, first_ref, second_ref) = rest[:5], rest[5:]
     aux = Aux(aux_ref)
     for k in range(got.shape[0]):
-        factor_ref[k : k + 1, :] = got[k, 32:33, :]
+        factor_ref[k : k + 1, :] = got[k, 8, 0:1, :]
 
     def put(q, value):
         state[pl.ds(16 * q, 16), :] = value.astype(BF16)
 
-    seams(aux, pred, got, lambda k: got[k, 32:33, :], drift, low, pair, pair_f, put)
+    seams(aux, pred, got, lambda k: got[k, 8, 0:1, :], drift, low, pair, pair_f, put)
     net(state, lambda: aux, (wide_in, w_down, w_mid, w_up, wide_out), first_ref, second_ref, outs[0], outs[1:])
 
 
@@ -414,8 +423,8 @@
         pltpu.VMEM((1536, 128), BF16),
     ]
     for step in range(STEPS):
-        tall = 40 if step == 0 else 32
-        net_out = (shape((1024, 128), BF16), shape((ys, tall, 128), F32), plane, plane, plane)
+        message = (9, 4, 128) if step == 0 else (32, 128)
+        net_out = (shape((1024, 128), BF16), shape((ys, *message), F32), plane, plane, plane)
         if step == 0:
             args = (latent[0, 0], occupancy[0], carry_x[0], carry_y[0], w_in, w_down, w_mid, w_up, w_out.T)
             held = [pltpu.VMEM(a.shape, a.dtype) for a in args]
@@ -453,7 +462,7 @@
         got = lax.all_to_all(msg, ("x", "core"), 0, 0)
         msg, *seam_ins = call(
             turn_kernel,
-            (shape((zs, tall, 128), F32), plane, plane, plane, row),
+            (shape((zs, *message), F32), plane, plane, plane, row),
             [],
             (aux, got, start, start_f, south, north),
             "turn",

time: 85.5 us -> 84.9 us (level)
  no operation moved by 1% of the time
where the time goes in v10:
time: 84.9 us; the launch traced here: 84.6 us
  blocking collectives  77.5 us (91%)
  Pallas kernels  6.99 us (8%)
    all_to_all x2, blocking collectives, per_device(): got = lax.all_to_all(msg, 'z', 0, 0)  28 us
    all_to_all x2, blocking collectives, per_device(): got = lax.all_to_all(msg, 'y', 0, 0)  26 us
    all_to_all x2, blocking collectives, per_device(): got = lax.all_to_all(msg, ('x', 'core'), 0, 0)  23.5 us
    pallas_call x7, Pallas kernels, call(): pl.pallas_call(kernel, out_shape=out_shape, in_specs=[pl.BlockSpec(memory...  6.99 us

profile of v10, /device:TPU:1, one launch (start us, length us, event | category | flops | bytes accessed | tf_op | source)
XLA Modules:
  0.0 84.6 jit_solution(4441695152744248991)
XLA Ops:
  0.0 3.3 %net_first.1 = (bf16[1024,128]{1,0:T(8,128)(2,1)S(1)}, f32[8,9,4,128]{3,2,1,0:T(4,128)S(1)}, f32[2,16,128]{2,1,0:T(8,128)S(1)}, f32[2,16,128]{2,1,0:T(8,128)S(1)...) custom-call(bf16[16,64,128]{2,1,0:T(8,128)(2,1)} %bitcast.6, ...), custom_call_target="tpu_custom_call" | custom-call | tf_op jit(solution)/shard_map/net_first/pallas_call | solution.py:405
  3.3 15.6 %all_to_all.30.got = f32[8,9,4,128]{3,2,1,0:T(4,128)S(1)} all-to-all(f32[8,9,4,128]{3,2,1,0:T(4,128)S(1)} %get-tuple-element.38), channel_id=1, replica_groups=mesh['x'=4,'y'=8,'z'=8,'core'=2] {'y'}, dimensions={0} | all-to-all | bytes 294912 | tf_op jit(solution)/shard_map/all_to_all | solution.py:448
  18.9 0.1 group.2
  19.0 11.9 %all_to_all.31.got = f32[8,40,128]{2,1,0:T(8,128)S(1)} all-to-all(f32[8,40,128]{2,1,0:T(8,128)S(1)} %get-tuple-element.42), channel_id=1, replica_groups=mesh['x'=4,'y'=8,'z'=8,'core'=2] {'x','core'}, dimensions={0} | all-to-all | bytes 327680 | tf_op jit(solution)/shard_map/all_to_all | solution.py:462
  31.0 0.0 copy-start
  31.0 0.1 turn.2
  31.1 0.0 copy-start.1
  31.1 0.0 copy-start.2
  31.1 17.9 %all_to_all.32.got = f32[8,9,4,128]{3,2,1,0:T(4,128)S(1)} all-to-all(f32[8,9,4,128]{3,2,1,0:T(4,128)S(1)} %get-tuple-element.45), channel_id=1, replica_groups=mesh['x'=4,'y'=8,'z'=8,'core'=2] {'z'}, dimensions={0} | all-to-all | bytes 294912 | tf_op jit(solution)/shard_map/all_to_all | solution.py:470
  49.0 0.0 copy-done
  49.0 0.0 copy-done.1
  49.0 0.0 copy-done.2
  49.0 2.2 %seams_net.1 = (bf16[1024,128]{1,0:T(8,128)(2,1)S(1)}, f32[8,32,128]{2,1,0:T(8,128)S(1)}, f32[2,16,128]{2,1,0:T(8,128)S(1)}, f32[2,16,128]{2,1,0:T(8,128)S(1)}, ...) custom-call(f32[24,128]{1,0:T(8,128)S(1)} %get-tuple-element.36.aux_ref, bf16[1024,128]{1,0:T(8,128)(2,1)S(1)} %get-tuple-element.37.pred, ...), custom_call_target="tpu_custom_call" | custom-call | tf_op jit(solution)/shard_map/seams_net/pallas_call | solution.py:405
  51.2 10.4 %all_to_all.33.got = f32[8,32,128]{2,1,0:T(8,128)S(1)} all-to-all(f32[8,32,128]{2,1,0:T(8,128)S(1)} %get-tuple-element.53), channel_id=1, replica_groups=mesh['x'=4,'y'=8,'z'=8,'core'=2] {'y'}, dimensions={0} | all-to-all | bytes 262144 | tf_op jit(solution)/shard_map/all_to_all | solution.py:448
  61.6 0.1 group.3
  61.8 11.6 %all_to_all.34.got = f32[8,40,128]{2,1,0:T(8,128)S(1)} all-to-all(f32[8,40,128]{2,1,0:T(8,128)S(1)} %get-tuple-element.58), channel_id=1, replica_groups=mesh['x'=4,'y'=8,'z'=8,'core'=2] {'x','core'}, dimensions={0} | all-to-all | bytes 327680 | tf_op jit(solution)/shard_map/all_to_all | solution.py:462
  73.3 0.1 turn.3
  73.4 10.1 %all_to_all.35.got = f32[8,32,128]{2,1,0:T(8,128)S(1)} all-to-all(f32[8,32,128]{2,1,0:T(8,128)S(1)} %get-tuple-element.61), channel_id=1, replica_groups=mesh['x'=4,'y'=8,'z'=8,'core'=2] {'z'}, dimensions={0} | all-to-all | bytes 262144 | tf_op jit(solution)/shard_map/all_to_all | solution.py:470
  83.6 1.0 %seams_last.1 = bf16[16,64,128]{2,1,0:T(8,128)(2,1)} custom-call(f32[24,128]{1,0:T(8,128)S(1)} %get-tuple-element.36.aux_ref, bf16[1024,128]{1,0:T(8,128)(2,1)S(1)} %get-tuple-element.52.pred, f32[8,32,128]{2,1,0:T(8,128)S(1)} %all_to_all.35.got, f32[2,16,128]{2,1,0:T(8,128)S(1)} %get-tuple-element.62.drift, f32[2,16,128]{2,1,0:T(8,128)S(1)} %get-tuple-element.63.low, ...), custom_call_target="tpu_custom_call" | custom-call | tf_op jit(solution)/shard_map/seams_last/pallas_call | solution.py:405
Async XLA Ops:
  31.0 18.0 %copy-start = (bf16[7,128,128]{2,1,0:T(8,128)(2,1)S(1)}, bf16[7,128,128]{2,1,0:T(8,128)(2,1)}, u32[]{:S(2)}) copy-start(bf16[7,128,128]{2,1,0:T(8,128)(2,1)} %w_mid.3) | copy-start | bytes 688132
  31.1 17.9 %copy-start.1 = (bf16[512,128]{1,0:T(8,128)(2,1)S(1)}, bf16[512,128]{1,0:T(8,128)(2,1)}, u32[]{:S(2)}) copy-start(bf16[512,128]{1,0:T(8,128)(2,1)} %w_down.3) | copy-start | bytes 393220
  31.1 17.9 %copy-start.2 = (bf16[128,512]{1,0:T(8,128)(2,1)S(1)}, bf16[128,512]{1,0:T(8,128)(2,1)}, u32[]{:S(2)}) copy-start(bf16[128,512]{1,0:T(8,128)(2,1)} %w_up.3) | copy-start | bytes 393220

commit v11 on v10

--- a/solution.py
+++ b/solution.py
@@ -248,11 +248,25 @@
         tail = jnp.concatenate(tail, axis=0)
         for core in range(2):
             for h in range(2):
-                msg[2 * x + core, pl.ds(16 * h, 16), :] = jnp.where(aux.core == core, total[h], term_y[h])
-            msg[2 * x + core, 32:40, :] = tail
-
-
-def turn_kernel(aux_ref, got, start_ref, start_f_ref, south, north, msg, drift_ref, low_ref, pair_ref, pair_f_ref):
+                value = jnp.where(aux.core == core, total[h], term_y[h])
+                if len(msg.shape) == 4:
+                    msg[2 * x + core, pl.ds(4 * h, 4)] = value.reshape(4, 4, 128)
+                else:
+                    msg[2 * x + core, pl.ds(16 * h, 16), :] = value
+            if len(msg.shape) == 4:
+                msg[2 * x + core, 8] = tail[0:4]
+            else:
+                msg[2 * x + core, 32:40, :] = tail
+
+
+def turn_kernel(aux_ref, got, start_ref, start_f_ref, south, north, *rest):
+    if len(got.shape) == 4:
+        kept, msg, drift_ref, low_ref, pair_ref, pair_f_ref = rest
+        tail_of = lambda peer: jnp.concatenate([got[peer, 8], kept[peer]], axis=0)
+    else:
+        msg, drift_ref, low_ref, pair_ref, pair_f_ref, kept = rest
+        kept[...] = got[:, 36:40, :]
+        tail_of = lambda peer: got[peer, 32:40, :]
     aux = Aux(aux_ref)
     first = aux.core == 0.0
     begin = [jnp.zeros((16, 128), F32)] * 2
@@ -260,7 +274,7 @@
     term, mine_tails = [0.0, 0.0], [0.0, 0.0]
     for x in range(got.shape[0] // 2):
         one, two = halves(got, 2 * x), halves(got, 2 * x + 1)
-        tails = got[2 * x, 32:40, :], got[2 * x + 1, 32:40, :]
+        tails = tail_of(2 * x), tail_of(2 * x + 1)
         tails = [jnp.where(first, *tails), jnp.where(first, *tails[::-1])]
         go, mine = aux.x > x, aux.x == x
         own = [jnp.where(first, one[h], two[h]) for h in range(2)]
@@ -446,7 +460,7 @@
                 "seams_net",
             )
         got = lax.all_to_all(msg, "y", 0, 0)
-        group_out = (shape((2 * xs, 40, 128), F32), plane, row)
+        group_out = (shape((2 * xs, *((40, 128) if step == 0 else (9, 4, 128))), F32), plane, row)
         if step == 0:
             msg, start, start_f, factors_y = call(
                 group_kernel,
@@ -460,13 +474,12 @@
                 group_kernel, group_out, [], (aux, got, factors_y, west, south, north), "group"
             )
         got = lax.all_to_all(msg, ("x", "core"), 0, 0)
-        msg, *seam_ins = call(
-            turn_kernel,
-            (shape((zs, *message), F32), plane, plane, plane, row),
-            [],
-            (aux, got, start, start_f, south, north),
-            "turn",
-        )
+        turn_out = (shape((zs, *message), F32), plane, plane, plane, row)
+        turn_args = (aux, got, start, start_f, south, north)
+        if step == 0:
+            msg, *seam_ins, kept = call(turn_kernel, (*turn_out, shape((2 * xs, 4, 128), F32)), [], turn_args, "turn")
+        else:
+            msg, *seam_ins = call(turn_kernel, turn_out, [], (*turn_args, kept), "turn")
         got = lax.all_to_all(msg, "z", 0, 0)
         seam_ins = (pred, got, *seam_ins)
     out = call(

time: 84.9 us -> 84.8 us (level)
  no operation moved by 1% of the time
where the time goes in v11:
time: 84.8 us; the launch traced here: 84.4 us
  blocking collectives  77.3 us (91%)
  Pallas kernels  7 us (8%)
    all_to_all x2, blocking collectives, per_device(): got = lax.all_to_all(msg, 'z', 0, 0)  28 us
    all_to_all x2, blocking collectives, per_device(): got = lax.all_to_all(msg, 'y', 0, 0)  26 us
    all_to_all x2, blocking collectives, per_device(): got = lax.all_to_all(msg, ('x', 'core'), 0, 0)  23.3 us
    pallas_call x7, Pallas kernels, call(): pl.pallas_call(kernel, out_shape=out_shape, in_specs=[pl.BlockSpec(memory...  7 us

profile of v11, /device:TPU:1, one launch (start us, length us, event | category | flops | bytes accessed | tf_op | source)
XLA Modules:
  0.0 84.4 jit_solution(11674532248868149254)
XLA Ops:
  0.0 3.3 %net_first.1 = (bf16[1024,128]{1,0:T(8,128)(2,1)S(1)}, f32[8,9,4,128]{3,2,1,0:T(4,128)S(1)}, f32[2,16,128]{2,1,0:T(8,128)S(1)}, f32[2,16,128]{2,1,0:T(8,128)S(1)...) custom-call(bf16[16,64,128]{2,1,0:T(8,128)(2,1)} %bitcast.6, ...), custom_call_target="tpu_custom_call" | custom-call | tf_op jit(solution)/shard_map/net_first/pallas_call | solution.py:419
  3.3 15.6 %all_to_all.30.got = f32[8,9,4,128]{3,2,1,0:T(4,128)S(1)} all-to-all(f32[8,9,4,128]{3,2,1,0:T(4,128)S(1)} %get-tuple-element.39), channel_id=1, replica_groups=mesh['x'=4,'y'=8,'z'=8,'core'=2] {'y'}, dimensions={0} | all-to-all | bytes 294912 | tf_op jit(solution)/shard_map/all_to_all | solution.py:462
  18.9 0.1 group.2
  19.0 11.9 %all_to_all.31.got = f32[8,40,128]{2,1,0:T(8,128)S(1)} all-to-all(f32[8,40,128]{2,1,0:T(8,128)S(1)} %get-tuple-element.43), channel_id=1, replica_groups=mesh['x'=4,'y'=8,'z'=8,'core'=2] {'x','core'}, dimensions={0} | all-to-all | bytes 327680 | tf_op jit(solution)/shard_map/all_to_all | solution.py:476
  31.0 0.0 copy-start
  31.0 0.1 turn.2
  31.1 0.0 copy-start.1
  31.1 0.0 copy-start.2
  31.1 17.9 %all_to_all.32.got = f32[8,9,4,128]{3,2,1,0:T(4,128)S(1)} all-to-all(f32[8,9,4,128]{3,2,1,0:T(4,128)S(1)} %get-tuple-element.46), channel_id=1, replica_groups=mesh['x'=4,'y'=8,'z'=8,'core'=2] {'z'}, dimensions={0} | all-to-all | bytes 294912 | tf_op jit(solution)/shard_map/all_to_all | solution.py:483
  49.0 0.0 copy-done
  49.0 0.0 copy-done.1
  49.0 0.0 copy-done.2
  49.0 2.2 %seams_net.1 = (bf16[1024,128]{1,0:T(8,128)(2,1)S(1)}, f32[8,32,128]{2,1,0:T(8,128)S(1)}, f32[2,16,128]{2,1,0:T(8,128)S(1)}, f32[2,16,128]{2,1,0:T(8,128)S(1)}, ...) custom-call(f32[24,128]{1,0:T(8,128)S(1)} %get-tuple-element.37.aux_ref, bf16[1024,128]{1,0:T(8,128)(2,1)S(1)} %get-tuple-element.38.pred, ...), custom_call_target="tpu_custom_call" | custom-call | tf_op jit(solution)/shard_map/seams_net/pallas_call | solution.py:419
  51.2 10.4 %all_to_all.33.got = f32[8,32,128]{2,1,0:T(8,128)S(1)} all-to-all(f32[8,32,128]{2,1,0:T(8,128)S(1)} %get-tuple-element.54), channel_id=1, replica_groups=mesh['x'=4,'y'=8,'z'=8,'core'=2] {'y'}, dimensions={0} | all-to-all | bytes 262144 | tf_op jit(solution)/shard_map/all_to_all | solution.py:462
  61.6 0.1 group.3
  61.8 11.4 %all_to_all.34.got = f32[8,9,4,128]{3,2,1,0:T(4,128)S(1)} all-to-all(f32[8,9,4,128]{3,2,1,0:T(4,128)S(1)} %get-tuple-element.59), channel_id=1, replica_groups=mesh['x'=4,'y'=8,'z'=8,'core'=2] {'x','core'}, dimensions={0} | all-to-all | bytes 294912 | tf_op jit(solution)/shard_map/all_to_all | solution.py:476
  73.2 0.1 turn.3
  73.3 10.1 %all_to_all.35.got = f32[8,32,128]{2,1,0:T(8,128)S(1)} all-to-all(f32[8,32,128]{2,1,0:T(8,128)S(1)} %get-tuple-element.63), channel_id=1, replica_groups=mesh['x'=4,'y'=8,'z'=8,'core'=2] {'z'}, dimensions={0} | all-to-all | bytes 262144 | tf_op jit(solution)/shard_map/all_to_all | solution.py:483
  83.4 1.0 %seams_last.1 = bf16[16,64,128]{2,1,0:T(8,128)(2,1)} custom-call(f32[24,128]{1,0:T(8,128)S(1)} %get-tuple-element.37.aux_ref, bf16[1024,128]{1,0:T(8,128)(2,1)S(1)} %get-tuple-element.53.pred, f32[8,32,128]{2,1,0:T(8,128)S(1)} %all_to_all.35.got, f32[2,16,128]{2,1,0:T(8,128)S(1)} %get-tuple-element.64.drift, f32[2,16,128]{2,1,0:T(8,128)S(1)} %get-tuple-element.65.low, ...), custom_call_target="tpu_custom_call" | custom-call | tf_op jit(solution)/shard_map/seams_last/pallas_call | solution.py:419
Async XLA Ops:
  31.0 18.0 %copy-start = (bf16[7,128,128]{2,1,0:T(8,128)(2,1)S(1)}, bf16[7,128,128]{2,1,0:T(8,128)(2,1)}, u32[]{:S(2)}) copy-start(bf16[7,128,128]{2,1,0:T(8,128)(2,1)} %w_mid.3) | copy-start | bytes 688132
  31.1 17.9 %copy-start.1 = (bf16[512,128]{1,0:T(8,128)(2,1)S(1)}, bf16[512,128]{1,0:T(8,128)(2,1)}, u32[]{:S(2)}) copy-start(bf16[512,128]{1,0:T(8,128)(2,1)} %w_down.3) | copy-start | bytes 393220
  31.1 17.9 %copy-start.2 = (bf16[128,512]{1,0:T(8,128)(2,1)S(1)}, bf16[128,512]{1,0:T(8,128)(2,1)}, u32[]{:S(2)}) copy-start(bf16[128,512]{1,0:T(8,128)(2,1)} %w_up.3) | copy-start | bytes 393220

commit v12 on v10

--- a/solution.py
+++ b/solution.py
@@ -169,7 +169,7 @@
 
 def halves(ref, k):
     if has_factor(ref):
-        return [ref[k, pl.ds(4 * h, 4)].reshape(16, 128) for h in range(2)]
+        return [ref[k, pl.ds(16 * h, 16)].reshape(16, 128) for h in range(2)]
     return [ref[k, pl.ds(16 * h, 16), :] for h in range(2)]
 
 
@@ -177,11 +177,11 @@
     n = msg.shape[0]
     for h, value in enumerate(planes):
         if has_factor(msg):
-            msg[:, pl.ds(4 * h, 4)] = jnp.broadcast_to(value.reshape(1, 4, 4, 128), (n, 4, 4, 128))
+            msg[:, pl.ds(16 * h, 16)] = jnp.broadcast_to(value.reshape(1, 16, 1, 128), (n, 16, 1, 128))
         else:
             msg[:, pl.ds(16 * h, 16), :] = jnp.broadcast_to(value[None], (n, 16, 128))
     if has_factor(msg):
-        msg[:, 8] = jnp.broadcast_to(factor[None], (n, 4, 128))
+        msg[:, 32] = jnp.broadcast_to(factor[None], (n, 1, 128))
 
 
 def line_of(planes):
@@ -217,7 +217,7 @@
     if has_factor(got):
         west, south, north, msg, start_ref, start_f_ref, factor_ref = rest
         for k in range(got.shape[0]):
-            factor_ref[k : k + 1, :] = got[k, 8, 0:1, :]
+            factor_ref[k : k + 1, :] = got[k, 32, 0:1, :]
     else:
         factor_ref, west, south, north, msg, start_ref, start_f_ref = rest
     aux = Aux(aux_ref)
@@ -375,12 +375,12 @@
     outs, (factor_ref, state, first_ref, second_ref) = rest[:5], rest[5:]
     aux = Aux(aux_ref)
     for k in range(got.shape[0]):
-        factor_ref[k : k + 1, :] = got[k, 8, 0:1, :]
+        factor_ref[k : k + 1, :] = got[k, 32, 0:1, :]
 
     def put(q, value):
         state[pl.ds(16 * q, 16), :] = value.astype(BF16)
 
-    seams(aux, pred, got, lambda k: got[k, 8, 0:1, :], drift, low, pair, pair_f, put)
+    seams(aux, pred, got, lambda k: got[k, 32, 0:1, :], drift, low, pair, pair_f, put)
     net(state, lambda: aux, (wide_in, w_down, w_mid, w_up, wide_out), first_ref, second_ref, outs[0], outs[1:])
 
 
@@ -423,7 +423,7 @@
         pltpu.VMEM((1536, 128), BF16),
     ]
     for step in range(STEPS):
-        message = (9, 4, 128) if step == 0 else (32, 128)
+        message = (33, 1, 128) if step == 0 else (32, 128)
         net_out = (shape((1024, 128), BF16), shape((ys, *message), F32), plane, plane, plane)
         if step == 0:
             args = (latent[0, 0], occupancy[0], carry_x[0], carry_y[0], w_in, w_down, w_mid, w_up, w_out.T)

time: 84.9 us -> 84.7 us (level)
  no operation moved by 1% of the time
where the time goes in v12:
time: 84.7 us; the launch traced here: 84.4 us
  blocking collectives  77.1 us (91%)
  Pallas kernels  7.19 us (8%)
    all_to_all x2, blocking collectives, per_device(): got = lax.all_to_all(msg, 'z', 0, 0)  28 us
    all_to_all x2, blocking collectives, per_device(): got = lax.all_to_all(msg, 'y', 0, 0)  25.8 us
    all_to_all x2, blocking collectives, per_device(): got = lax.all_to_all(msg, ('x', 'core'), 0, 0)  23.2 us
    pallas_call x7, Pallas kernels, call(): pl.pallas_call(kernel, out_shape=out_shape, in_specs=[pl.BlockSpec(memory...  7.19 us

profile of v12, /device:TPU:1, one launch (start us, length us, event | category | flops | bytes accessed | tf_op | source)
XLA Modules:
  0.0 84.4 jit_solution(9960473369430119153)
XLA Ops:
  0.0 3.4 %net_first.1 = (bf16[1024,128]{1,0:T(8,128)(2,1)S(1)}, f32[8,33,1,128]{3,2,1,0:T(1,128)S(1)}, f32[2,16,128]{2,1,0:T(8,128)S(1)}, f32[2,16,128]{2,1,0:T(8,128)S(1...) custom-call(bf16[16,64,128]{2,1,0:T(8,128)(2,1)} %bitcast.6, ...), custom_call_target="tpu_custom_call" | custom-call | tf_op jit(solution)/shard_map/net_first/pallas_call | solution.py:405
  3.4 15.4 %all_to_all.30.got = f32[8,33,1,128]{3,2,1,0:T(1,128)S(1)} all-to-all(f32[8,33,1,128]{3,2,1,0:T(1,128)S(1)} %get-tuple-element.38), channel_id=1, replica_groups=mesh['x'=4,'y'=8,'z'=8,'core'=2] {'y'}, dimensions={0} | all-to-all | bytes 270336 | tf_op jit(solution)/shard_map/all_to_all | solution.py:448
  18.8 0.2 group.2
  19.0 11.8 %all_to_all.31.got = f32[8,40,128]{2,1,0:T(8,128)S(1)} all-to-all(f32[8,40,128]{2,1,0:T(8,128)S(1)} %get-tuple-element.42), channel_id=1, replica_groups=mesh['x'=4,'y'=8,'z'=8,'core'=2] {'x','core'}, dimensions={0} | all-to-all | bytes 327680 | tf_op jit(solution)/shard_map/all_to_all | solution.py:462
  30.8 0.0 copy-start
  30.8 0.2 turn.2
  31.0 0.0 copy-start.1
  31.0 0.0 copy-start.2
  31.0 17.9 %all_to_all.32.got = f32[8,33,1,128]{3,2,1,0:T(1,128)S(1)} all-to-all(f32[8,33,1,128]{3,2,1,0:T(1,128)S(1)} %get-tuple-element.45), channel_id=1, replica_groups=mesh['x'=4,'y'=8,'z'=8,'core'=2] {'z'}, dimensions={0} | all-to-all | bytes 270336 | tf_op jit(solution)/shard_map/all_to_all | solution.py:470
  48.9 0.0 copy-done
  48.9 0.0 copy-done.1
  48.9 0.0 copy-done.2
  48.9 2.3 %seams_net.1 = (bf16[1024,128]{1,0:T(8,128)(2,1)S(1)}, f32[8,32,128]{2,1,0:T(8,128)S(1)}, f32[2,16,128]{2,1,0:T(8,128)S(1)}, f32[2,16,128]{2,1,0:T(8,128)S(1)}, ...) custom-call(f32[24,128]{1,0:T(8,128)S(1)} %get-tuple-element.36.aux_ref, bf16[1024,128]{1,0:T(8,128)(2,1)S(1)} %get-tuple-element.37.pred, ...), custom_call_target="tpu_custom_call" | custom-call | tf_op jit(solution)/shard_map/seams_net/pallas_call | solution.py:405
  51.2 10.4 %all_to_all.33.got = f32[8,32,128]{2,1,0:T(8,128)S(1)} all-to-all(f32[8,32,128]{2,1,0:T(8,128)S(1)} %get-tuple-element.53), channel_id=1, replica_groups=mesh['x'=4,'y'=8,'z'=8,'core'=2] {'y'}, dimensions={0} | all-to-all | bytes 262144 | tf_op jit(solution)/shard_map/all_to_all | solution.py:448
  61.6 0.1 group.3
  61.7 11.4 %all_to_all.34.got = f32[8,40,128]{2,1,0:T(8,128)S(1)} all-to-all(f32[8,40,128]{2,1,0:T(8,128)S(1)} %get-tuple-element.58), channel_id=1, replica_groups=mesh['x'=4,'y'=8,'z'=8,'core'=2] {'x','core'}, dimensions={0} | all-to-all | bytes 327680 | tf_op jit(solution)/shard_map/all_to_all | solution.py:462
  73.1 0.1 turn.3
  73.3 10.1 %all_to_all.35.got = f32[8,32,128]{2,1,0:T(8,128)S(1)} all-to-all(f32[8,32,128]{2,1,0:T(8,128)S(1)} %get-tuple-element.61), channel_id=1, replica_groups=mesh['x'=4,'y'=8,'z'=8,'core'=2] {'z'}, dimensions={0} | all-to-all | bytes 262144 | tf_op jit(solution)/shard_map/all_to_all | solution.py:470
  83.4 1.0 %seams_last.1 = bf16[16,64,128]{2,1,0:T(8,128)(2,1)} custom-call(f32[24,128]{1,0:T(8,128)S(1)} %get-tuple-element.36.aux_ref, bf16[1024,128]{1,0:T(8,128)(2,1)S(1)} %get-tuple-element.52.pred, f32[8,32,128]{2,1,0:T(8,128)S(1)} %all_to_all.35.got, f32[2,16,128]{2,1,0:T(8,128)S(1)} %get-tuple-element.62.drift, f32[2,16,128]{2,1,0:T(8,128)S(1)} %get-tuple-element.63.low, ...), custom_call_target="tpu_custom_call" | custom-call | tf_op jit(solution)/shard_map/seams_last/pallas_call | solution.py:405
Async XLA Ops:
  30.8 18.1 %copy-start = (bf16[7,128,128]{2,1,0:T(8,128)(2,1)S(1)}, bf16[7,128,128]{2,1,0:T(8,128)(2,1)}, u32[]{:S(2)}) copy-start(bf16[7,128,128]{2,1,0:T(8,128)(2,1)} %w_mid.3) | copy-start | bytes 688132
  31.0 17.9 %copy-start.1 = (bf16[512,128]{1,0:T(8,128)(2,1)S(1)}, bf16[512,128]{1,0:T(8,128)(2,1)}, u32[]{:S(2)}) copy-start(bf16[512,128]{1,0:T(8,128)(2,1)} %w_down.3) | copy-start | bytes 393220
  31.0 17.9 %copy-start.2 = (bf16[128,512]{1,0:T(8,128)(2,1)S(1)}, bf16[128,512]{1,0:T(8,128)(2,1)}, u32[]{:S(2)}) copy-start(bf16[128,512]{1,0:T(8,128)(2,1)} %w_up.3) | copy-start | bytes 393220
